TPU v7x, 256 devices: a whole 4x4x8 slice. The times are simulated.
256 devices in a mesh: mom: 32 (over x, y, z_hi), en: 8 (over z_lo, core).
Axes of the slice: x: 4, y: 4, z: 8 (z_hi: 2, z_lo: 4; z = z_hi * 4 + z_lo), core: 2. Of those that a mesh axis runs over, the one named last changes fastest.
Arguments:
- green: bfloat16 [2, 64, 1024, 256], P(None, 'mom', 'en'), may hold values from 0.0099487305 to 1
- mask: int32 [1024], P('en'), may hold values 0 or 1
- pair_order: int32 [4, 32, 2], P(None, 'mom'), may hold values from 0 to 1, each once within a row
- q_index: int32 [4, 64], P(None, 'mom'), may hold values from 0 to 127
- offsets: int32 [8], replicated, may hold values from 1 to 4, as said below
- occupancy: float32 [8], replicated, may hold values from 0.2 to 4
- coupling: float32 [128, 8], replicated, may hold values from 0.02 to 0.3
Outputs:
- sigma: bfloat16 [2, 64, 1024, 256], P(None, 'mom', 'en')
- polarization: float32 [128, 8, 256], P('mom')
Inputs may be any that keep to these rules, and one draw needn't show every extreme that they name: Each row pair_order[r, b] is a permutation of 0 to 1. `offsets`: every branch's offset lies between 1 and 4; some branch has 4 and some has 1.
All inputs are finite; a program needn't handle non-finite values. No bound on the sum of `mask` on one device may be relied on, other than what follows from the above.
Results may differ from a plain program's by a relative error of at most 0.012.
Values may be sent and summed in bfloat16 or wider, within the bound.
No kernel may reach another device: no remote copies, remote signals or barrier semaphores. Data moves between devices by JAX's collectives and lax.ppermute only.
A program may use at most 128 MiB of HBM per device.

v0:
```python
import jax
import jax.numpy as jnp
from jax import lax
from jax.sharding import PartitionSpec as P

HALO = 4
ROUNDS = 3


def padded(x, sides, width):
    for axis, dim in sides:
        size, length = (lax.axis_size(axis), x.shape[dim])
        up = [(i, (i + 1) % size) for i in range(size - 1)]
        down = [(j, i) for i, j in up]
        last = lax.slice_in_dim(x, length - width, length, axis=dim)
        first = lax.slice_in_dim(x, 0, width, axis=dim)
        before = lax.ppermute(last, axis, up)
        after = lax.ppermute(first, axis, down)
        x = jnp.concatenate([before, x, after], axis=dim)
    return x


def partner(block, axis, stride):
    count = lax.axis_size(axis)
    route = []
    for low in range(count):
        high = low | 1 << stride
        if high != low and high < count:
            route += [(low, high), (high, low)]
    return lax.ppermute(block, axis, route)


def pair_terms(own, part_ext, perm, q_row, offsets, occupancy, coupling, mask_row, scale):
    width = own.shape[2]
    rim = (part_ext.shape[2] - width) // 2
    part = jnp.take(part_ext, perm, axis=1)
    onehot = (q_row[:, None] == jnp.arange(coupling.shape[0], dtype=jnp.int32)[None, :]).astype(
        jnp.float32
    )
    strength = jnp.dot(
        onehot, coupling, precision=lax.Precision.HIGHEST, preferred_element_type=jnp.float32
    )
    weight = mask_row.astype(jnp.float32)[None, :, None]
    less_own = own[0].astype(jnp.float32) * weight
    sig_less = jnp.zeros(own.shape[1:], jnp.float32)
    sig_great = jnp.zeros(own.shape[1:], jnp.float32)
    columns = []
    for mode in range(coupling.shape[1]):
        shift = offsets[mode]
        above = lax.dynamic_slice_in_dim(part, rim + shift, width, 2).astype(jnp.float32)
        below = lax.dynamic_slice_in_dim(part, rim - shift, width, 2).astype(jnp.float32)
        occ = occupancy[mode]
        factor = strength[:, mode][:, None, None]
        sig_less = sig_less + factor * ((occ + 1.0) * above[0] + occ * below[0])
        sig_great = sig_great + factor * (occ * above[1] + (occ + 1.0) * below[1])
        columns.append(strength[:, mode][:, None] * jnp.sum(less_own * below[1], axis=1) * scale)
    stacked = jnp.stack(columns, axis=1)
    pol = jnp.einsum("kq,kmo->qmo", onehot, stacked, precision=lax.Precision.HIGHEST)
    return (sig_less, sig_great, pol, stacked)


def with_rims(block):
    return padded(block, (("en", 2),), HALO)


def from_partner(block, bit):
    return partner(block, "mom", bit)


def on_device(green, mask, pair_order, q_index, offsets, occupancy, coupling):
    width = green.shape[2]
    scale = 1.0 / (width * lax.axis_size("en"))
    own_ext = with_rims(green)
    total_less = jnp.zeros(green.shape[1:], jnp.float32)
    total_great = jnp.zeros(green.shape[1:], jnp.float32)
    pol_local = jnp.zeros((coupling.shape[0], coupling.shape[1], green.shape[3]), jnp.float32)
    row_terms = []
    row_ids = []
    for rnd in range(ROUNDS + 1):
        if rnd == 0:
            part = own_ext
        else:
            part = with_rims(from_partner(green, rnd - 1))
        less, great, term, stacked = pair_terms(
            green, part, pair_order[rnd, 0], q_index[rnd], offsets, occupancy, coupling, mask, scale
        )
        total_less = total_less + less
        total_great = total_great + great
        pol_local = pol_local + term
        row_terms.append(stacked)
        row_ids.append(q_index[rnd].astype(jnp.float32))
    pol_owned = lax.psum_scatter(
        pol_local.astype(jnp.bfloat16), "mom", scatter_dimension=0, tiled=True
    )
    polarization = lax.psum(pol_owned, "en").astype(jnp.float32)
    weight = mask.astype(jnp.float32)[None, :, None]
    sigma = jnp.stack([total_less * weight, total_great * weight]).astype(jnp.bfloat16)
    return (sigma, polarization)


def solution(mesh):
    in_specs = (
        P(None, "mom", "en", None),
        P("en"),
        P(None, "mom", None),
        P(None, "mom"),
        P(),
        P(),
        P(),
    )
    out_specs = (P(None, "mom", "en", None), P("mom", None, None))
    return jax.shard_map(
        on_device, mesh=mesh, in_specs=in_specs, out_specs=out_specs, check_vma=False
    )
```

profile of v0, /device:TPU:1, one launch (start us, length us, event | category | flops | bytes accessed | tf_op | source)
XLA Modules:
  0.0 383.6 jit_solution(2305330689850090436)
XLA Ops:
  7.2 3.8 collective-permute-start.8
  11.5 6.9 %collective-permute-start.2 = (bf16[2,2,128,256]{3,2,1,0:T(8,128)(2,1)}, bf16[2,2,128,256]{3,2,1,0:T(8,128)(2,1)}, u32[]{:S(2)}, u32[]{:S(2)}) collective-permute-start(bf16[2,2,128,256]{3,2,1,0:T(8,128)(2,1)} %param.9), channel_id=1, source_target_pairs={{0,8},{8,0},{16,24},{24,16},{32,40},{40,32},{48,56},{56,48},{64,72... | collective-permute-start | bytes 786440 | tf_op jit(solution)/shard_map/ppermute | solution.py:30
  19.1 3.4 collective-permute-start.1
  22.6 2.5 collective-permute-start
  59.7 3.8 %constant_dynamic-slice_fusion.13 = (bf16[2,2,128,256]{3,2,0,1:T(8,128)(2,1)S(1)}, bf16[2,2,128,256]{3,2,0,1:T(8,128)(2,1)S(1)}, bf16[2,2,128,256]{3,2,0,1:T(8,1...) fusion(bf16[2,2,136,256]{3,2,0,1:T(8,128)(2,1)S(1)} %select_bit, ...), kind=kLoop, calls=%fused_computation.486 | loop fusion | flops 131072 | bytes 8650816 | tf_op jit(solution)/shard_map/dynamic_slice | solution.py:51
  71.0 1.9 collective-permute-start.10
  72.9 3.6 collective-permute-start.9
  76.6 1.3 fusion.314
  77.9 1.9 collective-permute-start.7
  79.9 3.6 collective-permute-start.6
  83.5 1.4 fusion.313
  84.9 1.9 collective-permute-start.4
  86.8 3.8 collective-permute-start.3
  91.7 1.4 gather_fusion.3
  94.1 1.7 pad_maximum_fusion.2
  95.9 2.3 gather_fusion.2
  99.3 6.4 %dynamic-slice_convert_fusion.14 = (f32[2,2,128,256]{3,2,1,0:T(8,128)}, f32[2,2,128,256]{3,2,1,0:T(8,128)}, f32[2,2,128,256]{3,2,1,0:T(8,128)}, f32[2,2,128,256]...) fusion(bf16[2,2,136,256]{3,2,1,0:T(8,128)(2,1)S(1)} %fusion.1, ...), kind=kLoop, calls=%fused_computation.406 | loop fusion | flops 4194304 | bytes 25165888 | tf_op jit(solution)/shard_map/convert_element_type | solution.py:51
  105.7 1.8 pad_maximum_fusion.1
  107.5 1.6 gather_fusion.1
  110.2 3.0 dynamic-slice_convert_fusion.46
  132.2 14.3 %fusion.9 = bf16[1,2,128,256]{3,2,1,0:T(8,128)(2,1)S(1)} fusion(f32[2,2,128,256]{3,2,1,0:T(8,128)} %get-tuple-element.129, f32[2,2,128,256]{3,2,1,0:T(8,128)} %get-tuple-element.131, f32[2,2,128,256]{3,2,1,0:T(8,128)} %get-tuple-element.133, f32[2,2,128,256]{3,2,1,0:T(8,128)} %get-tuple-element.135, f32[2,2,128,256]{3,2,1,0:T(8,128)} %get-tuple-element.137, ...), kind=kLoop, calls=%fused_computation.25 | loop fusion | flops 10551296 | bytes 16909120 | tf_op jit(solution)/shard_map/convert.2
  146.9 9.6 %fusion.106 = bf16[1,2,128,256]{3,2,1,0:T(8,128)(2,1)S(1)} fusion(f32[2,2,128,256]{3,2,1,0:T(8,128)S(1)} %copy-done.8, f32[2,2,128,256]{3,2,1,0:T(8,128)} %get-tuple-element.129, f32[2,2,128,256]{3,2,1,0:T(8,128)S(1)} %copy-done.10, f32[2,2,128,256]{3,2,1,0:T(8,128)} %get-tuple-element.131, f32[2,2,128,256]{3,2,1,0:T(8,128)S(1)} %copy-done.12, ...), kind=kLoop, calls=%fused_computation.154 | loop fusion | flops 10551296 | bytes 16909120 | tf_op jit(solution)/shard_map/convert.1
  157.3 170.5 %reduce-scatter.2.cloned.1.call-done = bf16[4,8,256]{2,1,0:T(8,128)(2,1)} async-done(((bf16[128,8,256]{2,1,0:T(8,128)(2,1)}), bf16[4,8,256]{2,1,0:T(8,128)(2,1)}) %reduce-scatter.2.cloned.1.call-update) | async-done | bytes 16400 | tf_op jit(solution)/shard_map/reduce_scatter | solution.py:92
  327.8 48.3 %psum.7 = bf16[4,8,256]{2,1,0:T(8,128)(2,1)S(1)} all-reduce(bf16[4,8,256]{2,1,0:T(8,128)(2,1)} %reduce-scatter.2.cloned.1.call-done), channel_id=1, replica_groups=mesh['mom'=32,'en'=8] {'en'}, use_global_device_ids=true, to_apply=%region_33.35 | all-reduce | flops 8192 | bytes 32768 | tf_op jit(solution)/shard_map/psum | solution.py:95
  (269 shorter events, 42.2 us)
Async XLA Ops:
  7.2 23.3 %copy-start = (f32[128,8]{0,1:T(8,128)S(1)}, f32[128,8]{0,1:T(8,128)}, u32[]{:S(2)}) copy-start(f32[128,8]{0,1:T(8,128)} %param.15) | copy-start | bytes 12292
  7.2 320.6 %reduce-scatter.2.cloned.1.call-start = ((), (), s32[]{:S(2)}) async-start(), calls=%async_computation.1 | async-start | bytes 540672 | tf_op jit(solution)/shard_map/reduce_scatter | solution.py:92
  7.2 63.0 %collective-permute-start.8 = (bf16[2,2,128,256]{3,2,1,0:T(8,128)(2,1)}, bf16[2,2,128,256]{3,2,1,0:T(8,128)(2,1)}, u32[]{:S(2)}, u32[]{:S(2)}) collective-permute-start(bf16[2,2,128,256]{3,2,1,0:T(8,128)(2,1)} %param.9), channel_id=1, source_target_pairs={{0,32},{32,0},{8,40},{40,8},{16,48},{48,16},{24,56},{56,24},{64,96... | collective-permute-start | bytes 786440 | tf_op jit(solution)/shard_map/ppermute | solution.py:30
  11.1 65.5 %collective-permute-start.5 = (bf16[2,2,128,256]{3,2,1,0:T(8,128)(2,1)}, bf16[2,2,128,256]{3,2,1,0:T(8,128)(2,1)}, u32[]{:S(2)}, u32[]{:S(2)}) collective-permute-start(bf16[2,2,128,256]{3,2,1,0:T(8,128)(2,1)} %param.9), channel_id=1, source_target_pairs={{0,16},{16,0},{8,24},{24,8},{32,48},{48,32},{40,56},{56,40},{64,80... | collective-permute-start | bytes 786440 | tf_op jit(solution)/shard_map/ppermute | solution.py:30
  11.5 72.1 %collective-permute-start.2 = (bf16[2,2,128,256]{3,2,1,0:T(8,128)(2,1)}, bf16[2,2,128,256]{3,2,1,0:T(8,128)(2,1)}, u32[]{:S(2)}, u32[]{:S(2)}) collective-permute-start(bf16[2,2,128,256]{3,2,1,0:T(8,128)(2,1)} %param.9), channel_id=1, source_target_pairs={{0,8},{8,0},{16,24},{24,16},{32,40},{40,32},{48,56},{56,48},{64,72... | collective-permute-start | bytes 786440 | tf_op jit(solution)/shard_map/ppermute | solution.py:30
  19.1 39.8 %collective-permute-start.1 = (bf16[2,2,4,256]{3,2,1,0:T(4,128)(2,1)S(1)}, bf16[2,2,4,256]{3,2,1,0:T(4,128)(2,1)S(1)}, u32[]{:S(2)}, u32[]{:S(2)}) collective-permute-start(bf16[2,2,4,256]{3,2,1,0:T(4,128)(2,1)S(1)} %get-tuple-element.149), channel_id=1, source_target_pairs={{1,0},{2,1},{3,2},{4,3},{5,4},{6,5},{7,6},{9,8},{10,9},{11,10},{12... | collective-permute-start | bytes 24584 | tf_op jit(solution)/shard_map/ppermute | solution.py:18
  22.6 36.4 %collective-permute-start = (bf16[2,2,4,256]{3,2,1,0:T(4,128)(2,1)S(1)}, bf16[2,2,4,256]{3,2,1,0:T(4,128)(2,1)S(1)}, u32[]{:S(2)}, u32[]{:S(2)}) collective-permute-start(bf16[2,2,4,256]{3,2,1,0:T(4,128)(2,1)S(1)} %get-tuple-element.148), channel_id=1, source_target_pairs={{0,1},{1,2},{2,3},{3,4},{4,5},{5,6},{6,7},{8,9},{9,10},{10,11},{11... | collective-permute-start | bytes 24584 | tf_op jit(solution)/shard_map/ppermute | solution.py:17
  30.6 28.3 %copy-start.59 = (bf16[2,2,128,256]{3,2,1,0:T(8,128)(2,1)S(1)}, bf16[2,2,128,256]{3,2,1,0:T(8,128)(2,1)}, u32[]{:S(2)}) copy-start(bf16[2,2,128,256]{3,2,1,0:T(8,128)(2,1)} %param.9) | copy-start | bytes 786436
  71.0 15.8 %collective-permute-start.10 = (bf16[2,2,4,256]{3,2,1,0:T(4,128)(2,1)S(1)}, bf16[2,2,4,256]{3,2,1,0:T(4,128)(2,1)S(1)}, u32[]{:S(2)}, u32[]{:S(2)}) collective-permute-start(bf16[2,2,4,256]{3,2,1,0:T(4,128)(2,1)S(1)} %get-tuple-element.155), channel_id=1, source_target_pairs={{1,0},{2,1},{3,2},{4,3},{5,4},{6,5},{7,6},{9,8},{10,9},{11,10},{12... | collective-permute-start | bytes 24584 | tf_op jit(solution)/shard_map/ppermute | solution.py:18
  72.9 17.7 %collective-permute-start.9 = (bf16[2,2,4,256]{3,2,1,0:T(4,128)(2,1)S(1)}, bf16[2,2,4,256]{3,2,1,0:T(4,128)(2,1)S(1)}, u32[]{:S(2)}, u32[]{:S(2)}) collective-permute-start(bf16[2,2,4,256]{3,2,1,0:T(4,128)(2,1)S(1)} %get-tuple-element.154), channel_id=1, source_target_pairs={{0,1},{1,2},{2,3},{3,4},{4,5},{5,6},{6,7},{8,9},{9,10},{10,11},{11... | collective-permute-start | bytes 24584 | tf_op jit(solution)/shard_map/ppermute | solution.py:17
  77.9 16.2 %collective-permute-start.7 = (bf16[2,2,4,256]{3,2,1,0:T(4,128)(2,1)}, bf16[2,2,4,256]{3,2,1,0:T(4,128)(2,1)S(1)}, u32[]{:S(2)}, u32[]{:S(2)}) collective-permute-start(bf16[2,2,4,256]{3,2,1,0:T(4,128)(2,1)} %get-tuple-element.153), channel_id=1, source_target_pairs={{1,0},{2,1},{3,2},{4,3},{5,4},{6,5},{7,6},{9,8},{10,9},{11,10},{12... | collective-permute-start | bytes 24584 | tf_op jit(solution)/shard_map/ppermute | solution.py:18
  79.9 14.3 %collective-permute-start.6 = (bf16[2,2,4,256]{3,2,1,0:T(4,128)(2,1)}, bf16[2,2,4,256]{3,2,1,0:T(4,128)(2,1)S(1)}, u32[]{:S(2)}, u32[]{:S(2)}) collective-permute-start(bf16[2,2,4,256]{3,2,1,0:T(4,128)(2,1)} %get-tuple-element.152), channel_id=1, source_target_pairs={{0,1},{1,2},{2,3},{3,4},{4,5},{5,6},{6,7},{8,9},{9,10},{10,11},{11... | collective-permute-start | bytes 24584 | tf_op jit(solution)/shard_map/ppermute | solution.py:17
  84.9 20.8 %collective-permute-start.4 = (bf16[2,2,4,256]{3,2,1,0:T(4,128)(2,1)}, bf16[2,2,4,256]{3,2,1,0:T(4,128)(2,1)S(1)}, u32[]{:S(2)}, u32[]{:S(2)}) collective-permute-start(bf16[2,2,4,256]{3,2,1,0:T(4,128)(2,1)} %get-tuple-element.151), channel_id=1, source_target_pairs={{1,0},{2,1},{3,2},{4,3},{5,4},{6,5},{7,6},{9,8},{10,9},{11,10},{12... | collective-permute-start | bytes 24584 | tf_op jit(solution)/shard_map/ppermute | solution.py:18
  86.8 18.9 %collective-permute-start.3 = (bf16[2,2,4,256]{3,2,1,0:T(4,128)(2,1)}, bf16[2,2,4,256]{3,2,1,0:T(4,128)(2,1)S(1)}, u32[]{:S(2)}, u32[]{:S(2)}) collective-permute-start(bf16[2,2,4,256]{3,2,1,0:T(4,128)(2,1)} %get-tuple-element.150), channel_id=1, source_target_pairs={{0,1},{1,2},{2,3},{3,4},{4,5},{5,6},{6,7},{8,9},{9,10},{10,11},{11... | collective-permute-start | bytes 24584 | tf_op jit(solution)/shard_map/ppermute | solution.py:17
  131.9 14.7 %copy-start.2 = (f32[2,2,128,256]{3,2,1,0:T(8,128)S(1)}, f32[2,2,128,256]{3,2,1,0:T(8,128)}, u32[]{:S(2)}) copy-start(f32[2,2,128,256]{3,2,1,0:T(8,128)} %get-tuple-element.199) | copy-start | bytes 1572868
  131.9 14.7 %copy-start.4 = (f32[2,2,128,256]{3,2,1,0:T(8,128)S(1)}, f32[2,2,128,256]{3,2,1,0:T(8,128)}, u32[]{:S(2)}) copy-start(f32[2,2,128,256]{3,2,1,0:T(8,128)} %get-tuple-element.201) | copy-start | bytes 1572868
  131.9 14.7 %copy-start.6 = (f32[2,2,128,256]{3,2,1,0:T(8,128)S(1)}, f32[2,2,128,256]{3,2,1,0:T(8,128)}, u32[]{:S(2)}) copy-start(f32[2,2,128,256]{3,2,1,0:T(8,128)} %get-tuple-element.127) | copy-start | bytes 1572868
  131.9 14.7 %copy-start.8 = (f32[2,2,128,256]{3,2,1,0:T(8,128)S(1)}, f32[2,2,128,256]{3,2,1,0:T(8,128)}, u32[]{:S(2)}) copy-start(f32[2,2,128,256]{3,2,1,0:T(8,128)} %get-tuple-element.128) | copy-start | bytes 1572868
  132.0 14.7 %copy-start.10 = (f32[2,2,128,256]{3,2,1,0:T(8,128)S(1)}, f32[2,2,128,256]{3,2,1,0:T(8,128)}, u32[]{:S(2)}) copy-start(f32[2,2,128,256]{3,2,1,0:T(8,128)} %get-tuple-element.130) | copy-start | bytes 1572868
  132.0 14.7 %copy-start.12 = (f32[2,2,128,256]{3,2,1,0:T(8,128)S(1)}, f32[2,2,128,256]{3,2,1,0:T(8,128)}, u32[]{:S(2)}) copy-start(f32[2,2,128,256]{3,2,1,0:T(8,128)} %get-tuple-element.132) | copy-start | bytes 1572868
  132.0 14.7 %copy-start.14 = (f32[2,2,128,256]{3,2,1,0:T(8,128)S(1)}, f32[2,2,128,256]{3,2,1,0:T(8,128)}, u32[]{:S(2)}) copy-start(f32[2,2,128,256]{3,2,1,0:T(8,128)} %get-tuple-element.134) | copy-start | bytes 1572868
  132.0 14.7 %copy-start.16 = (f32[2,2,128,256]{3,2,1,0:T(8,128)S(1)}, f32[2,2,128,256]{3,2,1,0:T(8,128)}, u32[]{:S(2)}) copy-start(f32[2,2,128,256]{3,2,1,0:T(8,128)} %get-tuple-element.136) | copy-start | bytes 1572868
  132.0 14.7 %copy-start.18 = (f32[2,2,128,256]{3,2,1,0:T(8,128)S(1)}, f32[2,2,128,256]{3,2,1,0:T(8,128)}, u32[]{:S(2)}) copy-start(f32[2,2,128,256]{3,2,1,0:T(8,128)} %get-tuple-element.138) | copy-start | bytes 1572868
  132.0 14.7 %copy-start.20 = (f32[2,2,128,256]{3,2,1,0:T(8,128)S(1)}, f32[2,2,128,256]{3,2,1,0:T(8,128)}, u32[]{:S(2)}) copy-start(f32[2,2,128,256]{3,2,1,0:T(8,128)} %get-tuple-element.140) | copy-start | bytes 1572868
  (75 other events, 492.4 us)
Sparse Core Ops, SparseCore 0:
  132.0 195.7 reduce-scatter.1
where the time goes:
time: 386 us; the launch traced here: 384 us
  waiting for transfers between devices  171 us (44%)
  other arithmetic  59.2 us (15%)
  blocking collectives  48.3 us (13%)
  between operations  40.2 us (10%)
  starting transfers between devices  34 us (9%)
  local copies, waits for them, and re-layouts  27.8 us (7%)
    reduce_scatter x1, waiting for transfers between devices, on_device(): lax.psum_scatter(pol_local.astype(jnp.bfloat16), 'mom', scatter_dimension...  171 us
    psum x1, blocking collectives, on_device(): polarization = lax.psum(pol_owned, 'en').astype(jnp.float32)  48.3 us
    another operation x2, other arithmetic  24 us
    ppermute x4, starting transfers between devices, padded(): before = lax.ppermute(last, axis, up)  13.6 us
    unnamed x174, local copies, waits for them, and re-layouts  13.4 us
    ppermute x3, starting transfers between devices, partner(): return lax.ppermute(block, axis, route)  11.1 us
    convert_element_type x2, other arithmetic, pair_terms(): lax.dynamic_slice_in_dim(part, rim - shift, width, 2).astype(jnp.float32)  9.44 us
    ppermute x4, starting transfers between devices, padded(): after = lax.ppermute(first, axis, down)  9.16 us
  transfers between devices with their start and end apart: 12, of which 1 were waited for; matrix products, arithmetic and copies ran while one was open for 16% of the time, Pallas kernels for 0%

commit v1 on v0

v1 whole, which is shorter than its diff:
```python
import jax
import jax.numpy as jnp
from jax import lax
from jax.experimental import pallas as pl
from jax.experimental.pallas import tpu as pltpu
from jax.sharding import Mesh, PartitionSpec as P

HALO = 4
AXES = ("x", "y", "zh", "zl", "c")
F32 = jnp.float32
BF16 = jnp.bfloat16
HIGHEST = lax.Precision.HIGHEST
SMEM = pl.BlockSpec(memory_space=pltpu.SMEM)
LIMIT = 48 * 1024 * 1024


def iota(shape, dim):
    return lax.broadcasted_iota(jnp.int32, shape, dim)


def dot(a, b, precision=None):
    return lax.dot_general(
        a, b, (((1,), (0,)), ((), ())), precision=precision, preferred_element_type=F32
    )


def band(dif, above, below):
    out = jnp.zeros(dif.shape, F32)
    for d in range(1, HALO + 1):
        out = jnp.where(dif == d, above[d - 1], out)
        out = jnp.where(dif == -d, below[d - 1], out)
    return out


def pair_products(great, shifted, k):
    great = great.astype(F32)
    return [
        jnp.sum(great * shifted[k * HALO + d].astype(F32), axis=0, keepdims=True)
        for d in range(HALO)
    ]


def prepare_kernel(
    order, q_row, offsets, occupancy, coupling, mask, green, rim, main, edge, place, onehot, shifted, first
):
    width = mask.shape[1]
    modes = coupling.shape[0]
    pairs = q_row.shape[0] * q_row.shape[1]
    kd = q_row.shape[1]
    q_of = [q_row[p // kd, p % kd] for p in range(pairs)]

    q_col = jnp.zeros((pairs, coupling.shape[1]), jnp.int32)
    for p in range(pairs):
        q_col = jnp.where(iota(q_col.shape, 0) == p, q_of[p], q_col)
    chosen = (q_col == iota(q_col.shape, 1)).astype(F32)
    strength = lax.dot_general(
        chosen, coupling[...], (((1,), (1,)), ((), ())), precision=HIGHEST, preferred_element_type=F32
    )
    off_col = jnp.zeros((modes, width), jnp.int32)
    occ_col = jnp.zeros((modes, width), F32)
    for m in range(modes):
        off_col = jnp.where(iota(off_col.shape, 0) == m, offsets[m], off_col)
        occ_col = jnp.where(iota(off_col.shape, 0) == m, occupancy[m], occ_col)
    emit, absorb = [], []
    for d in range(1, HALO + 1):
        emit.append(dot(strength, jnp.where(off_col == d, occ_col + 1.0, 0.0), HIGHEST))
        absorb.append(dot(strength, jnp.where(off_col == d, occ_col, 0.0), HIGHEST))

    row, col = iota((width, width), 0), iota((width, width), 1)
    active = jnp.sum(jnp.where(row == col, mask[...], 0).astype(F32), axis=1, keepdims=True)
    live = jnp.where(active > 0.0, col - row, 2 * width)
    rows = iota((8 * HALO, 2 * 16), 0)
    cols = iota((8 * HALO, 2 * 16), 1)
    source = jnp.where(cols < 16, cols, cols + (width - 32))
    step = rows % HALO
    target = jnp.where(rows < 4 * HALO, width + step, step - HALO)
    part_of = (rows // HALO) % 4
    for comp in range(2):
        for k in range(kd):
            ck = comp * kd + k
            edges = []
            for r in range(pairs // kd):
                p = r * kd + k
                up = [x[p : p + 1, :] for x in emit]
                down = [x[p : p + 1, :] for x in absorb]
                if comp == 1:
                    up, down = down, up
                main[ck, :, r * width : (r + 1) * width] = band(live, up, down).astype(BF16)
                dif = jnp.where(part_of == ck, source - target, 2 * width)
                edges.append(band(dif, [x[:, :32] for x in up], [x[:, :32] for x in down]))
            edge[ck] = jnp.concatenate(edges, axis=1).astype(BF16)
            spot = iota((width, 32), 1)
            to = jnp.where(spot < 16, spot % HALO, width - HALO + spot % HALO)
            hit = (to == iota((width, 32), 0)) & ((spot // HALO) % 4 == ck) & (active > 0.0)
            place[ck] = hit.astype(F32).astype(BF16)

    goal = jnp.zeros((1, pairs * HALO), jnp.int32)
    lane = iota(goal.shape, 1)
    for p in range(pairs):
        goal = jnp.where(lane // HALO == p, q_of[p] * HALO + lane % HALO, goal)
    onehot[...] = (iota(onehot.shape, 0) == goal).astype(F32).astype(BF16)

    weights = jnp.broadcast_to(mask[...], (width, width)).astype(F32)
    for d in range(1, HALO + 1):
        move = jnp.where(col == row + d, weights, 0.0).astype(BF16)
        edge_row, edge_col = iota((width, 16), 0), iota((width, 16), 1)
        wrap = (edge_col + width == edge_row + d).astype(F32).astype(BF16)
        for k in range(kd):
            moved = dot(move, green[0, k]) + dot(wrap, rim[k])
            shifted[k * HALO + d - 1] = moved.astype(BF16)
    lines = []
    for k in range(kd):
        lines += pair_products(green[1, order[0, k]], shifted, k)
    first[...] = jnp.concatenate(lines, axis=0)


def prepare(order, q_row, offsets, occupancy, coupling, mask, green, rim):
    _, kd, width, norb = green.shape
    pairs = q_row.shape[0] * kd
    modes, nq = coupling.shape
    rounds = q_row.shape[0]
    vmem = pl.BlockSpec(memory_space=pltpu.VMEM)
    return pl.pallas_call(
        prepare_kernel,
        out_shape=(
            jax.ShapeDtypeStruct((2 * kd, width, rounds * width), BF16),
            jax.ShapeDtypeStruct((2 * kd, 32, rounds * 32), BF16),
            jax.ShapeDtypeStruct((2 * kd, width, 32), BF16),
            jax.ShapeDtypeStruct((nq * HALO, pairs * HALO), BF16),
            jax.ShapeDtypeStruct((kd * HALO, width, norb), BF16),
            jax.ShapeDtypeStruct((kd * HALO, norb), F32),
        ),
        in_specs=[SMEM, SMEM, SMEM, SMEM, vmem, vmem, vmem, vmem],
        out_specs=(vmem,) * 6,
        compiler_params=pltpu.CompilerParams(vmem_limit_bytes=LIMIT),
        cost_estimate=pl.CostEstimate(flops=2**20, bytes_accessed=2**21, transcendentals=0),
        name="prepare",
    )(order, q_row, offsets, occupancy, coupling, mask, green, rim)


def terms_kernel(order, far, near, next_near, shifted, first, onehot, out):
    lines = [first[...]]
    kd = far.shape[0]
    for r, ref in ((1, far), (2, near), (3, next_near)):
        for k in range(kd):
            index = order[r, k]
            great = ref[index] if r == 1 else ref[0, index]
            lines += pair_products(great, shifted, k)
    terms = jnp.concatenate(lines, axis=0).astype(BF16)
    out[...] = dot(onehot[...], terms).astype(BF16)


def terms(order, far, near, next_near, shifted, first, onehot):
    _, kd, width, norb = near.shape
    vmem = pl.BlockSpec(memory_space=pltpu.VMEM)
    great = pl.BlockSpec((1, kd, width, norb), lambda i: (1, 0, 0, 0))
    return pl.pallas_call(
        terms_kernel,
        grid=(1,),
        out_shape=jax.ShapeDtypeStruct((onehot.shape[0], norb), BF16),
        in_specs=[SMEM, vmem, great, great, vmem, vmem, vmem],
        out_specs=vmem,
        compiler_params=pltpu.CompilerParams(vmem_limit_bytes=LIMIT),
        cost_estimate=pl.CostEstimate(flops=2**20, bytes_accessed=2**20, transcendentals=0),
        name="terms",
    )(order, far, near, next_near, shifted, first, onehot)


def column_kernel(
    order, place, got, edge, own_t, own_b, less_t, less_b, great_t, great_b, near_t, near_b, next_t, next_b, out
):
    total = jnp.sum(got[...].astype(F32), axis=0)
    half = total.shape[0] // 2
    count = out.shape[0] // 2
    for dest in range(out.shape[0]):
        at = (dest // count) * half
        out[dest, :half] = total[at : at + half].astype(BF16)
        out[dest, half:] = jnp.zeros((out.shape[1] - half, out.shape[2]), BF16)
    kd = less_t.shape[0]
    moved = jnp.zeros((32, out.shape[2]), F32)
    for comp in range(2):
        far_t, far_b = (less_t, less_b) if comp == 0 else (great_t, great_b)
        for k in range(kd):
            parts = []
            for r, (top, bottom) in enumerate(
                ((own_t, own_b), (far_t, far_b), (near_t, near_b), (next_t, next_b))
            ):
                index = order[r, k]
                if r == 1:
                    parts += [top[index], bottom[index]]
                else:
                    parts += [top[comp, index], bottom[comp, index]]
            moved = moved + dot(edge[comp * kd + k], jnp.concatenate(parts, axis=0))
    block = place[0]
    me = place[1]

    @pl.when(me < count - 1)
    def _():
        out[block * count + me + 1, half:] = moved[:16].astype(BF16)

    @pl.when(me > 0)
    def _():
        out[block * count + me - 1, half:] = moved[16:].astype(BF16)


def column(order, place, got, edge, own, less, great, near, next_near):
    _, kd, width, norb = own.shape
    vmem = pl.BlockSpec(memory_space=pltpu.VMEM)
    last = width // 16 - 1
    top4 = pl.BlockSpec((2, kd, 16, norb), lambda i: (0, 0, 0, 0))
    low4 = pl.BlockSpec((2, kd, 16, norb), lambda i: (0, 0, last, 0))
    top3 = pl.BlockSpec((kd, 16, norb), lambda i: (0, 0, 0))
    low3 = pl.BlockSpec((kd, 16, norb), lambda i: (0, last, 0))
    return pl.pallas_call(
        column_kernel,
        grid=(1,),
        out_shape=jax.ShapeDtypeStruct((16, 32, norb), BF16),
        in_specs=[SMEM, SMEM, vmem, vmem, top4, low4, top3, low3, top3, low3, top4, low4, top4, low4],
        out_specs=vmem,
        compiler_params=pltpu.CompilerParams(vmem_limit_bytes=LIMIT),
        cost_estimate=pl.CostEstimate(flops=2**20, bytes_accessed=2**20, transcendentals=0),
        name="column",
    )(order, place, got, edge, own, own, less, less, great, great, near, near, next_near, next_near)


def finish_kernel(
    order, place, offsets, coupling, got, main, spots, own, less, great, near, next_near, sigma, pol, total
):
    kd = less.shape[0]
    half = got.shape[1] // 2
    count = got.shape[0] // 2
    me = place[1]
    base = place[0] * count
    before = got[base + jnp.maximum(me - 1, 0), half:]
    after = got[base + jnp.minimum(me + 1, count - 1), half:]
    before = jnp.where(me > 0, before.astype(F32), 0.0).astype(BF16)
    after = jnp.where(me < count - 1, after.astype(F32), 0.0).astype(BF16)
    rims = jnp.concatenate([before, after], axis=0)
    for comp in range(2):
        far = less if comp == 0 else great
        for k in range(kd):
            ck = comp * kd + k
            blocks = [own[comp, order[0, k]], far[order[1, k]]]
            blocks += [near[comp, order[2, k]], next_near[comp, order[3, k]]]
            acc = dot(main[ck], jnp.concatenate(blocks, axis=0)) + dot(spots[ck], rims)
            sigma[comp, k] = acc.astype(BF16)
    total[...] = jnp.sum(got[:, :half].astype(F32), axis=0)
    scale = place[2].astype(F32)
    scale = 1.0 / scale
    for j in range(pol.shape[0]):
        for m in range(pol.shape[1]):
            factor = coupling[m, place[3] + j] * scale
            pol[j, m : m + 1, :] = factor * total[pl.ds(j * HALO + offsets[m] - 1, 1), :]


def finish(order, place, offsets, coupling, got, main, spots, own, less, great, near, next_near, owned):
    norb = own.shape[3]
    vmem = pl.BlockSpec(memory_space=pltpu.VMEM)
    return pl.pallas_call(
        finish_kernel,
        out_shape=(
            jax.ShapeDtypeStruct(own.shape, BF16),
            jax.ShapeDtypeStruct((owned, coupling.shape[0], norb), F32),
        ),
        in_specs=[SMEM] * 4 + [vmem] * 8,
        out_specs=(vmem, vmem),
        scratch_shapes=[pltpu.VMEM((got.shape[1] // 2, norb), F32)],
        compiler_params=pltpu.CompilerParams(vmem_limit_bytes=LIMIT),
        cost_estimate=pl.CostEstimate(flops=2**24, bytes_accessed=2**21, transcendentals=0),
        name="finish",
    )(order, place, offsets, coupling, got, main, spots, own, less, great, near, next_near)


def on_device(green, mask, pair_order, q_index, offsets, occupancy, coupling):
    _, kd, width, norb = green.shape
    count = lax.axis_size(("zl", "c"))
    owned = coupling.shape[0] // lax.axis_size(("x", "y", "zh"))
    order = pair_order[:, 0]
    spread = coupling.T
    place = jnp.stack(
        [
            lax.axis_index("zh"),
            lax.axis_index(("zl", "c")),
            width * count,
            lax.axis_index(("x", "y", "zh")) * owned,
        ]
    ).astype(jnp.int32)

    swap = [(0, 1), (1, 0)]
    great = lax.ppermute(green[1], "zh", swap)
    rim = green[0, :, :16] * mask[None, :16, None].astype(BF16)
    rim = lax.ppermute(rim, ("zl", "c"), [(i + 1, i) for i in range(count - 1)])
    near = lax.ppermute(green, "y", [(i, i ^ 1) for i in range(4)])
    next_near = lax.ppermute(green, "y", [(i, i ^ 2) for i in range(4)])
    main, edge, spots, onehot, shifted, first = prepare(
        order, q_index, offsets, occupancy, spread, mask[None, :], green, rim
    )
    held, first = lax.optimization_barrier((green[0], first))
    less = lax.ppermute(held, "zh", swap)

    dense = terms(order, great, near, next_near, shifted, first, onehot)
    got = lax.all_to_all(dense.reshape(16, -1, norb), ("x", "y"), 0, 0, tiled=True)
    sent = column(order, place, got, edge, green, less, great, near, next_near)
    got = lax.all_to_all(sent, ("zh", "zl", "c"), 0, 0, tiled=True)
    return finish(
        order, place, offsets, spread, got, main, spots, green, less, great, near, next_near, owned
    )


def solution(mesh):
    split = Mesh(mesh.devices.reshape(4, 4, 2, 4, 2), AXES)
    mom, en = ("x", "y", "zh"), ("zl", "c")
    in_specs = (P(None, mom, en, None), P(en), P(None, mom, None), P(None, mom), P(), P(), P())
    out_specs = (P(None, mom, en, None), P(mom, None, None))
    return jax.shard_map(
        on_device, mesh=split, in_specs=in_specs, out_specs=out_specs, check_vma=False
    )
```

time: 386 us -> 58.3 us (0.15)
  waiting for transfers between devices: 171 us -> 10.9 us
  other arithmetic: 59.2 us -> 0.15 us
  between operations: 40.2 us -> 0.72 us
  blocking collectives: 48.3 us -> 18 us
  local copies, waits for them, and re-layouts: 27.8 us -> 2.44 us
  starting transfers between devices: 34 us -> 19.8 us
  Pallas kernels: 0 us -> 5.94 us
    reduce_scatter x1 -> x0, waiting for transfers between devices: 171 us -> none  [on_device(): lax.psum_scatter(pol_local.astype(jnp.bfloat16), 'mom', scatter_dimension...]
    psum x1 -> x0, blocking collectives: 48.3 us -> none  [on_device(): polarization = lax.psum(pol_owned, 'en').astype(jnp.float32)]
    another operation x7 -> x2, other arithmetic: 25 us -> 0.08 us  [the longest x1 0.08 us: on_device(): jnp.stack([lax.axis_index('zh'), lax.axis_index(('zl', 'c')), width * cou...]
    ppermute x11 -> x5, starting transfers between devices: 33.9 us -> 15.6 us  [the longest x1 7 us: on_device(): great = lax.ppermute(green[1], 'zh', swap)]
    all_to_all x0 -> x1, blocking collectives: none -> 18 us  [on_device(): got = lax.all_to_all(sent, ('zh', 'zl', 'c'), 0, 0, tiled=True)]
    convert_element_type x11 -> x0, other arithmetic: 16.8 us -> none  [the longest x2 9.44 us: pair_terms(): lax.dynamic_slice_in_dim(part, rim - shift, width, 2).astype(jnp.float32)]
    unnamed x174 -> x15, local copies, waits for them, and re-layouts: 13.4 us -> 1.36 us
    ppermute x11 -> x5, waiting for transfers between devices: 0.03 us -> 10.9 us  [the longest x1 7.59 us: on_device(): less = lax.ppermute(held, 'zh', swap)]
  transfers between devices with their start and end apart: 12 -> 6, of which waited for: 1 -> 2; matrix products, arithmetic and copies ran while one was open for 16% -> 2% of each run, Pallas kernels for 0% -> 3%
where the time goes in v1:
time: 58.3 us; the launch traced here: 57.9 us
  starting transfers between devices  19.8 us (34%)
  blocking collectives  18 us (31%)
  waiting for transfers between devices  10.9 us (19%)
  Pallas kernels  5.94 us (10%)
  local copies, waits for them, and re-layouts  2.44 us (4%)
  between operations  0.72 us (1%)
    all_to_all x1, blocking collectives, on_device(): got = lax.all_to_all(sent, ('zh', 'zl', 'c'), 0, 0, tiled=True)  18 us
    ppermute x1, waiting for transfers between devices, on_device(): less = lax.ppermute(held, 'zh', swap)  7.59 us
    ppermute x1, starting transfers between devices, on_device(): great = lax.ppermute(green[1], 'zh', swap)  7 us
    all_to_all x1, starting transfers between devices, on_device(): lax.all_to_all(dense.reshape(16, -1, norb), ('x', 'y'), 0, 0, tiled=True)  4.18 us
    ppermute x1, starting transfers between devices, on_device(): rim = lax.ppermute(rim, ('zl', 'c'), [(i + 1, i) for i in range(count - 1)])  3.55 us
    ppermute x1, waiting for transfers between devices, on_device(): rim = lax.ppermute(rim, ('zl', 'c'), [(i + 1, i) for i in range(count - 1)])  3.26 us
    ppermute x1, starting transfers between devices, on_device(): next_near = lax.ppermute(green, 'y', [(i, i ^ 2) for i in range(4)])  2.62 us
    ppermute x1, starting transfers between devices, on_device(): near = lax.ppermute(green, 'y', [(i, i ^ 1) for i in range(4)])  2.21 us
  transfers between devices with their start and end apart: 6, of which 2 were waited for; matrix products, arithmetic and copies ran while one was open for 2% of the time, Pallas kernels for 3%

profile of v1, /device:TPU:1, one launch (start us, length us, event | category | flops | bytes accessed | tf_op | source)
XLA Modules:
  0.0 57.9 jit_solution(5023451874182978643)
XLA Ops:
  0.6 2.2 %collective-permute-start.1 = (bf16[2,2,128,256]{3,2,1,0:T(8,128)(2,1)}, bf16[2,2,128,256]{3,2,1,0:T(8,128)(2,1)S(1)}, u32[]{:S(2)}, u32[]{:S(2)}) collective-permute-start(bf16[2,2,128,256]{3,2,1,0:T(8,128)(2,1)} %own.1), channel_id=1, source_target_pairs={{0,16},{16,0},{32,48},{48,32},{1,17},{17,1},{33,49},{49,33},{2,18}... | collective-permute-start | bytes 786440 | tf_op jit(solution)/shard_map/ppermute | solution.py:293
  2.9 2.6 %collective-permute-start.2 = (bf16[2,2,128,256]{3,2,1,0:T(8,128)(2,1)}, bf16[2,2,128,256]{3,2,1,0:T(8,128)(2,1)S(1)}, u32[]{:S(2)}, u32[]{:S(2)}) collective-permute-start(bf16[2,2,128,256]{3,2,1,0:T(8,128)(2,1)} %own.1), channel_id=1, source_target_pairs={{0,32},{16,48},{32,0},{48,16},{1,33},{17,49},{33,1},{49,17},{2,34}... | collective-permute-start | bytes 786440 | tf_op jit(solution)/shard_map/ppermute | solution.py:294
  5.5 1.0 %slice_bitcast_fusion = (bf16[2,128,256]{2,1,0:T(8,128)(2,1)S(1)}, bf16[2,128,256]{2,1,0:T(8,128)(2,1)S(1)}) fusion(bf16[2,2,128,256]{3,2,1,0:T(8,128)(2,1)} %own.1), kind=kLoop, calls=%fused_computation | loop fusion | bytes 524288 | tf_op jit(solution)/shard_map/squeeze | solution.py:298
  6.5 0.0 copy-start.4
  6.5 7.0 %collective-permute-start = (bf16[2,128,256]{2,1,0:T(8,128)(2,1)S(1)}, bf16[2,128,256]{2,1,0:T(8,128)(2,1)S(1)}, u32[]{:S(2)}, u32[]{:S(2)}) collective-permute-start(bf16[2,128,256]{2,1,0:T(8,128)(2,1)S(1)} %get-tuple-element.19), channel_id=1, source_target_pairs={{0,8},{8,0},{1,9},{9,1},{2,10},{10,2},{3,11},{11,3},{4,12},{12,4},... | collective-permute-start | bytes 393224 | tf_op jit(solution)/shard_map/ppermute | solution.py:290
  13.5 0.1 bitcast_multiply_fusion
  13.6 3.5 %collective-permute-start.3 = (bf16[2,16,256]{2,1,0:T(8,128)(2,1)S(1)}, bf16[2,16,256]{2,1,0:T(8,128)(2,1)S(1)}, u32[]{:S(2)}, u32[]{:S(2)}) collective-permute-start(bf16[2,16,256]{2,1,0:T(8,128)(2,1)S(1)} %bitcast_multiply_fusion), channel_id=1, source_target_pairs={{1,0},{2,1},{3,2},{4,3},{5,4},{6,5},{7,6},{9,8},{10,9},{11,10},{12... | collective-permute-start | bytes 49160 | tf_op jit(solution)/shard_map/ppermute | solution.py:292
  17.1 0.0 copy-start.6
  17.1 0.1 copy.13.order
  17.2 0.6 copy-done.6
  17.8 0.1 copy.10.q_row
  17.9 3.3 %collective-permute-done.3.rim = bf16[2,16,256]{2,1,0:T(8,128)(2,1)S(1)} collective-permute-done((bf16[2,16,256]{2,1,0:T(8,128)(2,1)S(1)}, bf16[2,16,256]{2,1,0:T(8,128)(2,1)S(1)}, u32[]{:S(2)}, u32[]{:S(2)}) %collective-permute-start.3) | collective-permute-done | bytes 16416 | tf_op jit(solution)/shard_map/ppermute | solution.py:292
  21.2 0.6 %copy-done.2 = s32[8]{0:T(128)S(1)} copy-done((s32[8]{0:T(128)S(1)}, s32[8]{0:T(128)}, u32[]{:S(2)}) %copy-start.2) | copy-done | bytes 56
  21.8 0.0 copy-done.3
  21.8 1.9 %prepare.1 = (bf16[4,128,512]{2,1,0:T(8,128)(2,1)S(1)}, bf16[4,32,128]{2,1,0:T(8,128)(2,1)S(1)}, bf16[4,128,32]{2,1,0:T(8,128)(2,1)S(1)}, bf16[512,32]{1,0:T(8,1...) custom-call(s32[4,2]{1,0:T(4,128)S(1)} %copy.13.order, s32[4,2]{1,0:T(4,128)S(1)} %copy.10.q_row, ...), custom_call_target="tpu_custom_call" | custom-call | flops 1048576 | bytes 2097152 | tf_op jit(solution)/shard_map/prepare/pallas_call | solution.py:123
  23.7 0.0 collective-permute-done.1.near.near_t.near_b
  23.8 1.6 %terms.1 = bf16[512,256]{1,0:T(8,128)(2,1)} custom-call(s32[4,2]{1,0:T(4,128)S(1)} %copy.13.order, bf16[2,128,256]{2,1,0:T(8,128)(2,1)S(1)} %collective-permute-done.far.great_t.great_b.great, bf16[2,2,128,256]{3,2,1,0:T(8,128)(2,1)S(1)} %collective-permute-done.1.near.near_t.near_b, ...), custom_call_target="tpu_custom_call" | custom-call | flops 1048576 | bytes 1048576 | tf_op jit(solution)/shard_map/terms/pallas_call | solution.py:157
  25.4 4.2 %all-to-all-start = ((bf16[16,32,256]{2,1,0:T(8,128)(2,1)}), bf16[16,32,256]{2,1,0:T(8,128)(2,1)S(1)}, u32[]{:S(2)}, u32[]{:S(2)}) async-start(bf16[16,32,256]{2,1,0:T(8,128)(2,1)} %bitcast.9), calls=%async_computation | async-start | bytes 524288 | tf_op jit(solution)/shard_map/all_to_all | solution.py:302
  29.5 0.3 collective-permute-start.4
  29.8 0.1 pad_add_fusion.place
  29.9 7.6 %collective-permute-done.4.less_t.less_b.less = bf16[2,128,256]{2,1,0:T(8,128)(2,1)S(1)} collective-permute-done((bf16[2,128,256]{2,1,0:T(8,128)(2,1)S(1)}, bf16[2,128,256]{2,1,0:T(8,128)(2,1)S(1)}, u32[]{:S(2)}, u32[]{:S(2)}) %collective-permute-start.4) | collective-permute-done | bytes 131104 | tf_op jit(solution)/shard_map/ppermute | solution.py:299
  37.5 0.7 %column.1 = bf16[16,32,256]{2,1,0:T(8,128)(2,1)S(1)} custom-call(s32[4,2]{1,0:T(4,128)S(1)} %copy.13.order, s32[4]{0:T(128)S(1)} %pad_add_fusion.place, bf16[16,32,256]{2,1,0:T(8,128)(2,1)S(1)} %all-to-all-done.got, bf16[4,32,128]{2,1,0:T(8,128)(2,1)S(1)} %get-tuple-element.14.edge, bf16[2,2,128,256]{3,2,1,0:T(8,128)(2,1)S(1)} %copy-done, ...), custom_call_target="tpu_custom_call" | custom-call | flops 1048576 | bytes 1048576 | tf_op jit(solution)/shard_map/column/pallas_call | solution.py:214
  38.2 18.0 %all_to_all.10.got = bf16[16,32,256]{2,1,0:T(8,128)(2,1)S(1)} all-to-all(bf16[16,32,256]{2,1,0:T(8,128)(2,1)S(1)} %column.1), channel_id=1, replica_groups=mesh['x'=4,'y'=4,'zh'=2,'zl'=4,'c'=2] {'zh','zl','c'}, dimensions={0} | all-to-all | bytes 524288 | tf_op jit(solution)/shard_map/all_to_all | solution.py:304
  56.2 1.7 %finish.1 = (bf16[2,2,128,256]{3,2,1,0:T(8,128)(2,1)}, f32[4,8,256]{2,1,0:T(8,128)}) custom-call(s32[4,2]{1,0:T(4,128)S(1)} %copy.13.order, s32[4]{0:T(128)S(1)} %pad_add_fusion.place, s32[8]{0:T(128)S(1)} %copy-done.2, f32[8,128]{1,0:T(8,128)S(1)} %bitcast.15, bf16[16,32,256]{2,1,0:T(8,128)(2,1)S(1)} %all_to_all.10.got, ...), custom_call_target="tpu_custom_call" | custom-call | flops 16777216 | bytes 2097152 | tf_op jit(solution)/shard_map/finish/pallas_call | solution.py:259
  (13 shorter events, 0.0 us)
Async XLA Ops:
  0.6 12.9 %copy-start = (bf16[2,2,128,256]{3,2,1,0:T(8,128)(2,1)S(1)}, bf16[2,2,128,256]{3,2,1,0:T(8,128)(2,1)}, u32[]{:S(2)}) copy-start(bf16[2,2,128,256]{3,2,1,0:T(8,128)(2,1)} %own.1) | copy-start | bytes 786436
  0.6 23.1 %collective-permute-start.1 = (bf16[2,2,128,256]{3,2,1,0:T(8,128)(2,1)}, bf16[2,2,128,256]{3,2,1,0:T(8,128)(2,1)S(1)}, u32[]{:S(2)}, u32[]{:S(2)}) collective-permute-start(bf16[2,2,128,256]{3,2,1,0:T(8,128)(2,1)} %own.1), channel_id=1, source_target_pairs={{0,16},{16,0},{32,48},{48,32},{1,17},{17,1},{33,49},{49,33},{2,18}... | collective-permute-start | bytes 786440 | tf_op jit(solution)/shard_map/ppermute | solution.py:293
  2.9 20.9 %collective-permute-start.2 = (bf16[2,2,128,256]{3,2,1,0:T(8,128)(2,1)}, bf16[2,2,128,256]{3,2,1,0:T(8,128)(2,1)S(1)}, u32[]{:S(2)}, u32[]{:S(2)}) collective-permute-start(bf16[2,2,128,256]{3,2,1,0:T(8,128)(2,1)} %own.1), channel_id=1, source_target_pairs={{0,32},{16,48},{32,0},{48,16},{1,33},{17,49},{33,1},{49,17},{2,34}... | collective-permute-start | bytes 786440 | tf_op jit(solution)/shard_map/ppermute | solution.py:294
  6.5 7.0 %copy-start.4 = (s32[128]{0:T(128)S(1)}, s32[128]{0:T(128)}, u32[]{:S(2)}) copy-start(s32[128]{0:T(128)} %param.8) | copy-start | bytes 1540
  6.5 17.2 %collective-permute-start = (bf16[2,128,256]{2,1,0:T(8,128)(2,1)S(1)}, bf16[2,128,256]{2,1,0:T(8,128)(2,1)S(1)}, u32[]{:S(2)}, u32[]{:S(2)}) collective-permute-start(bf16[2,128,256]{2,1,0:T(8,128)(2,1)S(1)} %get-tuple-element.19), channel_id=1, source_target_pairs={{0,8},{8,0},{1,9},{9,1},{2,10},{10,2},{3,11},{11,3},{4,12},{12,4},... | collective-permute-start | bytes 393224 | tf_op jit(solution)/shard_map/ppermute | solution.py:290
  13.6 3.6 %copy-start.5 = (s32[4,1,2]{0,2,1:T(2,128)S(1)}, s32[4,1,2]{0,2,1:T(2,128)}, u32[]{:S(2)}) copy-start(s32[4,1,2]{0,2,1:T(2,128)} %param.9) | copy-start | bytes 100
  13.6 7.6 %collective-permute-start.3 = (bf16[2,16,256]{2,1,0:T(8,128)(2,1)S(1)}, bf16[2,16,256]{2,1,0:T(8,128)(2,1)S(1)}, u32[]{:S(2)}, u32[]{:S(2)}) collective-permute-start(bf16[2,16,256]{2,1,0:T(8,128)(2,1)S(1)} %bitcast_multiply_fusion), channel_id=1, source_target_pairs={{1,0},{2,1},{3,2},{4,3},{5,4},{6,5},{7,6},{9,8},{10,9},{11,10},{12... | collective-permute-start | bytes 49160 | tf_op jit(solution)/shard_map/ppermute | solution.py:292
  17.1 0.7 %copy-start.6 = (s32[4,2]{0,1:T(2,128)S(1)}, s32[4,2]{0,1:T(2,128)}, u32[]{:S(2)}) copy-start(s32[4,2]{0,1:T(2,128)} %param.10) | copy-start | bytes 100
  17.8 3.4 %copy-start.1 = (f32[128,8]{0,1:T(8,128)S(1)}, f32[128,8]{0,1:T(8,128)}, u32[]{:S(2)}) copy-start(f32[128,8]{0,1:T(8,128)} %param.13) | copy-start | bytes 12292
  21.2 0.7 %copy-start.2 = (s32[8]{0:T(128)S(1)}, s32[8]{0:T(128)}, u32[]{:S(2)}) copy-start(s32[8]{0:T(128)} %offsets.3) | copy-start | bytes 100
  21.2 0.7 %copy-start.3 = (f32[8]{0:T(128)S(1)}, f32[8]{0:T(128)}, u32[]{:S(2)}) copy-start(f32[8]{0:T(128)} %occupancy.1) | copy-start | bytes 100
  25.4 12.1 %all-to-all-start = ((bf16[16,32,256]{2,1,0:T(8,128)(2,1)}), bf16[16,32,256]{2,1,0:T(8,128)(2,1)S(1)}, u32[]{:S(2)}, u32[]{:S(2)}) async-start(bf16[16,32,256]{2,1,0:T(8,128)(2,1)} %bitcast.9), calls=%async_computation | async-start | bytes 524288 | tf_op jit(solution)/shard_map/all_to_all | solution.py:302
  29.5 7.9 %collective-permute-start.4 = (bf16[2,128,256]{2,1,0:T(8,128)(2,1)S(1)}, bf16[2,128,256]{2,1,0:T(8,128)(2,1)S(1)}, u32[]{:S(2)}, u32[]{:S(2)}) collective-permute-start(bf16[2,128,256]{2,1,0:T(8,128)(2,1)S(1)} %get-tuple-element.15), channel_id=1, source_target_pairs={{0,8},{8,0},{1,9},{9,1},{2,10},{10,2},{3,11},{11,3},{4,12},{12,4},... | collective-permute-start | bytes 393224 | tf_op jit(solution)/shard_map/ppermute | solution.py:299

commit v2 on v0

v2 whole, which is shorter than its diff:
```python
import functools

import jax
import jax.numpy as jnp
from jax import lax
from jax.experimental import pallas as pl
from jax.experimental.pallas import tpu as pltpu
from jax.sharding import Mesh, PartitionSpec as P

HALO = 4
AXES = ("x", "y", "zh", "zl", "c")
F32 = jnp.float32
BF16 = jnp.bfloat16
HIGHEST = lax.Precision.HIGHEST
SMEM = pl.BlockSpec(memory_space=pltpu.SMEM)
LIMIT = 40 * 1024 * 1024
VMEM = pl.BlockSpec(memory_space=pltpu.VMEM)


def iota(shape, dim):
    return lax.broadcasted_iota(jnp.int32, shape, dim)


def dot(a, b, precision=None):
    return lax.dot_general(
        a, b, (((1,), (0,)), ((), ())), precision=precision, preferred_element_type=F32
    )


def band(dif, above, below):
    out = jnp.zeros(dif.shape, F32)
    for d in range(1, HALO + 1):
        out = jnp.where(dif == d, above[d - 1], out)
        out = jnp.where(dif == -d, below[d - 1], out)
    return out


def pair_products(great, shifted, k):
    great = great.astype(F32)
    return [
        jnp.sum(great * shifted[k * HALO + d].astype(F32), axis=0, keepdims=True)
        for d in range(HALO)
    ]


def call(kernel, name, outs, specs, args, scratch=(), flops=2**20):
    return pl.pallas_call(
        kernel,
        out_shape=outs,
        in_specs=specs,
        out_specs=jax.tree.map(lambda _: VMEM, outs),
        scratch_shapes=scratch,
        compiler_params=pltpu.CompilerParams(vmem_limit_bytes=LIMIT),
        cost_estimate=pl.CostEstimate(flops=flops, bytes_accessed=2**20, transcendentals=0),
        name=name,
    )(*args)


def shape(*dims, dtype=BF16):
    return jax.ShapeDtypeStruct(dims, dtype)


def shift_kernel(order, q_row, mask, green, onehot, shifted, first):
    kd, rounds = order.shape
    width = mask.shape[1]
    goal = jnp.zeros((1, onehot.shape[1]), jnp.int32)
    lane = iota(goal.shape, 1)
    for p in range(rounds * kd):
        goal = jnp.where(lane // HALO == p, q_row[p % kd, p // kd] * HALO + lane % HALO, goal)
    onehot[...] = (iota(onehot.shape, 0) == goal).astype(F32).astype(BF16)

    row, col = iota((width, width), 0), iota((width, width), 1)
    weights = jnp.broadcast_to(mask[...], (width, width)).astype(F32)
    for d in range(1, HALO + 1):
        move = jnp.where(col == row + d, weights, 0.0).astype(BF16)
        for k in range(kd):
            shifted[k * HALO + d - 1] = dot(move, green[0, k]).astype(BF16)
    lines = []
    for k in range(kd):
        lines += pair_products(green[1, order[k, 0]], shifted, k)
    first[...] = jnp.concatenate(lines, axis=0)


def tail_kernel(order, green, shifted, rim, first, tail, total):
    kd, width = green.shape[1:3]
    rows, cols = iota((16, 16), 0), iota((16, 16), 1)
    lines = []
    for k in range(kd):
        last = green[1, order[k, 0], width - 16 :].astype(F32)
        for d in range(1, HALO + 1):
            wrap = (cols + 16 == rows + d).astype(F32).astype(BF16)
            at = k * HALO + d - 1
            moved = dot(wrap, rim[k])
            tail[at] = (shifted[at, width - 16 :].astype(F32) + moved).astype(BF16)
            lines.append(jnp.sum(last * moved, axis=0, keepdims=True))
    total[...] = first[...] + jnp.concatenate(lines, axis=0)


def terms_kernel(order, far, near, next_near, shifted, tail, first, onehot, out):
    lines = [first[...]]
    kd, width, _ = far.shape
    for r, ref in ((1, far), (2, near), (3, next_near)):
        for k in range(kd):
            great = ref[order[k, r]].astype(F32)
            for d in range(HALO):
                at = k * HALO + d
                body = great[: width - 16] * shifted[at, : width - 16].astype(F32)
                end = great[width - 16 :] * tail[at].astype(F32)
                lines.append(
                    jnp.sum(body, axis=0, keepdims=True) + jnp.sum(end, axis=0, keepdims=True)
                )
    terms = jnp.concatenate(lines, axis=0).astype(BF16)
    out[...] = dot(onehot[...], terms).astype(BF16)


def column_kernel(got, out):
    total = jnp.sum(got[...].astype(F32), axis=0).astype(BF16)
    half = out.shape[1]
    for dest in range(out.shape[0]):
        at = (dest // (out.shape[0] // 2)) * half
        out[dest] = total[at : at + half]


def weights_kernel(q_row, place, offsets, occupancy, coupling, mask, main, edge, owner, *, scale):
    kd, rounds = q_row.shape
    width = mask.shape[1]
    modes = coupling.shape[0]
    pairs = rounds * kd

    q_col = jnp.zeros((pairs, coupling.shape[1]), jnp.int32)
    for p in range(pairs):
        q_col = jnp.where(iota(q_col.shape, 0) == p, q_row[p % kd, p // kd], q_col)
    chosen = (q_col == iota(q_col.shape, 1)).astype(F32)
    strength = lax.dot_general(
        chosen, coupling[...], (((1,), (1,)), ((), ())), precision=HIGHEST, preferred_element_type=F32
    )
    off_col = jnp.zeros((modes, width), jnp.int32)
    occ_col = jnp.zeros((modes, width), F32)
    for m in range(modes):
        off_col = jnp.where(iota(off_col.shape, 0) == m, offsets[m], off_col)
        occ_col = jnp.where(iota(off_col.shape, 0) == m, occupancy[m], occ_col)
    emit, absorb = [], []
    for d in range(1, HALO + 1):
        emit.append(dot(strength, jnp.where(off_col == d, occ_col + 1.0, 0.0), HIGHEST))
        absorb.append(dot(strength, jnp.where(off_col == d, occ_col, 0.0), HIGHEST))

    rows, cols = iota(owner.shape, 0), iota(owner.shape, 1)
    wide = (owner.shape[0], coupling.shape[1])
    mine = (iota(wide, 1) == place[0] + iota(wide, 0) // modes).astype(F32)
    factor = lax.dot_general(
        mine, coupling[...], (((1,), (1,)), ((), ())), precision=HIGHEST, preferred_element_type=F32
    )
    branch = iota(factor.shape, 1) == iota(factor.shape, 0) % modes
    factor = jnp.sum(jnp.where(branch, factor, 0.0), axis=1, keepdims=True) * scale
    off = jnp.zeros(owner.shape, jnp.int32)
    for m in range(modes):
        off = jnp.where(rows % modes == m, offsets[m], off)
    hit = (rows // modes == cols // HALO) & (off == cols % HALO + 1)
    owner[...] = jnp.where(hit, factor, 0.0)

    row, col = iota((width, width), 0), iota((width, width), 1)
    active = jnp.sum(jnp.where(row == col, mask[...], 0).astype(F32), axis=1, keepdims=True)
    live = jnp.where(active > 0.0, col - row, 2 * width)
    rows, cols = iota((32, 32), 0), iota((32, 32), 1)
    source = jnp.where(cols < 16, cols, cols + (width - 32))
    target = jnp.where(rows < 16, width + rows % HALO, rows % HALO - HALO)
    part_of = (rows // HALO) % 4
    for comp in range(2):
        for k in range(kd):
            ck = comp * kd + k
            dif = jnp.where(part_of == ck, source - target, 2 * width)
            edges = []
            for r in range(rounds):
                p = r * kd + k
                up = [x[p : p + 1, :] for x in emit]
                down = [x[p : p + 1, :] for x in absorb]
                if comp == 1:
                    up, down = down, up
                main[ck, :, r * width : (r + 1) * width] = band(live, up, down).astype(BF16)
                edges.append(band(dif, [x[:, :32] for x in up], [x[:, :32] for x in down]))
            edge[ck] = jnp.concatenate(edges, axis=1).astype(BF16)


def sigma_kernel(
    order, place, main, edge, own, less1, less2, less3, great1, great2, great3, _after,
    sigma, rims, core_edge, chip_edge
):
    kd, rounds = order.shape
    width = own.shape[2]
    moved = jnp.zeros((32, own.shape[3]), F32)
    for comp in range(2):
        for k in range(kd):
            ck = comp * kd + k
            others = (less1, less2, less3) if comp == 0 else (great1, great2, great3)
            blocks = [own[comp, order[k, 0]]]
            blocks += [x[order[k, r + 1]] for r, x in enumerate(others)]
            ends = []
            for x in blocks:
                ends += [x[:16], x[width - 16 :]]
            acc = dot(main[ck], jnp.concatenate(blocks, axis=0))
            sigma[comp, k] = acc.astype(BF16)
            rims[ck, :16] = acc[:16]
            rims[ck, 16:] = acc[width - 16 :]
            moved = moved + dot(edge[ck], jnp.concatenate(ends, axis=0))
    first_core = jnp.broadcast_to(place[1], (16, moved.shape[1])) == 0
    core_edge[...] = jnp.where(first_core, moved[:16], moved[16:]).astype(BF16)
    chip_edge[...] = jnp.where(first_core, moved[16:], moved[:16]).astype(BF16)


def rim_kernel(place, mask, rims, core_edge, chip_edge, _, sigma):
    kd = sigma.shape[1]
    width = mask.shape[1]
    step = pl.program_id(0)
    from_core = jnp.broadcast_to(place[1] ^ step, core_edge.shape) == 1
    edge = jnp.where(from_core, core_edge[...].astype(F32), chip_edge[...].astype(F32)).astype(BF16)
    at = iota((16, width), 0) + step * (width - 16)
    active = jnp.sum(
        jnp.where(at == iota((16, width), 1), mask[...], 0).astype(F32), axis=1, keepdims=True
    )
    rows, cols = iota((16, 16), 0), iota((16, 16), 1)
    to = cols % HALO + step * (16 - HALO)
    for comp in range(2):
        for k in range(kd):
            ck = comp * kd + k
            hit = (rows == to) & (cols // HALO == ck) & (active > 0.0)
            total = rims[ck, pl.ds(step * 16, 16)] + dot(hit.astype(F32).astype(BF16), edge)
            sigma[comp, k] = total.astype(BF16)


def add_rims(place, mask, rims, core_edge, chip_edge, sigma):
    _, kd, width, norb = sigma.shape
    last = width // 16 - 1
    return pl.pallas_call(
        rim_kernel,
        grid=(2,),
        out_shape=shape(*sigma.shape),
        in_specs=[SMEM] + [VMEM] * 4 + [pl.BlockSpec(memory_space=pl.ANY)],
        out_specs=pl.BlockSpec((2, kd, 16, norb), lambda i: (0, 0, i * last, 0)),
        input_output_aliases={5: 0},
        compiler_params=pltpu.CompilerParams(vmem_limit_bytes=LIMIT),
        cost_estimate=pl.CostEstimate(flops=2**20, bytes_accessed=2**20, transcendentals=0),
        name="rims",
    )(place, mask, rims, core_edge, chip_edge, sigma)


def owner_kernel(got, owner, pol):
    total = jnp.sum(got[...].astype(F32), axis=0)
    pol[...] = dot(owner[...], total, HIGHEST)


def tie(x, y):
    return lax.optimization_barrier((x, y))[0]


def on_device(green, mask, pair_order, q_index, offsets, occupancy, coupling):
    _, kd, width, norb = green.shape
    rounds = pair_order.shape[0]
    count = lax.axis_size(("zl", "c"))
    owned = coupling.shape[0] // lax.axis_size(("x", "y", "zh"))
    order, q_row, spread, mask_row = pair_order[:, 0].T, q_index.T, coupling.T, mask[None, :]
    place = [lax.axis_index(("x", "y", "zh")) * owned, lax.axis_index("c")]
    place = jnp.stack([jnp.asarray(x, jnp.int32) for x in place])

    swap = [(0, 1), (1, 0)]

    def exchange(x):
        near = lax.ppermute(x, "y", [(i, i ^ 1) for i in range(4)])
        next_near = lax.ppermute(x, "y", [(i, i ^ 2) for i in range(4)])
        return lax.ppermute(x, "zh", swap), near, next_near

    great = exchange(green[1])
    rim = green[0, :, :16] * mask[None, :16, None].astype(BF16)
    rim = lax.ppermute(rim, ("zl", "c"), [(i + 1, i) for i in range(count - 1)])
    main, edge, owner = call(
        functools.partial(weights_kernel, scale=1.0 / (width * count)),
        "weights",
        (
            shape(2 * kd, width, rounds * width),
            shape(2 * kd, 32, rounds * 32),
            shape(owned * offsets.shape[0], owned * HALO, dtype=F32),
        ),
        [SMEM] * 4 + [VMEM] * 2,
        (q_row, place, offsets, occupancy, spread, mask_row),
    )
    onehot, shifted, first = call(
        shift_kernel,
        "shift",
        (
            shape(coupling.shape[0] * HALO, rounds * kd * HALO),
            shape(kd * HALO, width, norb),
            shape(kd * HALO, norb, dtype=F32),
        ),
        [SMEM, SMEM, VMEM, VMEM],
        (order, q_row, mask_row, green),
    )
    tail, first = call(
        tail_kernel,
        "tail",
        (shape(kd * HALO, 16, norb), shape(*first.shape, dtype=F32)),
        [SMEM] + [VMEM] * 4,
        (order, green, shifted, rim, first),
    )
    dense = call(
        terms_kernel,
        "terms",
        shape(onehot.shape[0], norb),
        [SMEM] + [VMEM] * 7,
        (order, *great, tie(shifted, main), tail, first, onehot),
    )
    less = exchange(tie(green[0], dense))
    got = lax.all_to_all(dense.reshape(16, -1, norb), ("x", "y"), 0, 0, tiled=True)
    sent = call(
        column_kernel, "column", shape(2 * count, owned * HALO, norb), [VMEM], (got,)
    )
    got = lax.all_to_all(sent, ("zh", "zl", "c"), 0, 0, tiled=True)
    sigma, rims, core_edge, chip_edge = call(
        sigma_kernel,
        "sigma",
        (
            shape(*green.shape),
            shape(2 * kd, 32, norb, dtype=F32),
            shape(2 * kd * HALO, norb),
            shape(2 * kd * HALO, norb),
        ),
        [SMEM] * 2 + [VMEM] * 9 + [pl.BlockSpec(memory_space=pl.ANY)],
        (order, place, main, edge, green, *less, *great, sent),
        flops=2**34,
    )
    from_core = lax.ppermute(core_edge, "c", swap)
    meet = [(i, i + 1) for i in range(1, count - 1, 2)]
    from_chip = lax.ppermute(chip_edge, ("zl", "c"), meet + [(j, i) for i, j in meet])
    sigma = add_rims(place, mask_row, rims, from_core, from_chip, sigma)

    pol = call(
        owner_kernel,
        "owner",
        shape(owner.shape[0], norb, dtype=F32),
        [VMEM] * 2,
        (got, owner),
    )
    return sigma, pol.reshape(owned, -1, norb)


def solution(mesh):
    split = Mesh(mesh.devices.reshape(4, 4, 2, 4, 2), AXES)
    mom, en = ("x", "y", "zh"), ("zl", "c")
    in_specs = (P(None, mom, en, None), P(en), P(None, mom, None), P(None, mom), P(), P(), P())
    out_specs = (P(None, mom, en, None), P(mom, None, None))
    return jax.shard_map(
        on_device, mesh=split, in_specs=in_specs, out_specs=out_specs, check_vma=False
    )
```

time: 386 us -> 53.7 us (0.14)
  waiting for transfers between devices: 171 us -> 8.21 us
  other arithmetic: 59.2 us -> 0.15 us
  blocking collectives: 48.3 us -> 0 us
  between operations: 40.2 us -> 0.8 us
  local copies, waits for them, and re-layouts: 27.8 us -> 2.37 us
  Pallas kernels: 0 us -> 9.49 us
    reduce_scatter x1 -> x0, waiting for transfers between devices: 171 us -> none  [on_device(): lax.psum_scatter(pol_local.astype(jnp.bfloat16), 'mom', scatter_dimension...]
    psum x1 -> x0, blocking collectives: 48.3 us -> none  [on_device(): polarization = lax.psum(pol_owned, 'en').astype(jnp.float32)]
    another operation x7 -> x2, other arithmetic: 25 us -> 0.08 us  [the longest x1 0.08 us: on_device(): place = jnp.stack([jnp.asarray(x, jnp.int32) for x in place])]
    convert_element_type x11 -> x0, other arithmetic: 16.8 us -> none  [the longest x2 9.44 us: pair_terms(): lax.dynamic_slice_in_dim(part, rim - shift, width, 2).astype(jnp.float32)]
    ppermute x11 -> x9, starting transfers between devices: 33.9 us -> 21.4 us  [the longest x2 6.91 us: exchange(): return (lax.ppermute(x, 'zh', swap), near, next_near)]
    unnamed x174 -> x14, local copies, waits for them, and re-layouts: 13.4 us -> 1.34 us
    all_to_all x0 -> x2, starting transfers between devices: none -> 10.8 us  [the longest x1 5.44 us: on_device(): got = lax.all_to_all(sent, ('zh', 'zl', 'c'), 0, 0, tiled=True)]
    pallas_call x0 -> x8, Pallas kernels: none -> 9.49 us  [the longest x7 7.92 us: call(): pl.pallas_call(kernel, out_shape=outs, in_specs=specs, out_specs=jax.tree...]
  transfers between devices with their start and end apart: 12 -> 11, of which waited for: 1 -> 4; matrix products, arithmetic and copies ran while one was open for 16% -> 0% of each run, Pallas kernels for 0% -> 13%
where the time goes in v2:
time: 53.7 us; the launch traced here: 53.2 us
  starting transfers between devices  32.2 us (60%)
  Pallas kernels  9.49 us (18%)
  waiting for transfers between devices  8.21 us (15%)
  local copies, waits for them, and re-layouts  2.37 us (4%)
  between operations  0.8 us (1%)
    pallas_call x7, Pallas kernels, call(): pl.pallas_call(kernel, out_shape=outs, in_specs=specs, out_specs=jax.tree...  7.92 us
    ppermute x2, starting transfers between devices, exchange(): return (lax.ppermute(x, 'zh', swap), near, next_near)  6.91 us
    ppermute x2, starting transfers between devices, exchange(): next_near = lax.ppermute(x, 'y', [(i, i ^ 2) for i in range(4)])  6.7 us
    all_to_all x1, waiting for transfers between devices, on_device(): lax.all_to_all(dense.reshape(16, -1, norb), ('x', 'y'), 0, 0, tiled=True)  5.68 us
    all_to_all x1, starting transfers between devices, on_device(): got = lax.all_to_all(sent, ('zh', 'zl', 'c'), 0, 0, tiled=True)  5.44 us
    all_to_all x1, starting transfers between devices, on_device(): lax.all_to_all(dense.reshape(16, -1, norb), ('x', 'y'), 0, 0, tiled=True)  5.4 us
    ppermute x1, starting transfers between devices, on_device(): lax.ppermute(chip_edge, ('zl', 'c'), meet + [(j, i) for i, j in meet])  3.57 us
    ppermute x1, starting transfers between devices, on_device(): rim = lax.ppermute(rim, ('zl', 'c'), [(i + 1, i) for i in range(count - 1)])  3.41 us
  transfers between devices with their start and end apart: 11, of which 4 were waited for; matrix products, arithmetic and copies ran while one was open for 0% of the time, Pallas kernels for 13%

profile of v2, /device:TPU:1, one launch (start us, length us, event | category | flops | bytes accessed | tf_op | source)
XLA Modules:
  0.0 53.2 jit_solution(9431672315905378512)
XLA Ops:
  0.6 1.0 %slice_bitcast_fusion = (bf16[2,128,256]{2,1,0:T(8,128)(2,1)S(1)}, bf16[2,128,256]{2,1,0:T(8,128)(2,1)S(1)}) fusion(bf16[2,2,128,256]{3,2,1,0:T(8,128)(2,1)} %own.1), kind=kLoop, calls=%fused_computation | loop fusion | bytes 524288 | tf_op jit(solution)/shard_map/squeeze | solution.py:271
  1.7 3.8 %collective-permute-start.2 = (bf16[2,128,256]{2,1,0:T(8,128)(2,1)S(1)}, bf16[2,128,256]{2,1,0:T(8,128)(2,1)S(1)}, u32[]{:S(2)}, u32[]{:S(2)}) collective-permute-start(bf16[2,128,256]{2,1,0:T(8,128)(2,1)S(1)} %get-tuple-element.30), channel_id=1, source_target_pairs={{0,32},{16,48},{32,0},{48,16},{1,33},{17,49},{33,1},{49,17},{2,34}... | collective-permute-start | bytes 393224 | tf_op jit(solution)/shard_map/ppermute | solution.py:268
  5.5 0.4 collective-permute-start.1
  5.9 6.9 %collective-permute-start = (bf16[2,128,256]{2,1,0:T(8,128)(2,1)S(1)}, bf16[2,128,256]{2,1,0:T(8,128)(2,1)S(1)}, u32[]{:S(2)}, u32[]{:S(2)}) collective-permute-start(bf16[2,128,256]{2,1,0:T(8,128)(2,1)S(1)} %get-tuple-element.30), channel_id=1, source_target_pairs={{0,8},{8,0},{1,9},{9,1},{2,10},{10,2},{3,11},{11,3},{4,12},{12,4},... | collective-permute-start | bytes 393224 | tf_op jit(solution)/shard_map/ppermute | solution.py:269
  12.9 3.4 %collective-permute-start.3 = (bf16[2,16,256]{2,1,0:T(8,128)(2,1)S(1)}, bf16[2,16,256]{2,1,0:T(8,128)(2,1)S(1)}, u32[]{:S(2)}, u32[]{:S(2)}) collective-permute-start(bf16[2,16,256]{2,1,0:T(8,128)(2,1)S(1)} %bitcast_multiply_fusion), channel_id=1, source_target_pairs={{1,0},{2,1},{3,2},{4,3},{5,4},{6,5},{7,6},{9,8},{10,9},{11,10},{12... | collective-permute-start | bytes 49160 | tf_op jit(solution)/shard_map/ppermute | solution.py:273
  16.4 0.6 %copy-done.3 = s32[4,2]{0,1:T(2,128)S(1)} copy-done((s32[4,2]{0,1:T(2,128)S(1)}, s32[4,2]{0,1:T(2,128)}, u32[]{:S(2)}) %copy-start.3) | copy-done | bytes 56
  17.1 0.9 %shift.1 = (bf16[512,32]{1,0:T(8,128)(2,1)S(1)}, bf16[8,128,256]{2,1,0:T(8,128)(2,1)S(1)}, f32[8,256]{1,0:T(8,128)S(1)}) custom-call(s32[2,4]{1,0:T(2,128)S(1)} %bitcast.17, s32[2,4]{1,0:T(2,128)S(1)} %bitcast.24, s32[1,128]{1,0:T(1,128)S(1)} %bitcast.21, bf16[2,2,128,256]{3,2,1,0:T(8,128)(2,1)S(1)} %copy-done), custom_call_target="tpu_custom_call" | custom-call | flops 1048576 | bytes 1048576 | tf_op jit(solution)/shard_map/shift/pallas_call | solution.py:47
  18.1 0.6 %copy-done.5 = s32[8]{0:T(128)S(1)} copy-done((s32[8]{0:T(128)S(1)}, s32[8]{0:T(128)}, u32[]{:S(2)}) %copy-start.5) | copy-done | bytes 56
  18.7 1.6 %weights.1 = (bf16[4,128,512]{2,1,0:T(8,128)(2,1)S(1)}, bf16[4,32,128]{2,1,0:T(8,128)(2,1)S(1)}, f32[32,16]{1,0:T(8,128)S(1)}) custom-call(s32[2,4]{1,0:T(2,128)S(1)} %bitcast.25, s32[2]{0:T(128)S(1)} %pad_add_fusion.place, s32[8]{0:T(128)S(1)} %copy-done.5, f32[8]{0:T(128)S(1)} %copy-done.6, f32[8,128]{1,0:T(8,128)S(1)} %bitcast.26, s32[1,128]{1,0:T(1,128)S(1)} %bitcast.22), custom_call_target="tpu_custom_call" | custom-call | flops 1048576 | bytes 1048576 | tf_op jit(solution)/shard_map/weights/pallas_call | solution.py:47
  20.3 0.2 collective-permute-done.3.rim
  20.5 0.7 %tail.1 = (bf16[8,16,256]{2,1,0:T(8,128)(2,1)S(1)}, f32[8,256]{1,0:T(8,128)S(1)}) custom-call(s32[2,4]{1,0:T(2,128)S(1)} %bitcast.18, bf16[2,2,128,256]{3,2,1,0:T(8,128)(2,1)S(1)} %copy-done, bf16[8,128,256]{2,1,0:T(8,128)(2,1)S(1)} %get-tuple-element.19.shifted, bf16[2,16,256]{2,1,0:T(8,128)(2,1)S(1)} %collective-permute-done.3.rim, ...), custom_call_target="tpu_custom_call" | custom-call | flops 1048576 | bytes 1048576 | tf_op jit(solution)/shard_map/tail/pallas_call | solution.py:47
  21.3 1.7 %terms.1 = bf16[512,256]{1,0:T(8,128)(2,1)} custom-call(s32[2,4]{1,0:T(2,128)S(1)} %bitcast.19, bf16[2,128,256]{2,1,0:T(8,128)(2,1)S(1)} %collective-permute-done.far.great1, bf16[2,128,256]{2,1,0:T(8,128)(2,1)S(1)} %collective-permute-done.1.near.great2, bf16[2,128,256]{2,1,0:T(8,128)(2,1)S(1)} %collective-permute-done.2.next_near.great3, ...), custom_call_target="tpu_custom_call" | custom-call | flops 1048576 | bytes 1048576 | tf_op jit(solution)/shard_map/terms/pallas_call | solution.py:47
  22.9 5.4 %all-to-all-start = ((bf16[16,32,256]{2,1,0:T(8,128)(2,1)}), bf16[16,32,256]{2,1,0:T(8,128)(2,1)S(1)}, u32[]{:S(2)}, u32[]{:S(2)}) async-start(bf16[16,32,256]{2,1,0:T(8,128)(2,1)} %bitcast.11), calls=%async_computation | async-start | bytes 524288 | tf_op jit(solution)/shard_map/all_to_all | solution.py:311
  28.3 2.9 %collective-permute-start.6 = (bf16[2,128,256]{2,1,0:T(8,128)(2,1)S(1)}, bf16[2,128,256]{2,1,0:T(8,128)(2,1)S(1)}, u32[]{:S(2)}, u32[]{:S(2)}) collective-permute-start(bf16[2,128,256]{2,1,0:T(8,128)(2,1)S(1)} %get-tuple-element.24), channel_id=1, source_target_pairs={{0,32},{16,48},{32,0},{48,16},{1,33},{17,49},{33,1},{49,17},{2,34}... | collective-permute-start | bytes 393224 | tf_op jit(solution)/shard_map/ppermute | solution.py:268
  31.2 0.3 collective-permute-start.5
  31.5 5.7 %all-to-all-done.got = bf16[16,32,256]{2,1,0:T(8,128)(2,1)S(1)} async-done(((bf16[16,32,256]{2,1,0:T(8,128)(2,1)}), bf16[16,32,256]{2,1,0:T(8,128)(2,1)S(1)}, u32[]{:S(2)}, u32[]{:S(2)}) %all-to-all-start) | async-done | bytes 262176 | tf_op jit(solution)/shard_map/all_to_all | solution.py:311
  37.2 0.7 %column.1._after = bf16[16,16,256]{2,1,0:T(8,128)(2,1)} custom-call(bf16[16,32,256]{2,1,0:T(8,128)(2,1)S(1)} %all-to-all-done.got), custom_call_target="tpu_custom_call" | custom-call | flops 1048576 | bytes 1048576 | tf_op jit(solution)/shard_map/column/pallas_call | solution.py:47
  37.8 5.4 %all-to-all-start.1 = ((bf16[16,16,256]{2,1,0:T(8,128)(2,1)}), bf16[16,16,256]{2,1,0:T(8,128)(2,1)S(1)}, u32[]{:S(2)}, u32[]{:S(2)}) async-start(bf16[16,16,256]{2,1,0:T(8,128)(2,1)} %column.1._after), calls=%async_computation.1 | async-start | bytes 262144 | tf_op jit(solution)/shard_map/all_to_all | solution.py:315
  43.3 1.6 %sigma.1 = (bf16[2,2,128,256]{3,2,1,0:T(8,128)(2,1)}, f32[4,32,256]{2,1,0:T(8,128)S(1)}, bf16[16,256]{1,0:T(8,128)(2,1)S(1)}, bf16[16,256]{1,0:T(8,128)(2,1)S(1)}) custom-call(s32[2,4]{1,0:T(2,128)S(1)} %bitcast.20, s32[2]{0:T(128)S(1)} %pad_add_fusion.place, bf16[4,128,512]{2,1,0:T(8,128)(2,1)S(1)} %get-tuple-element.16.main, ...), custom_call_target="tpu_custom_call" | custom-call | flops 17179869184 | bytes 1048576 | tf_op jit(solution)/shard_map/sigma/pallas_call | solution.py:47
  45.0 3.6 %collective-permute-start.8 = (bf16[16,256]{1,0:T(8,128)(2,1)S(1)}, bf16[16,256]{1,0:T(8,128)(2,1)S(1)}, u32[]{:S(2)}, u32[]{:S(2)}) collective-permute-start(bf16[16,256]{1,0:T(8,128)(2,1)S(1)} %get-tuple-element.27), channel_id=1, source_target_pairs={{1,2},{3,4},{5,6},{2,1},{4,3},{6,5},{9,10},{11,12},{13,14},{10,9},... | collective-permute-start | bytes 24584 | tf_op jit(solution)/shard_map/ppermute | solution.py:331
  48.6 1.7 %collective-permute-done.8.chip_edge = bf16[16,256]{1,0:T(8,128)(2,1)S(1)} collective-permute-done((bf16[16,256]{1,0:T(8,128)(2,1)S(1)}, bf16[16,256]{1,0:T(8,128)(2,1)S(1)}, u32[]{:S(2)}, u32[]{:S(2)}) %collective-permute-start.8) | collective-permute-done | bytes 8224 | tf_op jit(solution)/shard_map/ppermute | solution.py:331
  50.3 1.6 %rims.1 = bf16[2,2,128,256]{3,2,1,0:T(8,128)(2,1)} custom-call(s32[2]{0:T(128)S(1)} %pad_add_fusion.place, s32[1,128]{1,0:T(1,128)S(1)} %bitcast.23, f32[4,32,256]{2,1,0:T(8,128)S(1)} %get-tuple-element.25.rims, bf16[16,256]{1,0:T(8,128)(2,1)S(1)} %collective-permute-done.7.core_edge, ...), custom_call_target="tpu_custom_call", output_to_operand_aliasing={{}: (5, {})} | custom-call | flops 1048576 | bytes 1048576 | tf_op jit(solution)/shard_map/rims/pallas_call | solution.py:233
  51.9 0.6 %all-to-all-done.1.got = bf16[16,16,256]{2,1,0:T(8,128)(2,1)S(1)} async-done(((bf16[16,16,256]{2,1,0:T(8,128)(2,1)}), bf16[16,16,256]{2,1,0:T(8,128)(2,1)S(1)}, u32[]{:S(2)}, u32[]{:S(2)}) %all-to-all-start.1) | async-done | bytes 131104 | tf_op jit(solution)/shard_map/all_to_all | solution.py:315
  52.5 0.8 %owner.1 = f32[32,256]{1,0:T(8,128)} custom-call(bf16[16,16,256]{2,1,0:T(8,128)(2,1)S(1)} %all-to-all-done.1.got, f32[32,16]{1,0:T(8,128)S(1)} %get-tuple-element.29.owner), custom_call_target="tpu_custom_call" | custom-call | flops 1048576 | bytes 1048576 | tf_op jit(solution)/shard_map/owner/pallas_call | solution.py:47
  (24 shorter events, 0.4 us)
Async XLA Ops:
  0.6 12.2 %copy-start = (bf16[2,2,128,256]{3,2,1,0:T(8,128)(2,1)S(1)}, bf16[2,2,128,256]{3,2,1,0:T(8,128)(2,1)}, u32[]{:S(2)}) copy-start(bf16[2,2,128,256]{3,2,1,0:T(8,128)(2,1)} %own.1) | copy-start | bytes 786436
  1.7 11.2 %copy-start.2 = (s32[128]{0:T(128)S(1)}, s32[128]{0:T(128)}, u32[]{:S(2)}) copy-start(s32[128]{0:T(128)} %param.8) | copy-start | bytes 1540
  1.7 19.5 %collective-permute-start.2 = (bf16[2,128,256]{2,1,0:T(8,128)(2,1)S(1)}, bf16[2,128,256]{2,1,0:T(8,128)(2,1)S(1)}, u32[]{:S(2)}, u32[]{:S(2)}) collective-permute-start(bf16[2,128,256]{2,1,0:T(8,128)(2,1)S(1)} %get-tuple-element.30), channel_id=1, source_target_pairs={{0,32},{16,48},{32,0},{48,16},{1,33},{17,49},{33,1},{49,17},{2,34}... | collective-permute-start | bytes 393224 | tf_op jit(solution)/shard_map/ppermute | solution.py:268
  5.5 15.7 %collective-permute-start.1 = (bf16[2,128,256]{2,1,0:T(8,128)(2,1)S(1)}, bf16[2,128,256]{2,1,0:T(8,128)(2,1)S(1)}, u32[]{:S(2)}, u32[]{:S(2)}) collective-permute-start(bf16[2,128,256]{2,1,0:T(8,128)(2,1)S(1)} %get-tuple-element.30), channel_id=1, source_target_pairs={{0,16},{16,0},{32,48},{48,32},{1,17},{17,1},{33,49},{49,33},{2,18}... | collective-permute-start | bytes 393224 | tf_op jit(solution)/shard_map/ppermute | solution.py:267
  5.9 15.3 %collective-permute-start = (bf16[2,128,256]{2,1,0:T(8,128)(2,1)S(1)}, bf16[2,128,256]{2,1,0:T(8,128)(2,1)S(1)}, u32[]{:S(2)}, u32[]{:S(2)}) collective-permute-start(bf16[2,128,256]{2,1,0:T(8,128)(2,1)S(1)} %get-tuple-element.30), channel_id=1, source_target_pairs={{0,8},{8,0},{1,9},{9,1},{2,10},{10,2},{3,11},{11,3},{4,12},{12,4},... | collective-permute-start | bytes 393224 | tf_op jit(solution)/shard_map/ppermute | solution.py:269
  12.9 7.6 %collective-permute-start.3 = (bf16[2,16,256]{2,1,0:T(8,128)(2,1)S(1)}, bf16[2,16,256]{2,1,0:T(8,128)(2,1)S(1)}, u32[]{:S(2)}, u32[]{:S(2)}) collective-permute-start(bf16[2,16,256]{2,1,0:T(8,128)(2,1)S(1)} %bitcast_multiply_fusion), channel_id=1, source_target_pairs={{1,0},{2,1},{3,2},{4,3},{5,4},{6,5},{7,6},{9,8},{10,9},{11,10},{12... | collective-permute-start | bytes 49160 | tf_op jit(solution)/shard_map/ppermute | solution.py:273
  16.3 0.7 %copy-start.3 = (s32[4,2]{0,1:T(2,128)S(1)}, s32[4,2]{0,1:T(2,128)}, u32[]{:S(2)}) copy-start(s32[4,2]{0,1:T(2,128)} %param.10) | copy-start | bytes 100
  16.4 0.7 %copy-start.1 = (s32[4,1,2]{0,2,1:T(2,128)S(1)}, s32[4,1,2]{0,2,1:T(2,128)}, u32[]{:S(2)}) copy-start(s32[4,1,2]{0,2,1:T(2,128)} %param.9) | copy-start | bytes 100
  17.1 0.9 %copy-start.4 = (f32[128,8]{0,1:T(8,128)S(1)}, f32[128,8]{0,1:T(8,128)}, u32[]{:S(2)}) copy-start(f32[128,8]{0,1:T(8,128)} %param.13) | copy-start | bytes 12292
  18.0 0.7 %copy-start.5 = (s32[8]{0:T(128)S(1)}, s32[8]{0:T(128)}, u32[]{:S(2)}) copy-start(s32[8]{0:T(128)} %offsets.1) | copy-start | bytes 100
  18.0 0.7 %copy-start.6 = (f32[8]{0:T(128)S(1)}, f32[8]{0:T(128)}, u32[]{:S(2)}) copy-start(f32[8]{0:T(128)} %occupancy.1) | copy-start | bytes 100
  22.9 14.2 %all-to-all-start = ((bf16[16,32,256]{2,1,0:T(8,128)(2,1)}), bf16[16,32,256]{2,1,0:T(8,128)(2,1)S(1)}, u32[]{:S(2)}, u32[]{:S(2)}) async-start(bf16[16,32,256]{2,1,0:T(8,128)(2,1)} %bitcast.11), calls=%async_computation | async-start | bytes 524288 | tf_op jit(solution)/shard_map/all_to_all | solution.py:311
  28.3 15.0 %collective-permute-start.6 = (bf16[2,128,256]{2,1,0:T(8,128)(2,1)S(1)}, bf16[2,128,256]{2,1,0:T(8,128)(2,1)S(1)}, u32[]{:S(2)}, u32[]{:S(2)}) collective-permute-start(bf16[2,128,256]{2,1,0:T(8,128)(2,1)S(1)} %get-tuple-element.24), channel_id=1, source_target_pairs={{0,32},{16,48},{32,0},{48,16},{1,33},{17,49},{33,1},{49,17},{2,34}... | collective-permute-start | bytes 393224 | tf_op jit(solution)/shard_map/ppermute | solution.py:268
  31.2 12.1 %collective-permute-start.5 = (bf16[2,128,256]{2,1,0:T(8,128)(2,1)S(1)}, bf16[2,128,256]{2,1,0:T(8,128)(2,1)S(1)}, u32[]{:S(2)}, u32[]{:S(2)}) collective-permute-start(bf16[2,128,256]{2,1,0:T(8,128)(2,1)S(1)} %get-tuple-element.24), channel_id=1, source_target_pairs={{0,16},{16,0},{32,48},{48,32},{1,17},{17,1},{33,49},{49,33},{2,18}... | collective-permute-start | bytes 393224 | tf_op jit(solution)/shard_map/ppermute | solution.py:267
  31.5 11.8 %collective-permute-start.4 = (bf16[2,128,256]{2,1,0:T(8,128)(2,1)S(1)}, bf16[2,128,256]{2,1,0:T(8,128)(2,1)S(1)}, u32[]{:S(2)}, u32[]{:S(2)}) collective-permute-start(bf16[2,128,256]{2,1,0:T(8,128)(2,1)S(1)} %get-tuple-element.24), channel_id=1, source_target_pairs={{0,8},{8,0},{1,9},{9,1},{2,10},{10,2},{3,11},{11,3},{4,12},{12,4},... | collective-permute-start | bytes 393224 | tf_op jit(solution)/shard_map/ppermute | solution.py:269
  37.8 14.6 %all-to-all-start.1 = ((bf16[16,16,256]{2,1,0:T(8,128)(2,1)}), bf16[16,16,256]{2,1,0:T(8,128)(2,1)S(1)}, u32[]{:S(2)}, u32[]{:S(2)}) async-start(bf16[16,16,256]{2,1,0:T(8,128)(2,1)} %column.1._after), calls=%async_computation.1 | async-start | bytes 262144 | tf_op jit(solution)/shard_map/all_to_all | solution.py:315
  44.9 3.7 %collective-permute-start.7 = (bf16[16,256]{1,0:T(8,128)(2,1)S(1)}, bf16[16,256]{1,0:T(8,128)(2,1)S(1)}, u32[]{:S(2)}, u32[]{:S(2)}) collective-permute-start(bf16[16,256]{1,0:T(8,128)(2,1)S(1)} %get-tuple-element.26), channel_id=1, source_target_pairs={{0,1},{1,0},{2,3},{3,2},{4,5},{5,4},{6,7},{7,6},{8,9},{9,8},{10,11... | collective-permute-start | bytes 24584 | tf_op jit(solution)/shard_map/ppermute | solution.py:329
  45.0 5.3 %collective-permute-start.8 = (bf16[16,256]{1,0:T(8,128)(2,1)S(1)}, bf16[16,256]{1,0:T(8,128)(2,1)S(1)}, u32[]{:S(2)}, u32[]{:S(2)}) collective-permute-start(bf16[16,256]{1,0:T(8,128)(2,1)S(1)} %get-tuple-element.27), channel_id=1, source_target_pairs={{1,2},{3,4},{5,6},{2,1},{4,3},{6,5},{9,10},{11,12},{13,14},{10,9},... | collective-permute-start | bytes 24584 | tf_op jit(solution)/shard_map/ppermute | solution.py:331

commit v3 on v2

v3 whole, which is shorter than its diff:
```python
import functools

import jax
import jax.numpy as jnp
from jax import lax
from jax.experimental import pallas as pl
from jax.experimental.pallas import tpu as pltpu
from jax.sharding import Mesh, PartitionSpec as P

HALO = 4
AXES = ("x", "y", "zh", "zl", "c")
F32 = jnp.float32
BF16 = jnp.bfloat16
HIGHEST = lax.Precision.HIGHEST
SMEM = pl.BlockSpec(memory_space=pltpu.SMEM)
LIMIT = 12 * 1024 * 1024
VMEM = pl.BlockSpec(memory_space=pltpu.VMEM)


def iota(shape, dim):
    return lax.broadcasted_iota(jnp.int32, shape, dim)


def dot(a, b, precision=None):
    return lax.dot_general(
        a, b, (((1,), (0,)), ((), ())), precision=precision, preferred_element_type=F32
    )


def band(dif, above, below):
    out = jnp.zeros(dif.shape, F32)
    for d in range(1, HALO + 1):
        out = jnp.where(dif == d, above[d - 1], out)
        out = jnp.where(dif == -d, below[d - 1], out)
    return out


def pair_products(great, shifted, k):
    great = great.astype(F32)
    return [
        jnp.sum(great * shifted[k * HALO + d].astype(F32), axis=0, keepdims=True)
        for d in range(HALO)
    ]


def call(kernel, name, outs, specs, args, scratch=(), flops=2**20):
    return pl.pallas_call(
        kernel,
        out_shape=outs,
        in_specs=specs,
        out_specs=jax.tree.map(lambda _: VMEM, outs),
        scratch_shapes=scratch,
        compiler_params=pltpu.CompilerParams(vmem_limit_bytes=LIMIT),
        cost_estimate=pl.CostEstimate(flops=flops, bytes_accessed=2**20, transcendentals=0),
        name=name,
    )(*args)


def shape(*dims, dtype=BF16):
    return jax.ShapeDtypeStruct(dims, dtype)


def shift_kernel(q_row, mask, green, *rest):
    onehot, shifted = rest[-2:]
    kd, rounds = q_row.shape
    width = mask.shape[1]
    goal = jnp.zeros((1, onehot.shape[1]), jnp.int32)
    lane = iota(goal.shape, 1)
    for p in range(rounds * kd):
        goal = jnp.where(lane // HALO == p, q_row[p % kd, p // kd] * HALO + lane % HALO, goal)
    onehot[...] = (iota(onehot.shape, 0) == goal).astype(F32).astype(BF16)

    row, col = iota((width, width), 0), iota((width, width), 1)
    weights = jnp.broadcast_to(mask[...], (width, width)).astype(F32)
    for d in range(1, HALO + 1):
        move = jnp.where(col == row + d, weights, 0.0).astype(BF16)
        for k in range(kd):
            shifted[k * HALO + d - 1] = dot(move, green[0, k]).astype(BF16)


def halo_kernel(order, place, green, shifted, from_core, from_chip, full, first, extended):
    kd, width = green.shape[1:3]
    first_core = jnp.broadcast_to(place[1], from_core.shape) == 0
    core, chip = from_core[...].astype(F32), from_chip[...].astype(F32)
    before = jnp.where(first_core, chip, core).astype(BF16)
    after = jnp.where(first_core, core, chip).astype(BF16)
    rows, cols = iota((16, 16), 0), iota((16, 16), 1)
    row, col = iota((16, 64), 0), iota((16, 64), 1)
    kind = row // HALO
    pick = (col == kind * 16 + (1 - kind % 2) * (16 - HALO) + row % HALO).astype(F32).astype(BF16)
    for k in range(kd):
        for d in range(1, HALO + 1):
            at = k * HALO + d - 1
            wrap = (cols + 16 == rows + d).astype(F32).astype(BF16)
            moved = dot(wrap, after[2 * kd + k])
            full[at, : width - 16] = shifted[at, : width - 16]
            full[at, width - 16 :] = (shifted[at, width - 16 :].astype(F32) + moved).astype(BF16)
        ends = [before[k], after[k], before[kd + k], after[kd + k]]
        extended[k, :width] = green[0, k]
        extended[k, width:] = dot(pick, jnp.concatenate(ends, axis=0)).astype(BF16)
    lines = []
    for k in range(kd):
        lines += pair_products(green[1, order[k, 0]], full, k)
    first[...] = jnp.concatenate(lines, axis=0)


def terms_kernel(order, far, near, next_near, shifted, first, onehot, out):
    lines = [first[...]]
    for r, ref in ((1, far), (2, near), (3, next_near)):
        for k in range(far.shape[0]):
            lines += pair_products(ref[order[k, r]], shifted, k)
    terms = jnp.concatenate(lines, axis=0).astype(BF16)
    out[...] = dot(onehot[...], terms).astype(BF16)


def column_kernel(got, out):
    total = jnp.sum(got[...].astype(F32), axis=0).astype(BF16)
    half = out.shape[1]
    for dest in range(out.shape[0]):
        at = (dest // (out.shape[0] // 2)) * half
        out[dest] = total[at : at + half]


def weights_kernel(q_row, place, offsets, occupancy, coupling, mask, main, owner, *, scale):
    kd, rounds = q_row.shape
    width = mask.shape[1]
    modes = coupling.shape[0]
    pairs = rounds * kd

    q_col = jnp.zeros((pairs, coupling.shape[1]), jnp.int32)
    for p in range(pairs):
        q_col = jnp.where(iota(q_col.shape, 0) == p, q_row[p % kd, p // kd], q_col)
    chosen = (q_col == iota(q_col.shape, 1)).astype(F32)
    strength = lax.dot_general(
        chosen, coupling[...], (((1,), (1,)), ((), ())), precision=HIGHEST, preferred_element_type=F32
    )
    off_col = jnp.zeros((modes, width), jnp.int32)
    occ_col = jnp.zeros((modes, width), F32)
    for m in range(modes):
        off_col = jnp.where(iota(off_col.shape, 0) == m, offsets[m], off_col)
        occ_col = jnp.where(iota(off_col.shape, 0) == m, occupancy[m], occ_col)
    emit, absorb = [], []
    for d in range(1, HALO + 1):
        emit.append(dot(strength, jnp.where(off_col == d, occ_col + 1.0, 0.0), HIGHEST))
        absorb.append(dot(strength, jnp.where(off_col == d, occ_col, 0.0), HIGHEST))

    rows, cols = iota(owner.shape, 0), iota(owner.shape, 1)
    wide = (owner.shape[0], coupling.shape[1])
    mine = (iota(wide, 1) == place[0] + iota(wide, 0) // modes).astype(F32)
    factor = lax.dot_general(
        mine, coupling[...], (((1,), (1,)), ((), ())), precision=HIGHEST, preferred_element_type=F32
    )
    branch = iota(factor.shape, 1) == iota(factor.shape, 0) % modes
    factor = jnp.sum(jnp.where(branch, factor, 0.0), axis=1, keepdims=True) * scale
    off = jnp.zeros(owner.shape, jnp.int32)
    for m in range(modes):
        off = jnp.where(rows % modes == m, offsets[m], off)
    hit = (rows // modes == cols // HALO) & (off == cols % HALO + 1)
    owner[...] = jnp.where(hit, factor, 0.0)

    row, col = iota((width, width), 0), iota((width, width), 1)
    active = jnp.sum(jnp.where(row == col, mask[...], 0).astype(F32), axis=1, keepdims=True)
    live = jnp.where(active > 0.0, col - row, 2 * width)
    beyond = iota((width, 16), 1)
    source = jnp.where(beyond % 8 < HALO, beyond % 8 - HALO, width + beyond % 8 - HALO)
    gap = jnp.where(active > 0.0, source - iota((width, 16), 0), 2 * width)
    for comp in range(2):
        dif = jnp.where(beyond // 8 == comp, gap, 2 * width)
        for k in range(kd):
            ck = comp * kd + k
            ends = []
            for r in range(rounds):
                p = r * kd + k
                up = [x[p : p + 1, :] for x in emit]
                down = [x[p : p + 1, :] for x in absorb]
                if comp == 1:
                    up, down = down, up
                main[ck, :, r * width : (r + 1) * width] = band(live, up, down).astype(BF16)
                ends.append(band(dif, [x[:, :16] for x in up], [x[:, :16] for x in down]))
            main[ck, :, rounds * width :] = jnp.concatenate(ends, axis=1).astype(BF16)


def sigma_kernel(order, main, green, own, less1, less2, less3, great1, great2, great3, sigma):
    kd, rounds = order.shape
    width = green.shape[2]
    less = (own, less1, less2, less3)
    for k in range(kd):
        index = [order[k, r] for r in range(rounds)]
        ends = jnp.concatenate([x[i, width:] for x, i in zip(less, index)], axis=0)
        for comp in range(2):
            if comp == 0:
                blocks = [x[i, :width] for x, i in zip(less, index)]
            else:
                blocks = [green[1, index[0]]]
                blocks += [x[i] for x, i in zip((great1, great2, great3), index[1:])]
            weights = main[comp * kd + k]
            acc = dot(weights[:, : rounds * width], jnp.concatenate(blocks, axis=0))
            sigma[comp, k] = (acc + dot(weights[:, rounds * width :], ends)).astype(BF16)


def owner_kernel(got, owner, pol):
    total = jnp.sum(got[...].astype(F32), axis=0)
    pol[...] = dot(owner[...], total, HIGHEST)


def tie(x, y):
    return lax.optimization_barrier((x, y))[0]


def on_device(green, mask, pair_order, q_index, offsets, occupancy, coupling):
    _, kd, width, norb = green.shape
    rounds = pair_order.shape[0]
    count = lax.axis_size(("zl", "c"))
    owned = coupling.shape[0] // lax.axis_size(("x", "y", "zh"))
    order, q_row, spread, mask_row = pair_order[:, 0].T, q_index.T, coupling.T, mask[None, :]
    place = [lax.axis_index(("x", "y", "zh")) * owned, lax.axis_index("c")]
    place = jnp.stack([jnp.asarray(x, jnp.int32) for x in place])

    swap = [(0, 1), (1, 0)]

    def exchange(x):
        near = lax.ppermute(x, "y", [(i, i ^ 1) for i in range(4)])
        return near, lax.ppermute(x, "y", [(i, i ^ 2) for i in range(4)])

    more = green.reshape(-1, norb)[kd * width - 16 :]
    far = lax.ppermute(more, "zh", swap)[16:].reshape(kd, width, norb)
    first, last = green[:, :, :16], green[:, :, width - 16 :]
    masked = first[0] * mask[None, :16, None].astype(BF16)
    first_core = lax.axis_index("c") == 0

    def edge(x):
        return jnp.concatenate([x.reshape(2 * kd, 16, norb), masked], axis=0)

    from_core = lax.ppermute(edge(jnp.where(first_core, last, first)), "c", swap)
    meet = [(i, i + 1) for i in range(1, count - 1, 2)]
    to_chip = edge(jnp.where(first_core, first, last))
    from_chip = lax.ppermute(to_chip, ("zl", "c"), meet + [(j, i) for i, j in meet])
    great = (far, *exchange(tie(green[1], to_chip)))
    onehot, shifted = call(
        shift_kernel,
        "shift",
        (
            shape(coupling.shape[0] * HALO, rounds * kd * HALO),
            shape(kd * HALO, width, norb),
        ),
        [SMEM] + [VMEM] * 6,
        (q_row, mask_row, green, order, offsets[None], occupancy[None], spread),
    )
    shifted, first, extended = call(
        halo_kernel,
        "halo",
        (
            shape(*shifted.shape),
            shape(kd * HALO, norb, dtype=F32),
            shape(kd, width + 16, norb),
        ),
        [SMEM] * 2 + [VMEM] * 4,
        (order, place, green, shifted, from_core, from_chip),
    )
    dense = call(
        terms_kernel,
        "terms",
        shape(onehot.shape[0], norb),
        [SMEM] + [VMEM] * 6,
        (order, *great, shifted, first, onehot),
    )
    less = (lax.ppermute(extended, "zh", swap), *exchange(tie(extended, dense)))
    got = lax.all_to_all(dense.reshape(16, -1, norb), ("x", "y"), 0, 0, tiled=True)
    sent = call(
        column_kernel, "column", shape(2 * count, owned * HALO, norb), [VMEM], (got,)
    )
    got = lax.all_to_all(sent, ("zh", "zl", "c"), 0, 0, tiled=True)

    main, owner = call(
        functools.partial(weights_kernel, scale=1.0 / (width * count)),
        "weights",
        (
            shape(2 * kd, width, rounds * (width + 16)),
            shape(owned * offsets.shape[0], owned * HALO, dtype=F32),
        ),
        [SMEM] * 4 + [VMEM] * 2,
        (q_row, place, offsets, occupancy, tie(spread, sent), mask_row),
    )
    sigma = call(
        sigma_kernel,
        "sigma",
        shape(*green.shape),
        [SMEM] + [VMEM] * 9,
        (order, main, green, extended, *less, *great),
        flops=2**34,
    )
    pol = call(
        owner_kernel,
        "owner",
        shape(owner.shape[0], norb, dtype=F32),
        [VMEM] * 2,
        (got, owner),
    )
    return sigma, pol.reshape(owned, -1, norb)


def solution(mesh):
    split = Mesh(mesh.devices.reshape(4, 4, 2, 4, 2), AXES)
    mom, en = ("x", "y", "zh"), ("zl", "c")
    in_specs = (P(None, mom, en, None), P(en), P(None, mom, None), P(None, mom), P(), P(), P())
    out_specs = (P(None, mom, en, None), P(mom, None, None))
    return jax.shard_map(
        on_device, mesh=split, in_specs=in_specs, out_specs=out_specs, check_vma=False
    )
```

time: 53.7 us -> 51.8 us (0.965)
  starting transfers between devices: 32.2 us -> 29.5 us
  waiting for transfers between devices: 8.21 us -> 10.2 us
  Pallas kernels: 9.49 us -> 8.32 us
    all_to_all x1, waiting for transfers between devices: 0.6 us -> 5.46 us  [on_device(): got = lax.all_to_all(sent, ('zh', 'zl', 'c'), 0, 0, tiled=True)]
    ppermute x7 -> x6, starting transfers between devices: 20.7 us -> 17.9 us  [the longest x1 7.83 us: on_device(): far = lax.ppermute(more, 'zh', swap)[16:].reshape(kd, width, norb)]
    ppermute x7 -> x6, waiting for transfers between devices: 1.92 us -> 0.26 us  [the longest x1 0.25 us: on_device(): lax.ppermute(to_chip, ('zl', 'c'), meet + [(j, i) for i, j in meet])]
    pallas_call x1 -> x0, Pallas kernels: 1.57 us -> none  [add_rims(): pl.pallas_call(rim_kernel, grid=(2,), out_shape=shape(*sigma.shape), in_s...]
    all_to_all x1, waiting for transfers between devices: 5.68 us -> 4.45 us  [on_device(): lax.all_to_all(dense.reshape(16, -1, norb), ('x', 'y'), 0, 0, tiled=True)]
    squeeze x1, local copies, waits for them, and re-layouts: 1.03 us -> 0.01 us  [on_device(): great = (far, *exchange(tie(green[1], to_chip)))]
    slice x0 -> x2, local copies, waits for them, and re-layouts: none -> 0.99 us  [the longest x1 0.98 us: on_device(): more = green.reshape(-1, norb)[kd * width - 16:]]
  transfers between devices with their start and end apart: 11 -> 10, of which waited for: 4 -> 3; matrix products, arithmetic and copies ran while one was open for 0% -> 0% of each run, Pallas kernels for 13% -> 12%
where the time goes in v3:
time: 51.8 us; the launch traced here: 51.4 us
  starting transfers between devices  29.5 us (57%)
  waiting for transfers between devices  10.2 us (20%)
  Pallas kernels  8.32 us (16%)
  local copies, waits for them, and re-layouts  2.37 us (5%)
  between operations  0.81 us (2%)
    pallas_call x7, Pallas kernels, call(): pl.pallas_call(kernel, out_shape=outs, in_specs=specs, out_specs=jax.tree...  8.32 us
    ppermute x1, starting transfers between devices, on_device(): far = lax.ppermute(more, 'zh', swap)[16:].reshape(kd, width, norb)  7.83 us
    ppermute x2, starting transfers between devices, exchange(): return (near, lax.ppermute(x, 'y', [(i, i ^ 2) for i in range(4)]))  5.87 us
    all_to_all x1, starting transfers between devices, on_device(): got = lax.all_to_all(sent, ('zh', 'zl', 'c'), 0, 0, tiled=True)  5.52 us
    all_to_all x1, waiting for transfers between devices, on_device(): got = lax.all_to_all(sent, ('zh', 'zl', 'c'), 0, 0, tiled=True)  5.46 us
    all_to_all x1, starting transfers between devices, on_device(): lax.all_to_all(dense.reshape(16, -1, norb), ('x', 'y'), 0, 0, tiled=True)  5.4 us
    all_to_all x1, waiting for transfers between devices, on_device(): lax.all_to_all(dense.reshape(16, -1, norb), ('x', 'y'), 0, 0, tiled=True)  4.45 us
    ppermute x1, starting transfers between devices, on_device(): lax.ppermute(to_chip, ('zl', 'c'), meet + [(j, i) for i, j in meet])  4.04 us
  transfers between devices with their start and end apart: 10, of which 3 were waited for; matrix products, arithmetic and copies ran while one was open for 0% of the time, Pallas kernels for 12%

profile of v3, /device:TPU:1, one launch (start us, length us, event | category | flops | bytes accessed | tf_op | source)
XLA Modules:
  0.0 51.4 jit_solution(4152440383688981653)
XLA Ops:
  0.6 1.0 %slice.30 = bf16[272,256]{1,0:T(8,128)(2,1)S(1)} slice(bf16[512,256]{1,0:T(8,128)(2,1)} %bitcast.21), slice={[240:512], [0:256]} | slice | bytes 278528 | tf_op jit(solution)/shard_map/slice | solution.py:225
  1.6 7.8 %collective-permute-start = (bf16[272,256]{1,0:T(8,128)(2,1)S(1)}, bf16[272,256]{1,0:T(8,128)(2,1)S(1)}, u32[]{:S(2)}, u32[]{:S(2)}) collective-permute-start(bf16[272,256]{1,0:T(8,128)(2,1)S(1)} %slice.30), channel_id=1, source_target_pairs={{0,8},{8,0},{1,9},{9,1},{2,10},{10,2},{3,11},{11,3},{4,12},{12,4},... | collective-permute-start | bytes 417800 | tf_op jit(solution)/shard_map/ppermute | solution.py:226
  9.5 0.6 %copy-done.6 = s32[128]{0:T(128)S(1)} copy-done((s32[128]{0:T(128)S(1)}, s32[128]{0:T(128)}, u32[]{:S(2)}) %copy-start.6) | copy-done | bytes 536
  10.1 0.1 bitcast_multiply_fusion
  10.2 3.0 %collective-permute-start.2 = (bf16[2,128,256]{2,1,0:T(8,128)(2,1)S(1)}, bf16[2,128,256]{2,1,0:T(8,128)(2,1)S(1)}, u32[]{:S(2)}, u32[]{:S(2)}) collective-permute-start(bf16[2,128,256]{2,1,0:T(8,128)(2,1)S(1)} %slice_bitcast_fusion), channel_id=1, source_target_pairs={{0,32},{16,48},{32,0},{48,16},{1,33},{17,49},{33,1},{49,17},{2,34}... | collective-permute-start | bytes 393224 | tf_op jit(solution)/shard_map/ppermute | solution.py:223
  13.2 0.4 collective-permute-start.1
  13.6 4.0 %collective-permute-start.4 = (bf16[6,16,256]{2,1,0:T(8,128)(2,1)S(1)}, bf16[6,16,256]{2,1,0:T(8,128)(2,1)S(1)}, u32[]{:S(2)}, u32[]{:S(2)}) collective-permute-start(bf16[6,16,256]{2,1,0:T(8,128)(2,1)S(1)} %get-tuple-element.25), channel_id=1, source_target_pairs={{1,2},{3,4},{5,6},{2,1},{4,3},{6,5},{9,10},{11,12},{13,14},{10,9},... | collective-permute-start | bytes 147464 | tf_op jit(solution)/shard_map/ppermute | solution.py:237
  17.7 0.1 collective-permute-start.3
  17.9 0.7 %copy-done.3 = s32[4,2]{0,1:T(2,128)S(1)} copy-done((s32[4,2]{0,1:T(2,128)S(1)}, s32[4,2]{0,1:T(2,128)}, u32[]{:S(2)}) %copy-start.3) | copy-done | bytes 56
  18.6 0.9 %shift.1 = (bf16[512,32]{1,0:T(8,128)(2,1)S(1)}, bf16[8,128,256]{2,1,0:T(8,128)(2,1)S(1)}) custom-call(s32[2,4]{1,0:T(2,128)S(1)} %bitcast.30, s32[1,128]{1,0:T(1,128)S(1)} %bitcast.34, bf16[2,2,128,256]{3,2,1,0:T(8,128)(2,1)S(1)} %copy-done, s32[2,4]{1,0:T(2,128)S(1)} %bitcast.26, s32[1,8]{1,0:T(1,128)S(1)} %bitcast.32, f32[1,8]{1,0:T(1,128)S(1)} %bitcast.33, ...), custom_call_target="tpu_custom_call" | custom-call | flops 1048576 | bytes 1048576 | tf_op jit(solution)/shard_map/shift/pallas_call | solution.py:47
  19.5 0.2 collective-permute-done.4.from_chip
  19.7 0.7 %halo.1 = (bf16[8,128,256]{2,1,0:T(8,128)(2,1)S(1)}, f32[8,256]{1,0:T(8,128)S(1)}, bf16[2,144,256]{2,1,0:T(8,128)(2,1)S(1)}) custom-call(s32[2,4]{1,0:T(2,128)S(1)} %bitcast.27, s32[2]{0:T(128)S(1)} %pad_add_fusion.place, bf16[2,2,128,256]{3,2,1,0:T(8,128)(2,1)S(1)} %copy-done, bf16[8,128,256]{2,1,0:T(8,128)(2,1)S(1)} %get-tuple-element.13.shifted, ...), custom_call_target="tpu_custom_call" | custom-call | flops 1048576 | bytes 1048576 | tf_op jit(solution)/shard_map/halo/pallas_call | solution.py:47
  20.5 1.6 %terms.1 = bf16[512,256]{1,0:T(8,128)(2,1)} custom-call(s32[2,4]{1,0:T(2,128)S(1)} %bitcast.28, bf16[2,128,256]{2,1,0:T(8,128)(2,1)S(1)} %bitcast.22, bf16[2,128,256]{2,1,0:T(8,128)(2,1)S(1)} %collective-permute-done.1.near.great2, bf16[2,128,256]{2,1,0:T(8,128)(2,1)S(1)} %collective-permute-done.2.next_near.great3, ...), custom_call_target="tpu_custom_call" | custom-call | flops 1048576 | bytes 1048576 | tf_op jit(solution)/shard_map/terms/pallas_call | solution.py:47
  22.1 5.4 %all-to-all-start = ((bf16[16,32,256]{2,1,0:T(8,128)(2,1)}), bf16[16,32,256]{2,1,0:T(8,128)(2,1)S(1)}, u32[]{:S(2)}, u32[]{:S(2)}) async-start(bf16[16,32,256]{2,1,0:T(8,128)(2,1)} %bitcast.16), calls=%async_computation | async-start | bytes 524288 | tf_op jit(solution)/shard_map/all_to_all | solution.py:268
  27.5 0.1 collective-permute-start.5
  27.6 2.9 %collective-permute-start.7 = (bf16[2,144,256]{2,1,0:T(8,128)(2,1)S(1)}, bf16[2,144,256]{2,1,0:T(8,128)(2,1)S(1)}, u32[]{:S(2)}, u32[]{:S(2)}) collective-permute-start(bf16[2,144,256]{2,1,0:T(8,128)(2,1)S(1)} %get-tuple-element.20.own), channel_id=1, source_target_pairs={{0,32},{16,48},{32,0},{48,16},{1,33},{17,49},{33,1},{49,17},{2,34}... | collective-permute-start | bytes 442376 | tf_op jit(solution)/shard_map/ppermute | solution.py:223
  30.5 0.3 collective-permute-start.6
  30.8 4.4 %all-to-all-done.got = bf16[16,32,256]{2,1,0:T(8,128)(2,1)S(1)} async-done(((bf16[16,32,256]{2,1,0:T(8,128)(2,1)}), bf16[16,32,256]{2,1,0:T(8,128)(2,1)S(1)}, u32[]{:S(2)}, u32[]{:S(2)}) %all-to-all-start) | async-done | bytes 262176 | tf_op jit(solution)/shard_map/all_to_all | solution.py:268
  35.2 0.7 %column.1 = bf16[16,16,256]{2,1,0:T(8,128)(2,1)} custom-call(bf16[16,32,256]{2,1,0:T(8,128)(2,1)S(1)} %all-to-all-done.got), custom_call_target="tpu_custom_call" | custom-call | flops 1048576 | bytes 1048576 | tf_op jit(solution)/shard_map/column/pallas_call | solution.py:47
  35.9 5.5 %all-to-all-start.1 = ((bf16[16,16,256]{2,1,0:T(8,128)(2,1)}), bf16[16,16,256]{2,1,0:T(8,128)(2,1)S(1)}, u32[]{:S(2)}, u32[]{:S(2)}) async-start(bf16[16,16,256]{2,1,0:T(8,128)(2,1)} %column.1), calls=%async_computation.1 | async-start | bytes 262144 | tf_op jit(solution)/shard_map/all_to_all | solution.py:272
  41.4 2.0 %weights.1 = (bf16[4,128,576]{2,1,0:T(8,128)(2,1)S(1)}, f32[32,16]{1,0:T(8,128)S(1)}) custom-call(s32[2,4]{1,0:T(2,128)S(1)} %bitcast.31, s32[2]{0:T(128)S(1)} %pad_add_fusion.place, s32[8]{0:T(128)S(1)} %copy-done.4, f32[8]{0:T(128)S(1)} %copy-done.5, f32[8,128]{1,0:T(8,128)S(1)} %bitcast.25, s32[1,128]{1,0:T(1,128)S(1)} %bitcast.35), custom_call_target="tpu_custom_call" | custom-call | flops 1048576 | bytes 1048576 | tf_op jit(solution)/shard_map/weights/pallas_call | solution.py:47
  43.5 1.6 %sigma.1 = bf16[2,2,128,256]{3,2,1,0:T(8,128)(2,1)} custom-call(s32[2,4]{1,0:T(2,128)S(1)} %bitcast.29, bf16[4,128,576]{2,1,0:T(8,128)(2,1)S(1)} %get-tuple-element.18.main, bf16[2,2,128,256]{3,2,1,0:T(8,128)(2,1)S(1)} %copy-done, bf16[2,144,256]{2,1,0:T(8,128)(2,1)S(1)} %get-tuple-element.20.own, bf16[2,144,256]{2,1,0:T(8,128)(2,1)S(1)} %collective-permute-done.5.less1, ...), custom_call_target="tpu_custom_call" | custom-call | flops 17179869184 | bytes 1048576 | tf_op jit(solution)/shard_map/sigma/pallas_call | solution.py:47
  45.1 5.5 %all-to-all-done.1.got = bf16[16,16,256]{2,1,0:T(8,128)(2,1)S(1)} async-done(((bf16[16,16,256]{2,1,0:T(8,128)(2,1)}), bf16[16,16,256]{2,1,0:T(8,128)(2,1)S(1)}, u32[]{:S(2)}, u32[]{:S(2)}) %all-to-all-start.1) | async-done | bytes 131104 | tf_op jit(solution)/shard_map/all_to_all | solution.py:272
  50.6 0.8 %owner.1 = f32[32,256]{1,0:T(8,128)} custom-call(bf16[16,16,256]{2,1,0:T(8,128)(2,1)S(1)} %all-to-all-done.1.got, f32[32,16]{1,0:T(8,128)S(1)} %get-tuple-element.21.owner), custom_call_target="tpu_custom_call" | custom-call | flops 1048576 | bytes 1048576 | tf_op jit(solution)/shard_map/owner/pallas_call | solution.py:47
  (25 shorter events, 0.2 us)
Async XLA Ops:
  0.6 8.8 %copy-start = (bf16[2,2,128,256]{3,2,1,0:T(8,128)(2,1)S(1)}, bf16[2,2,128,256]{3,2,1,0:T(8,128)(2,1)}, u32[]{:S(2)}) copy-start(bf16[2,2,128,256]{3,2,1,0:T(8,128)(2,1)} %green.5) | copy-start | bytes 786436
  1.6 18.8 %collective-permute-start = (bf16[272,256]{1,0:T(8,128)(2,1)S(1)}, bf16[272,256]{1,0:T(8,128)(2,1)S(1)}, u32[]{:S(2)}, u32[]{:S(2)}) collective-permute-start(bf16[272,256]{1,0:T(8,128)(2,1)S(1)} %slice.30), channel_id=1, source_target_pairs={{0,8},{8,0},{1,9},{9,1},{2,10},{10,2},{3,11},{11,3},{4,12},{12,4},... | collective-permute-start | bytes 417800 | tf_op jit(solution)/shard_map/ppermute | solution.py:226
  9.5 0.7 %copy-start.6 = (s32[128]{0:T(128)S(1)}, s32[128]{0:T(128)}, u32[]{:S(2)}) copy-start(s32[128]{0:T(128)} %param.8) | copy-start | bytes 1540
  10.2 10.3 %collective-permute-start.2 = (bf16[2,128,256]{2,1,0:T(8,128)(2,1)S(1)}, bf16[2,128,256]{2,1,0:T(8,128)(2,1)S(1)}, u32[]{:S(2)}, u32[]{:S(2)}) collective-permute-start(bf16[2,128,256]{2,1,0:T(8,128)(2,1)S(1)} %slice_bitcast_fusion), channel_id=1, source_target_pairs={{0,32},{16,48},{32,0},{48,16},{1,33},{17,49},{33,1},{49,17},{2,34}... | collective-permute-start | bytes 393224 | tf_op jit(solution)/shard_map/ppermute | solution.py:223
  13.2 7.3 %collective-permute-start.1 = (bf16[2,128,256]{2,1,0:T(8,128)(2,1)S(1)}, bf16[2,128,256]{2,1,0:T(8,128)(2,1)S(1)}, u32[]{:S(2)}, u32[]{:S(2)}) collective-permute-start(bf16[2,128,256]{2,1,0:T(8,128)(2,1)S(1)} %slice_bitcast_fusion), channel_id=1, source_target_pairs={{0,16},{16,0},{32,48},{48,32},{1,17},{17,1},{33,49},{49,33},{2,18}... | collective-permute-start | bytes 393224 | tf_op jit(solution)/shard_map/ppermute | solution.py:222
  13.6 6.1 %collective-permute-start.4 = (bf16[6,16,256]{2,1,0:T(8,128)(2,1)S(1)}, bf16[6,16,256]{2,1,0:T(8,128)(2,1)S(1)}, u32[]{:S(2)}, u32[]{:S(2)}) collective-permute-start(bf16[6,16,256]{2,1,0:T(8,128)(2,1)S(1)} %get-tuple-element.25), channel_id=1, source_target_pairs={{1,2},{3,4},{5,6},{2,1},{4,3},{6,5},{9,10},{11,12},{13,14},{10,9},... | collective-permute-start | bytes 147464 | tf_op jit(solution)/shard_map/ppermute | solution.py:237
  17.7 1.8 %collective-permute-start.3 = (bf16[6,16,256]{2,1,0:T(8,128)(2,1)S(1)}, bf16[6,16,256]{2,1,0:T(8,128)(2,1)S(1)}, u32[]{:S(2)}, u32[]{:S(2)}) collective-permute-start(bf16[6,16,256]{2,1,0:T(8,128)(2,1)S(1)} %get-tuple-element.24), channel_id=1, source_target_pairs={{0,1},{1,0},{2,3},{3,2},{4,5},{5,4},{6,7},{7,6},{8,9},{9,8},{10,11... | collective-permute-start | bytes 147464 | tf_op jit(solution)/shard_map/ppermute | solution.py:234
  17.9 0.7 %copy-start.3 = (s32[4,2]{0,1:T(2,128)S(1)}, s32[4,2]{0,1:T(2,128)}, u32[]{:S(2)}) copy-start(s32[4,2]{0,1:T(2,128)} %param.10) | copy-start | bytes 100
  17.9 0.7 %copy-start.5 = (f32[8]{0:T(128)S(1)}, f32[8]{0:T(128)}, u32[]{:S(2)}) copy-start(f32[8]{0:T(128)} %occupancy.1) | copy-start | bytes 100
  17.9 0.7 %copy-start.1 = (f32[128,8]{0,1:T(8,128)S(1)}, f32[128,8]{0,1:T(8,128)}, u32[]{:S(2)}) copy-start(f32[128,8]{0,1:T(8,128)} %param.13) | copy-start | bytes 12292
  17.9 0.7 %copy-start.2 = (s32[4,1,2]{0,2,1:T(2,128)S(1)}, s32[4,1,2]{0,2,1:T(2,128)}, u32[]{:S(2)}) copy-start(s32[4,1,2]{0,2,1:T(2,128)} %param.9) | copy-start | bytes 100
  17.9 0.7 %copy-start.4 = (s32[8]{0:T(128)S(1)}, s32[8]{0:T(128)}, u32[]{:S(2)}) copy-start(s32[8]{0:T(128)} %offsets.1) | copy-start | bytes 100
  22.1 13.1 %all-to-all-start = ((bf16[16,32,256]{2,1,0:T(8,128)(2,1)}), bf16[16,32,256]{2,1,0:T(8,128)(2,1)S(1)}, u32[]{:S(2)}, u32[]{:S(2)}) async-start(bf16[16,32,256]{2,1,0:T(8,128)(2,1)} %bitcast.16), calls=%async_computation | async-start | bytes 524288 | tf_op jit(solution)/shard_map/all_to_all | solution.py:268
  27.5 16.0 %collective-permute-start.5 = (bf16[2,144,256]{2,1,0:T(8,128)(2,1)S(1)}, bf16[2,144,256]{2,1,0:T(8,128)(2,1)S(1)}, u32[]{:S(2)}, u32[]{:S(2)}) collective-permute-start(bf16[2,144,256]{2,1,0:T(8,128)(2,1)S(1)} %get-tuple-element.20.own), channel_id=1, source_target_pairs={{0,8},{8,0},{1,9},{9,1},{2,10},{10,2},{3,11},{11,3},{4,12},{12,4},... | collective-permute-start | bytes 442376 | tf_op jit(solution)/shard_map/ppermute | solution.py:267
  27.6 15.9 %collective-permute-start.7 = (bf16[2,144,256]{2,1,0:T(8,128)(2,1)S(1)}, bf16[2,144,256]{2,1,0:T(8,128)(2,1)S(1)}, u32[]{:S(2)}, u32[]{:S(2)}) collective-permute-start(bf16[2,144,256]{2,1,0:T(8,128)(2,1)S(1)} %get-tuple-element.20.own), channel_id=1, source_target_pairs={{0,32},{16,48},{32,0},{48,16},{1,33},{17,49},{33,1},{49,17},{2,34}... | collective-permute-start | bytes 442376 | tf_op jit(solution)/shard_map/ppermute | solution.py:223
  30.5 13.0 %collective-permute-start.6 = (bf16[2,144,256]{2,1,0:T(8,128)(2,1)S(1)}, bf16[2,144,256]{2,1,0:T(8,128)(2,1)S(1)}, u32[]{:S(2)}, u32[]{:S(2)}) collective-permute-start(bf16[2,144,256]{2,1,0:T(8,128)(2,1)S(1)} %get-tuple-element.20.own), channel_id=1, source_target_pairs={{0,16},{16,0},{32,48},{48,32},{1,17},{17,1},{33,49},{49,33},{2,18}... | collective-permute-start | bytes 442376 | tf_op jit(solution)/shard_map/ppermute | solution.py:222
  35.9 14.7 %all-to-all-start.1 = ((bf16[16,16,256]{2,1,0:T(8,128)(2,1)}), bf16[16,16,256]{2,1,0:T(8,128)(2,1)S(1)}, u32[]{:S(2)}, u32[]{:S(2)}) async-start(bf16[16,16,256]{2,1,0:T(8,128)(2,1)} %column.1), calls=%async_computation.1 | async-start | bytes 262144 | tf_op jit(solution)/shard_map/all_to_all | solution.py:272

commit v4 on v3

--- a/solution.py
+++ b/solution.py
@@ -10,10 +10,12 @@
 HALO = 4
 AXES = ("x", "y", "zh", "zl", "c")
 F32 = jnp.float32
+PIECES = 4
 BF16 = jnp.bfloat16
 HIGHEST = lax.Precision.HIGHEST
 SMEM = pl.BlockSpec(memory_space=pltpu.SMEM)
 LIMIT = 12 * 1024 * 1024
+BEGIN_LIMIT = 12 * 1024 * 1024
 VMEM = pl.BlockSpec(memory_space=pltpu.VMEM)
 
 
@@ -36,19 +38,27 @@
 
 
 def pair_products(great, shifted, k):
-    great = great.astype(F32)
     return [
         jnp.sum(great * shifted[k * HALO + d].astype(F32), axis=0, keepdims=True)
         for d in range(HALO)
     ]
 
 
-def call(kernel, name, outs, specs, args, scratch=(), flops=2**20):
+def entry(table, i, j):
+    return table[i : i + 1, j : j + 1]
+
+
+def choose(blocks, index):
+    low, high = blocks[0].astype(F32), blocks[1].astype(F32)
+    return jnp.where(jnp.broadcast_to(index, low.shape) == 0, low, high)
+
+
+def call(kernel, name, outs, specs, args, scratch=(), flops=2**20, out_specs=None):
     return pl.pallas_call(
         kernel,
         out_shape=outs,
         in_specs=specs,
-        out_specs=jax.tree.map(lambda _: VMEM, outs),
+        out_specs=out_specs or jax.tree.map(lambda _: VMEM, outs),
         scratch_shapes=scratch,
         compiler_params=pltpu.CompilerParams(vmem_limit_bytes=LIMIT),
         cost_estimate=pl.CostEstimate(flops=flops, bytes_accessed=2**20, transcendentals=0),
@@ -60,14 +70,46 @@
     return jax.ShapeDtypeStruct(dims, dtype)
 
 
-def shift_kernel(q_row, mask, green, *rest):
-    onehot, shifted = rest[-2:]
+def begin_kernel(green, *refs):
+    count = (len(refs) - 3) // 2
+    small, great, wide, kept, sems = refs[:count], refs[count], refs[count + 1], refs[count + 2 : -1], refs[-1]
+    pairs = list(zip(small, kept))
+    kd, width, _ = great.shape
+    pairs.append((green.at[0, 0, pl.ds(0, 16)], wide.at[pl.ds(0, 16)]))
+    for k in range(kd):
+        pairs.append((green.at[1, k], great.at[k]))
+        pairs.append((green.at[1, k], wide.at[pl.ds(16 + k * width, width)]))
+    copies = [pltpu.make_async_copy(a, b, sems.at[i]) for i, (a, b) in enumerate(pairs)]
+    for copy in reversed(copies):
+        copy.start()
+    for copy in copies:
+        copy.wait()
+
+
+def begin(green, *small):
+    anywhere = pl.BlockSpec(memory_space=pltpu.HBM)
+    _, kd, width, norb = green.shape
+    outs = [shape(kd, width, norb), shape(16 + kd * width, norb)] + [shape(*x.shape, dtype=x.dtype) for x in small]
+    green, *small = [pltpu.with_memory_space_constraint(x, pltpu.HBM) for x in (green, *small)]
+    return pl.pallas_call(
+        begin_kernel,
+        out_shape=outs,
+        in_specs=[anywhere] * (1 + len(small)),
+        out_specs=[VMEM] * len(outs),
+        scratch_shapes=[pltpu.SemaphoreType.DMA((len(small) + 2 * kd + 1,))],
+        compiler_params=pltpu.CompilerParams(vmem_limit_bytes=BEGIN_LIMIT),
+        cost_estimate=pl.CostEstimate(flops=0, bytes_accessed=2**18, transcendentals=0),
+        name="begin",
+    )(green, *small)
+
+
+def shift_kernel(q_row, mask, green, onehot, shifted):
     kd, rounds = q_row.shape
     width = mask.shape[1]
     goal = jnp.zeros((1, onehot.shape[1]), jnp.int32)
     lane = iota(goal.shape, 1)
     for p in range(rounds * kd):
-        goal = jnp.where(lane // HALO == p, q_row[p % kd, p // kd] * HALO + lane % HALO, goal)
+        goal = jnp.where(lane // HALO == p, entry(q_row, p % kd, p // kd) * HALO + lane % HALO, goal)
     onehot[...] = (iota(onehot.shape, 0) == goal).astype(F32).astype(BF16)
 
     row, col = iota((width, width), 0), iota((width, width), 1)
@@ -80,7 +122,7 @@
 
 def halo_kernel(order, place, green, shifted, from_core, from_chip, full, first, extended):
     kd, width = green.shape[1:3]
-    first_core = jnp.broadcast_to(place[1], from_core.shape) == 0
+    first_core = jnp.broadcast_to(entry(place, 0, 1)[None], from_core.shape) == 0
     core, chip = from_core[...].astype(F32), from_chip[...].astype(F32)
     before = jnp.where(first_core, chip, core).astype(BF16)
     after = jnp.where(first_core, core, chip).astype(BF16)
@@ -100,17 +142,25 @@
         extended[k, width:] = dot(pick, jnp.concatenate(ends, axis=0)).astype(BF16)
     lines = []
     for k in range(kd):
-        lines += pair_products(green[1, order[k, 0]], full, k)
+        lines += pair_products(choose(green[1], entry(order, k, 0)), full, k)
     first[...] = jnp.concatenate(lines, axis=0)
 
 
-def terms_kernel(order, far, near, next_near, shifted, first, onehot, out):
+def terms_kernel(order, far, near, next_near, shifted, first, onehot, out, held, sems):
     lines = [first[...]]
     for r, ref in ((1, far), (2, near), (3, next_near)):
         for k in range(far.shape[0]):
-            lines += pair_products(ref[order[k, r]], shifted, k)
+            lines += pair_products(choose(ref, entry(order, k, r)), shifted, k)
     terms = jnp.concatenate(lines, axis=0).astype(BF16)
-    out[...] = dot(onehot[...], terms).astype(BF16)
+    step = out.shape[0] // PIECES
+    copies = []
+    for i in range(PIECES):
+        rows = pl.ds(i * step, step)
+        held[rows] = dot(onehot[rows], terms).astype(BF16)
+        copies.append(pltpu.make_async_copy(held.at[rows], out.at[rows], sems.at[i]))
+        copies[-1].start()
+    for copy in copies:
+        copy.wait()
 
 
 def column_kernel(got, out):
@@ -137,8 +187,8 @@
     off_col = jnp.zeros((modes, width), jnp.int32)
     occ_col = jnp.zeros((modes, width), F32)
     for m in range(modes):
-        off_col = jnp.where(iota(off_col.shape, 0) == m, offsets[m], off_col)
-        occ_col = jnp.where(iota(off_col.shape, 0) == m, occupancy[m], occ_col)
+        off_col = jnp.where(iota(off_col.shape, 0) == m, offsets[0, m], off_col)
+        occ_col = jnp.where(iota(off_col.shape, 0) == m, occupancy[0, m], occ_col)
     emit, absorb = [], []
     for d in range(1, HALO + 1):
         emit.append(dot(strength, jnp.where(off_col == d, occ_col + 1.0, 0.0), HIGHEST))
@@ -146,7 +196,7 @@
 
     rows, cols = iota(owner.shape, 0), iota(owner.shape, 1)
     wide = (owner.shape[0], coupling.shape[1])
-    mine = (iota(wide, 1) == place[0] + iota(wide, 0) // modes).astype(F32)
+    mine = (iota(wide, 1) == place[0, 0] + iota(wide, 0) // modes).astype(F32)
     factor = lax.dot_general(
         mine, coupling[...], (((1,), (1,)), ((), ())), precision=HIGHEST, preferred_element_type=F32
     )
@@ -154,7 +204,7 @@
     factor = jnp.sum(jnp.where(branch, factor, 0.0), axis=1, keepdims=True) * scale
     off = jnp.zeros(owner.shape, jnp.int32)
     for m in range(modes):
-        off = jnp.where(rows % modes == m, offsets[m], off)
+        off = jnp.where(rows % modes == m, offsets[0, m], off)
     hit = (rows // modes == cols // HALO) & (off == cols % HALO + 1)
     owner[...] = jnp.where(hit, factor, 0.0)
 
@@ -212,9 +262,17 @@
     rounds = pair_order.shape[0]
     count = lax.axis_size(("zl", "c"))
     owned = coupling.shape[0] // lax.axis_size(("x", "y", "zh"))
-    order, q_row, spread, mask_row = pair_order[:, 0].T, q_index.T, coupling.T, mask[None, :]
+    mine, wide, order, q_row, spread, mask_row, offset_row, occupancy_row = begin(
+        green,
+        pair_order[:, 0].T,
+        q_index.T,
+        coupling.T,
+        mask[None, :],
+        offsets[None, :],
+        occupancy[None, :],
+    )
     place = [lax.axis_index(("x", "y", "zh")) * owned, lax.axis_index("c")]
-    place = jnp.stack([jnp.asarray(x, jnp.int32) for x in place])
+    place = jnp.stack([jnp.asarray(x, jnp.int32) for x in place])[None]
 
     swap = [(0, 1), (1, 0)]
 
@@ -222,10 +280,9 @@
         near = lax.ppermute(x, "y", [(i, i ^ 1) for i in range(4)])
         return near, lax.ppermute(x, "y", [(i, i ^ 2) for i in range(4)])
 
-    more = green.reshape(-1, norb)[kd * width - 16 :]
-    far = lax.ppermute(more, "zh", swap)[16:].reshape(kd, width, norb)
+    far = lax.ppermute(wide, "zh", swap)[16:].reshape(kd, width, norb)
     first, last = green[:, :, :16], green[:, :, width - 16 :]
-    masked = first[0] * mask[None, :16, None].astype(BF16)
+    masked = first[0] * mask_row[0, None, :16, None].astype(BF16)
     first_core = lax.axis_index("c") == 0
 
     def edge(x):
@@ -235,7 +292,7 @@
     meet = [(i, i + 1) for i in range(1, count - 1, 2)]
     to_chip = edge(jnp.where(first_core, first, last))
     from_chip = lax.ppermute(to_chip, ("zl", "c"), meet + [(j, i) for i, j in meet])
-    great = (far, *exchange(tie(green[1], to_chip)))
+    great = (far, *exchange(tie(mine, to_chip)))
     onehot, shifted = call(
         shift_kernel,
         "shift",
@@ -243,8 +300,8 @@
             shape(coupling.shape[0] * HALO, rounds * kd * HALO),
             shape(kd * HALO, width, norb),
         ),
-        [SMEM] + [VMEM] * 6,
-        (q_row, mask_row, green, order, offsets[None], occupancy[None], spread),
+        [VMEM] * 3,
+        (q_row, mask_row, green),
     )
     shifted, first, extended = call(
         halo_kernel,
@@ -254,15 +311,17 @@
             shape(kd * HALO, norb, dtype=F32),
             shape(kd, width + 16, norb),
         ),
-        [SMEM] * 2 + [VMEM] * 4,
+        [VMEM] * 6,
         (order, place, green, shifted, from_core, from_chip),
     )
     dense = call(
         terms_kernel,
         "terms",
         shape(onehot.shape[0], norb),
-        [SMEM] + [VMEM] * 6,
+        [VMEM] * 7,
         (order, *great, shifted, first, onehot),
+        scratch=[pltpu.VMEM((onehot.shape[0], norb), BF16), pltpu.SemaphoreType.DMA((PIECES,))],
+        out_specs=pl.BlockSpec(memory_space=pl.ANY),
     )
     less = (lax.ppermute(extended, "zh", swap), *exchange(tie(extended, dense)))
     got = lax.all_to_all(dense.reshape(16, -1, norb), ("x", "y"), 0, 0, tiled=True)
@@ -279,7 +338,7 @@
             shape(owned * offsets.shape[0], owned * HALO, dtype=F32),
         ),
         [SMEM] * 4 + [VMEM] * 2,
-        (q_row, place, offsets, occupancy, tie(spread, sent), mask_row),
+        (q_row, place, offset_row, occupancy_row, tie(spread, sent), mask_row),
     )
     sigma = call(
         sigma_kernel,

time: 51.8 us -> 51.6 us (level)
  local copies, waits for them, and re-layouts: 2.37 us -> 0.02 us
  starting transfers between devices: 29.5 us -> 30.8 us
  waiting for transfers between devices: 10.2 us -> 11.3 us
    unnamed x14 -> x2, local copies, waits for them, and re-layouts: 1.37 us -> 0.01 us
    all_to_all x1, starting transfers between devices: 5.52 us -> 6.62 us  [on_device(): got = lax.all_to_all(sent, ('zh', 'zl', 'c'), 0, 0, tiled=True)]
    slice x2 -> x1, local copies, waits for them, and re-layouts: 0.99 us -> 0.01 us  [on_device(): far = lax.ppermute(wide, 'zh', swap)[16:].reshape(kd, width, norb)]
    ppermute x1, waiting for transfers between devices: 0.01 us -> 0.84 us  [on_device(): lax.ppermute(edge(jnp.where(first_core, last, first)), 'c', swap)]
    pallas_call x7 -> x8, Pallas kernels: 8.32 us -> 8.16 us  [the longest x7 7.08 us: call(): pl.pallas_call(kernel, out_shape=outs, in_specs=specs, out_specs=out_spec...]
  transfers between devices with their start and end apart: 10 -> 10, of which waited for: 3 -> 4; matrix products, arithmetic and copies ran while one was open for 0% -> 0% of each run, Pallas kernels for 12% -> 10%
where the time goes in v4:
time: 51.6 us; the launch traced here: 51.3 us
  starting transfers between devices  30.8 us (60%)
  waiting for transfers between devices  11.3 us (22%)
  Pallas kernels  8.16 us (16%)
  between operations  0.8 us (2%)
    ppermute x1, starting transfers between devices, on_device(): far = lax.ppermute(wide, 'zh', swap)[16:].reshape(kd, width, norb)  7.83 us
    pallas_call x7, Pallas kernels, call(): pl.pallas_call(kernel, out_shape=outs, in_specs=specs, out_specs=out_spec...  7.08 us
    all_to_all x1, starting transfers between devices, on_device(): got = lax.all_to_all(sent, ('zh', 'zl', 'c'), 0, 0, tiled=True)  6.62 us
    ppermute x2, starting transfers between devices, exchange(): return (near, lax.ppermute(x, 'y', [(i, i ^ 2) for i in range(4)]))  5.87 us
    all_to_all x1, starting transfers between devices, on_device(): lax.all_to_all(dense.reshape(16, -1, norb), ('x', 'y'), 0, 0, tiled=True)  5.62 us
    all_to_all x1, waiting for transfers between devices, on_device(): got = lax.all_to_all(sent, ('zh', 'zl', 'c'), 0, 0, tiled=True)  5.46 us
    all_to_all x1, waiting for transfers between devices, on_device(): lax.all_to_all(dense.reshape(16, -1, norb), ('x', 'y'), 0, 0, tiled=True)  4.22 us
    ppermute x1, starting transfers between devices, on_device(): lax.ppermute(to_chip, ('zl', 'c'), meet + [(j, i) for i, j in meet])  4.04 us
  transfers between devices with their start and end apart: 10, of which 4 were waited for; matrix products, arithmetic and copies ran while one was open for 0% of the time, Pallas kernels for 10%

profile of v4, /device:TPU:1, one launch (start us, length us, event | category | flops | bytes accessed | tf_op | source)
XLA Modules:
  0.0 51.3 jit_solution(15426641623312946369)
XLA Ops:
  0.6 1.1 %begin.1 = (bf16[2,128,256]{2,1,0:T(8,128)(2,1)S(1)}, bf16[272,256]{1,0:T(8,128)(2,1)S(1)}, s32[2,4]{1,0:T(2,128)S(1)}, s32[2,4]{1,0:T(2,128)S(1)}, f32[8,128]{1...) custom-call(bf16[2,2,128,256]{3,2,1,0:T(8,128)(2,1)} %green.7, s32[2,4]{1,0:T(2,128)} %bitcast.27, ...), custom_call_target="tpu_custom_call" | custom-call | bytes 262144 | tf_op jit(solution)/shard_map/begin/pallas_call | solution.py:94
  1.7 7.8 %collective-permute-start = (bf16[272,256]{1,0:T(8,128)(2,1)S(1)}, bf16[272,256]{1,0:T(8,128)(2,1)S(1)}, u32[]{:S(2)}, u32[]{:S(2)}) collective-permute-start(bf16[272,256]{1,0:T(8,128)(2,1)S(1)} %get-tuple-element.25), channel_id=1, source_target_pairs={{0,8},{8,0},{1,9},{9,1},{2,10},{10,2},{3,11},{11,3},{4,12},{12,4},... | collective-permute-start | bytes 417800 | tf_op jit(solution)/shard_map/ppermute | solution.py:283
  9.6 0.1 bitcast_multiply_fusion
  9.7 3.0 %collective-permute-start.2 = (bf16[2,128,256]{2,1,0:T(8,128)(2,1)S(1)}, bf16[2,128,256]{2,1,0:T(8,128)(2,1)S(1)}, u32[]{:S(2)}, u32[]{:S(2)}) collective-permute-start(bf16[2,128,256]{2,1,0:T(8,128)(2,1)S(1)} %get-tuple-element.28), channel_id=1, source_target_pairs={{0,32},{16,48},{32,0},{48,16},{1,33},{17,49},{33,1},{49,17},{2,34}... | collective-permute-start | bytes 393224 | tf_op jit(solution)/shard_map/ppermute | solution.py:281
  12.7 0.4 collective-permute-start.1
  13.1 4.0 %collective-permute-start.4 = (bf16[6,16,256]{2,1,0:T(8,128)(2,1)S(1)}, bf16[6,16,256]{2,1,0:T(8,128)(2,1)S(1)}, u32[]{:S(2)}, u32[]{:S(2)}) collective-permute-start(bf16[6,16,256]{2,1,0:T(8,128)(2,1)S(1)} %get-tuple-element.41), channel_id=1, source_target_pairs={{1,2},{3,4},{5,6},{2,1},{4,3},{6,5},{9,10},{11,12},{13,14},{10,9},... | collective-permute-start | bytes 147464 | tf_op jit(solution)/shard_map/ppermute | solution.py:294
  17.1 0.1 collective-permute-start.3
  17.2 0.1 add_bitcast_fusion.place
  17.3 0.3 shift.1
  17.6 0.8 %collective-permute-done.3.from_core = bf16[6,16,256]{2,1,0:T(8,128)(2,1)S(1)} collective-permute-done((bf16[6,16,256]{2,1,0:T(8,128)(2,1)S(1)}, bf16[6,16,256]{2,1,0:T(8,128)(2,1)S(1)}, u32[]{:S(2)}, u32[]{:S(2)}) %collective-permute-start.3) | collective-permute-done | bytes 49184 | tf_op jit(solution)/shard_map/ppermute | solution.py:291
  18.4 0.7 %collective-permute-done.4.from_chip = bf16[6,16,256]{2,1,0:T(8,128)(2,1)S(1)} collective-permute-done((bf16[6,16,256]{2,1,0:T(8,128)(2,1)S(1)}, bf16[6,16,256]{2,1,0:T(8,128)(2,1)S(1)}, u32[]{:S(2)}, u32[]{:S(2)}) %collective-permute-start.4) | collective-permute-done | bytes 49184 | tf_op jit(solution)/shard_map/ppermute | solution.py:294
  19.2 0.3 halo.1
  19.5 1.3 %terms.1 = bf16[512,256]{1,0:T(8,128)(2,1)} custom-call(s32[2,4]{1,0:T(2,128)S(1)} %get-tuple-element.20.order, bf16[2,128,256]{2,1,0:T(8,128)(2,1)S(1)} %bitcast.21, bf16[2,128,256]{2,1,0:T(8,128)(2,1)S(1)} %collective-permute-done.1.near.great2, bf16[2,128,256]{2,1,0:T(8,128)(2,1)S(1)} %collective-permute-done.2.next_near.great3, ...), custom_call_target="tpu_custom_call" | custom-call | flops 1048576 | bytes 1048576 | tf_op jit(solution)/shard_map/terms/pallas_call | solution.py:57
  20.9 5.6 %all-to-all-start = ((bf16[16,32,256]{2,1,0:T(8,128)(2,1)}), bf16[16,32,256]{2,1,0:T(8,128)(2,1)S(1)}, u32[]{:S(2)}, u32[]{:S(2)}) async-start(bf16[16,32,256]{2,1,0:T(8,128)(2,1)} %bitcast.15), calls=%async_computation | async-start | bytes 524288 | tf_op jit(solution)/shard_map/all_to_all | solution.py:327
  26.5 0.1 collective-permute-start.5
  26.6 2.9 %collective-permute-start.7 = (bf16[2,144,256]{2,1,0:T(8,128)(2,1)S(1)}, bf16[2,144,256]{2,1,0:T(8,128)(2,1)S(1)}, u32[]{:S(2)}, u32[]{:S(2)}) collective-permute-start(bf16[2,144,256]{2,1,0:T(8,128)(2,1)S(1)} %get-tuple-element.36.own), channel_id=1, source_target_pairs={{0,32},{16,48},{32,0},{48,16},{1,33},{17,49},{33,1},{49,17},{2,34}... | collective-permute-start | bytes 442376 | tf_op jit(solution)/shard_map/ppermute | solution.py:281
  29.5 0.3 collective-permute-start.6
  29.7 4.2 %all-to-all-done.got = bf16[16,32,256]{2,1,0:T(8,128)(2,1)S(1)} async-done(((bf16[16,32,256]{2,1,0:T(8,128)(2,1)}), bf16[16,32,256]{2,1,0:T(8,128)(2,1)S(1)}, u32[]{:S(2)}, u32[]{:S(2)}) %all-to-all-start) | async-done | bytes 262176 | tf_op jit(solution)/shard_map/all_to_all | solution.py:327
  34.0 0.7 %column.1 = bf16[16,16,256]{2,1,0:T(8,128)(2,1)} custom-call(bf16[16,32,256]{2,1,0:T(8,128)(2,1)S(1)} %all-to-all-done.got), custom_call_target="tpu_custom_call" | custom-call | flops 1048576 | bytes 1048576 | tf_op jit(solution)/shard_map/column/pallas_call | solution.py:57
  34.7 6.6 %all-to-all-start.1 = ((bf16[16,16,256]{2,1,0:T(8,128)(2,1)}), bf16[16,16,256]{2,1,0:T(8,128)(2,1)S(1)}, u32[]{:S(2)}, u32[]{:S(2)}) async-start(bf16[16,16,256]{2,1,0:T(8,128)(2,1)} %column.1), calls=%async_computation.1 | async-start | bytes 262144 | tf_op jit(solution)/shard_map/all_to_all | solution.py:331
  41.3 2.0 %weights.1 = (bf16[4,128,576]{2,1,0:T(8,128)(2,1)S(1)}, f32[32,16]{1,0:T(8,128)S(1)}) custom-call(s32[2,4]{1,0:T(2,128)S(1)} %get-tuple-element.21.q_row, s32[1,2]{1,0:T(1,128)S(1)} %add_bitcast_fusion.place, s32[1,8]{1,0:T(1,128)S(1)} %get-tuple-element.22.offsets, f32[1,8]{1,0:T(1,128)S(1)} %get-tuple-element.23.occupancy, ...), custom_call_target="tpu_custom_call" | custom-call | flops 1048576 | bytes 1048576 | tf_op jit(solution)/shard_map/weights/pallas_call | solution.py:57
  43.4 1.6 %sigma.1 = bf16[2,2,128,256]{3,2,1,0:T(8,128)(2,1)} custom-call(s32[2,4]{1,0:T(2,128)S(1)} %get-tuple-element.20.order, bf16[4,128,576]{2,1,0:T(8,128)(2,1)S(1)} %get-tuple-element.34.main, bf16[2,2,128,256]{3,2,1,0:T(8,128)(2,1)S(1)} %copy-done, bf16[2,144,256]{2,1,0:T(8,128)(2,1)S(1)} %get-tuple-element.36.own, ...), custom_call_target="tpu_custom_call" | custom-call | flops 17179869184 | bytes 1048576 | tf_op jit(solution)/shard_map/sigma/pallas_call | solution.py:57
  45.0 5.5 %all-to-all-done.1.got = bf16[16,16,256]{2,1,0:T(8,128)(2,1)S(1)} async-done(((bf16[16,16,256]{2,1,0:T(8,128)(2,1)}), bf16[16,16,256]{2,1,0:T(8,128)(2,1)S(1)}, u32[]{:S(2)}, u32[]{:S(2)}) %all-to-all-start.1) | async-done | bytes 131104 | tf_op jit(solution)/shard_map/all_to_all | solution.py:331
  50.5 0.8 %owner.1 = f32[32,256]{1,0:T(8,128)} custom-call(bf16[16,16,256]{2,1,0:T(8,128)(2,1)S(1)} %all-to-all-done.1.got, f32[32,16]{1,0:T(8,128)S(1)} %get-tuple-element.37.owner), custom_call_target="tpu_custom_call" | custom-call | flops 1048576 | bytes 1048576 | tf_op jit(solution)/shard_map/owner/pallas_call | solution.py:57
  (13 shorter events, 0.1 us)
Async XLA Ops:
  0.6 8.9 %copy-start = (bf16[2,2,128,256]{3,2,1,0:T(8,128)(2,1)S(1)}, bf16[2,2,128,256]{3,2,1,0:T(8,128)(2,1)}, u32[]{:S(2)}) copy-start(bf16[2,2,128,256]{3,2,1,0:T(8,128)(2,1)} %green.7) | copy-start | bytes 786436
  1.7 17.7 %collective-permute-start = (bf16[272,256]{1,0:T(8,128)(2,1)S(1)}, bf16[272,256]{1,0:T(8,128)(2,1)S(1)}, u32[]{:S(2)}, u32[]{:S(2)}) collective-permute-start(bf16[272,256]{1,0:T(8,128)(2,1)S(1)} %get-tuple-element.25), channel_id=1, source_target_pairs={{0,8},{8,0},{1,9},{9,1},{2,10},{10,2},{3,11},{11,3},{4,12},{12,4},... | collective-permute-start | bytes 417800 | tf_op jit(solution)/shard_map/ppermute | solution.py:283
  9.7 9.8 %collective-permute-start.2 = (bf16[2,128,256]{2,1,0:T(8,128)(2,1)S(1)}, bf16[2,128,256]{2,1,0:T(8,128)(2,1)S(1)}, u32[]{:S(2)}, u32[]{:S(2)}) collective-permute-start(bf16[2,128,256]{2,1,0:T(8,128)(2,1)S(1)} %get-tuple-element.28), channel_id=1, source_target_pairs={{0,32},{16,48},{32,0},{48,16},{1,33},{17,49},{33,1},{49,17},{2,34}... | collective-permute-start | bytes 393224 | tf_op jit(solution)/shard_map/ppermute | solution.py:281
  12.7 6.8 %collective-permute-start.1 = (bf16[2,128,256]{2,1,0:T(8,128)(2,1)S(1)}, bf16[2,128,256]{2,1,0:T(8,128)(2,1)S(1)}, u32[]{:S(2)}, u32[]{:S(2)}) collective-permute-start(bf16[2,128,256]{2,1,0:T(8,128)(2,1)S(1)} %get-tuple-element.28), channel_id=1, source_target_pairs={{0,16},{16,0},{32,48},{48,32},{1,17},{17,1},{33,49},{49,33},{2,18}... | collective-permute-start | bytes 393224 | tf_op jit(solution)/shard_map/ppermute | solution.py:280
  13.1 6.1 %collective-permute-start.4 = (bf16[6,16,256]{2,1,0:T(8,128)(2,1)S(1)}, bf16[6,16,256]{2,1,0:T(8,128)(2,1)S(1)}, u32[]{:S(2)}, u32[]{:S(2)}) collective-permute-start(bf16[6,16,256]{2,1,0:T(8,128)(2,1)S(1)} %get-tuple-element.41), channel_id=1, source_target_pairs={{1,2},{3,4},{5,6},{2,1},{4,3},{6,5},{9,10},{11,12},{13,14},{10,9},... | collective-permute-start | bytes 147464 | tf_op jit(solution)/shard_map/ppermute | solution.py:294
  17.1 1.3 %collective-permute-start.3 = (bf16[6,16,256]{2,1,0:T(8,128)(2,1)S(1)}, bf16[6,16,256]{2,1,0:T(8,128)(2,1)S(1)}, u32[]{:S(2)}, u32[]{:S(2)}) collective-permute-start(bf16[6,16,256]{2,1,0:T(8,128)(2,1)S(1)} %get-tuple-element.40), channel_id=1, source_target_pairs={{0,1},{1,0},{2,3},{3,2},{4,5},{5,4},{6,7},{7,6},{8,9},{9,8},{10,11... | collective-permute-start | bytes 147464 | tf_op jit(solution)/shard_map/ppermute | solution.py:291
  20.9 13.1 %all-to-all-start = ((bf16[16,32,256]{2,1,0:T(8,128)(2,1)}), bf16[16,32,256]{2,1,0:T(8,128)(2,1)S(1)}, u32[]{:S(2)}, u32[]{:S(2)}) async-start(bf16[16,32,256]{2,1,0:T(8,128)(2,1)} %bitcast.15), calls=%async_computation | async-start | bytes 524288 | tf_op jit(solution)/shard_map/all_to_all | solution.py:327
  26.5 16.9 %collective-permute-start.5 = (bf16[2,144,256]{2,1,0:T(8,128)(2,1)S(1)}, bf16[2,144,256]{2,1,0:T(8,128)(2,1)S(1)}, u32[]{:S(2)}, u32[]{:S(2)}) collective-permute-start(bf16[2,144,256]{2,1,0:T(8,128)(2,1)S(1)} %get-tuple-element.36.own), channel_id=1, source_target_pairs={{0,8},{8,0},{1,9},{9,1},{2,10},{10,2},{3,11},{11,3},{4,12},{12,4},... | collective-permute-start | bytes 442376 | tf_op jit(solution)/shard_map/ppermute | solution.py:326
  26.6 16.8 %collective-permute-start.7 = (bf16[2,144,256]{2,1,0:T(8,128)(2,1)S(1)}, bf16[2,144,256]{2,1,0:T(8,128)(2,1)S(1)}, u32[]{:S(2)}, u32[]{:S(2)}) collective-permute-start(bf16[2,144,256]{2,1,0:T(8,128)(2,1)S(1)} %get-tuple-element.36.own), channel_id=1, source_target_pairs={{0,32},{16,48},{32,0},{48,16},{1,33},{17,49},{33,1},{49,17},{2,34}... | collective-permute-start | bytes 442376 | tf_op jit(solution)/shard_map/ppermute | solution.py:281
  29.5 13.9 %collective-permute-start.6 = (bf16[2,144,256]{2,1,0:T(8,128)(2,1)S(1)}, bf16[2,144,256]{2,1,0:T(8,128)(2,1)S(1)}, u32[]{:S(2)}, u32[]{:S(2)}) collective-permute-start(bf16[2,144,256]{2,1,0:T(8,128)(2,1)S(1)} %get-tuple-element.36.own), channel_id=1, source_target_pairs={{0,16},{16,0},{32,48},{48,32},{1,17},{17,1},{33,49},{49,33},{2,18}... | collective-permute-start | bytes 442376 | tf_op jit(solution)/shard_map/ppermute | solution.py:280
  34.7 15.8 %all-to-all-start.1 = ((bf16[16,16,256]{2,1,0:T(8,128)(2,1)}), bf16[16,16,256]{2,1,0:T(8,128)(2,1)S(1)}, u32[]{:S(2)}, u32[]{:S(2)}) async-start(bf16[16,16,256]{2,1,0:T(8,128)(2,1)} %column.1), calls=%async_computation.1 | async-start | bytes 262144 | tf_op jit(solution)/shard_map/all_to_all | solution.py:331

commit v5 on v4

--- a/solution.py
+++ b/solution.py
@@ -167,7 +167,7 @@
     total = jnp.sum(got[...].astype(F32), axis=0).astype(BF16)
     half = out.shape[1]
     for dest in range(out.shape[0]):
-        at = (dest // (out.shape[0] // 2)) * half
+        at = dest // (out.shape[0] // 4) % 2 * half
         out[dest] = total[at : at + half]
 
 
@@ -328,7 +328,7 @@
     sent = call(
         column_kernel, "column", shape(2 * count, owned * HALO, norb), [VMEM], (got,)
     )
-    got = lax.all_to_all(sent, ("zh", "zl", "c"), 0, 0, tiled=True)
+    got = lax.all_to_all(sent, ("c", "zh", "zl"), 0, 0, tiled=True)
 
     main, owner = call(
         functools.partial(weights_kernel, scale=1.0 / (width * count)),

time: 51.6 us -> 49.8 us (0.965)
  waiting for transfers between devices: 11.3 us -> 9.4 us
    all_to_all x1, waiting for transfers between devices: 5.46 us -> 3.58 us  [on_device(): got = lax.all_to_all(sent, ('c', 'zh', 'zl'), 0, 0, tiled=True)]
where the time goes in v5:
time: 49.8 us; the launch traced here: 49.4 us
  starting transfers between devices  30.8 us (62%)
  waiting for transfers between devices  9.4 us (19%)
  Pallas kernels  8.16 us (16%)
  between operations  0.8 us (2%)
    ppermute x1, starting transfers between devices, on_device(): far = lax.ppermute(wide, 'zh', swap)[16:].reshape(kd, width, norb)  7.83 us
    pallas_call x7, Pallas kernels, call(): pl.pallas_call(kernel, out_shape=outs, in_specs=specs, out_specs=out_spec...  7.08 us
    all_to_all x1, starting transfers between devices, on_device(): got = lax.all_to_all(sent, ('c', 'zh', 'zl'), 0, 0, tiled=True)  6.63 us
    ppermute x2, starting transfers between devices, exchange(): return (near, lax.ppermute(x, 'y', [(i, i ^ 2) for i in range(4)]))  5.87 us
    all_to_all x1, starting transfers between devices, on_device(): lax.all_to_all(dense.reshape(16, -1, norb), ('x', 'y'), 0, 0, tiled=True)  5.62 us
    all_to_all x1, waiting for transfers between devices, on_device(): lax.all_to_all(dense.reshape(16, -1, norb), ('x', 'y'), 0, 0, tiled=True)  4.22 us
    ppermute x1, starting transfers between devices, on_device(): lax.ppermute(to_chip, ('zl', 'c'), meet + [(j, i) for i, j in meet])  4.04 us
    all_to_all x1, waiting for transfers between devices, on_device(): got = lax.all_to_all(sent, ('c', 'zh', 'zl'), 0, 0, tiled=True)  3.58 us
  transfers between devices with their start and end apart: 10, of which 4 were waited for; matrix products, arithmetic and copies ran while one was open for 0% of the time, Pallas kernels for 10%

profile of v5, /device:TPU:1, one launch (start us, length us, event | category | flops | bytes accessed | tf_op | source)
XLA Modules:
  0.0 49.4 jit_solution(7560509288007533295)
XLA Ops:
  0.6 1.1 %begin.1 = (bf16[2,128,256]{2,1,0:T(8,128)(2,1)S(1)}, bf16[272,256]{1,0:T(8,128)(2,1)S(1)}, s32[2,4]{1,0:T(2,128)S(1)}, s32[2,4]{1,0:T(2,128)S(1)}, f32[8,128]{1...) custom-call(bf16[2,2,128,256]{3,2,1,0:T(8,128)(2,1)} %green.7, s32[2,4]{1,0:T(2,128)} %bitcast.27, ...), custom_call_target="tpu_custom_call" | custom-call | bytes 262144 | tf_op jit(solution)/shard_map/begin/pallas_call | solution.py:94
  1.7 7.8 %collective-permute-start = (bf16[272,256]{1,0:T(8,128)(2,1)S(1)}, bf16[272,256]{1,0:T(8,128)(2,1)S(1)}, u32[]{:S(2)}, u32[]{:S(2)}) collective-permute-start(bf16[272,256]{1,0:T(8,128)(2,1)S(1)} %get-tuple-element.25), channel_id=1, source_target_pairs={{0,8},{8,0},{1,9},{9,1},{2,10},{10,2},{3,11},{11,3},{4,12},{12,4},... | collective-permute-start | bytes 417800 | tf_op jit(solution)/shard_map/ppermute | solution.py:283
  9.6 0.1 bitcast_multiply_fusion
  9.7 3.0 %collective-permute-start.2 = (bf16[2,128,256]{2,1,0:T(8,128)(2,1)S(1)}, bf16[2,128,256]{2,1,0:T(8,128)(2,1)S(1)}, u32[]{:S(2)}, u32[]{:S(2)}) collective-permute-start(bf16[2,128,256]{2,1,0:T(8,128)(2,1)S(1)} %get-tuple-element.28), channel_id=1, source_target_pairs={{0,32},{16,48},{32,0},{48,16},{1,33},{17,49},{33,1},{49,17},{2,34}... | collective-permute-start | bytes 393224 | tf_op jit(solution)/shard_map/ppermute | solution.py:281
  12.7 0.4 collective-permute-start.1
  13.1 4.0 %collective-permute-start.4 = (bf16[6,16,256]{2,1,0:T(8,128)(2,1)S(1)}, bf16[6,16,256]{2,1,0:T(8,128)(2,1)S(1)}, u32[]{:S(2)}, u32[]{:S(2)}) collective-permute-start(bf16[6,16,256]{2,1,0:T(8,128)(2,1)S(1)} %get-tuple-element.41), channel_id=1, source_target_pairs={{1,2},{3,4},{5,6},{2,1},{4,3},{6,5},{9,10},{11,12},{13,14},{10,9},... | collective-permute-start | bytes 147464 | tf_op jit(solution)/shard_map/ppermute | solution.py:294
  17.1 0.1 collective-permute-start.3
  17.2 0.1 add_bitcast_fusion.place
  17.3 0.3 shift.1
  17.6 0.8 %collective-permute-done.3.from_core = bf16[6,16,256]{2,1,0:T(8,128)(2,1)S(1)} collective-permute-done((bf16[6,16,256]{2,1,0:T(8,128)(2,1)S(1)}, bf16[6,16,256]{2,1,0:T(8,128)(2,1)S(1)}, u32[]{:S(2)}, u32[]{:S(2)}) %collective-permute-start.3) | collective-permute-done | bytes 49184 | tf_op jit(solution)/shard_map/ppermute | solution.py:291
  18.4 0.7 %collective-permute-done.4.from_chip = bf16[6,16,256]{2,1,0:T(8,128)(2,1)S(1)} collective-permute-done((bf16[6,16,256]{2,1,0:T(8,128)(2,1)S(1)}, bf16[6,16,256]{2,1,0:T(8,128)(2,1)S(1)}, u32[]{:S(2)}, u32[]{:S(2)}) %collective-permute-start.4) | collective-permute-done | bytes 49184 | tf_op jit(solution)/shard_map/ppermute | solution.py:294
  19.2 0.3 halo.1
  19.5 1.3 %terms.1 = bf16[512,256]{1,0:T(8,128)(2,1)} custom-call(s32[2,4]{1,0:T(2,128)S(1)} %get-tuple-element.20.order, bf16[2,128,256]{2,1,0:T(8,128)(2,1)S(1)} %bitcast.21, bf16[2,128,256]{2,1,0:T(8,128)(2,1)S(1)} %collective-permute-done.1.near.great2, bf16[2,128,256]{2,1,0:T(8,128)(2,1)S(1)} %collective-permute-done.2.next_near.great3, ...), custom_call_target="tpu_custom_call" | custom-call | flops 1048576 | bytes 1048576 | tf_op jit(solution)/shard_map/terms/pallas_call | solution.py:57
  20.9 5.6 %all-to-all-start = ((bf16[16,32,256]{2,1,0:T(8,128)(2,1)}), bf16[16,32,256]{2,1,0:T(8,128)(2,1)S(1)}, u32[]{:S(2)}, u32[]{:S(2)}) async-start(bf16[16,32,256]{2,1,0:T(8,128)(2,1)} %bitcast.15), calls=%async_computation | async-start | bytes 524288 | tf_op jit(solution)/shard_map/all_to_all | solution.py:327
  26.5 0.1 collective-permute-start.5
  26.6 2.9 %collective-permute-start.7 = (bf16[2,144,256]{2,1,0:T(8,128)(2,1)S(1)}, bf16[2,144,256]{2,1,0:T(8,128)(2,1)S(1)}, u32[]{:S(2)}, u32[]{:S(2)}) collective-permute-start(bf16[2,144,256]{2,1,0:T(8,128)(2,1)S(1)} %get-tuple-element.36.own), channel_id=1, source_target_pairs={{0,32},{16,48},{32,0},{48,16},{1,33},{17,49},{33,1},{49,17},{2,34}... | collective-permute-start | bytes 442376 | tf_op jit(solution)/shard_map/ppermute | solution.py:281
  29.5 0.3 collective-permute-start.6
  29.7 4.2 %all-to-all-done.got = bf16[16,32,256]{2,1,0:T(8,128)(2,1)S(1)} async-done(((bf16[16,32,256]{2,1,0:T(8,128)(2,1)}), bf16[16,32,256]{2,1,0:T(8,128)(2,1)S(1)}, u32[]{:S(2)}, u32[]{:S(2)}) %all-to-all-start) | async-done | bytes 262176 | tf_op jit(solution)/shard_map/all_to_all | solution.py:327
  34.0 0.7 %column.1 = bf16[16,16,256]{2,1,0:T(8,128)(2,1)} custom-call(bf16[16,32,256]{2,1,0:T(8,128)(2,1)S(1)} %all-to-all-done.got), custom_call_target="tpu_custom_call" | custom-call | flops 1048576 | bytes 1048576 | tf_op jit(solution)/shard_map/column/pallas_call | solution.py:57
  34.7 6.6 %all-to-all-start.1 = ((bf16[16,16,256]{2,1,0:T(8,128)(2,1)}), bf16[16,16,256]{2,1,0:T(8,128)(2,1)S(1)}, u32[]{:S(2)}, u32[]{:S(2)}) async-start(bf16[16,16,256]{2,1,0:T(8,128)(2,1)} %column.1), calls=%async_computation.1 | async-start | bytes 262144 | tf_op jit(solution)/shard_map/all_to_all | solution.py:331
  41.3 2.0 %weights.1 = (bf16[4,128,576]{2,1,0:T(8,128)(2,1)S(1)}, f32[32,16]{1,0:T(8,128)S(1)}) custom-call(s32[2,4]{1,0:T(2,128)S(1)} %get-tuple-element.21.q_row, s32[1,2]{1,0:T(1,128)S(1)} %add_bitcast_fusion.place, s32[1,8]{1,0:T(1,128)S(1)} %get-tuple-element.22.offsets, f32[1,8]{1,0:T(1,128)S(1)} %get-tuple-element.23.occupancy, ...), custom_call_target="tpu_custom_call" | custom-call | flops 1048576 | bytes 1048576 | tf_op jit(solution)/shard_map/weights/pallas_call | solution.py:57
  43.4 1.6 %sigma.1 = bf16[2,2,128,256]{3,2,1,0:T(8,128)(2,1)} custom-call(s32[2,4]{1,0:T(2,128)S(1)} %get-tuple-element.20.order, bf16[4,128,576]{2,1,0:T(8,128)(2,1)S(1)} %get-tuple-element.34.main, bf16[2,2,128,256]{3,2,1,0:T(8,128)(2,1)S(1)} %copy-done, bf16[2,144,256]{2,1,0:T(8,128)(2,1)S(1)} %get-tuple-element.36.own, ...), custom_call_target="tpu_custom_call" | custom-call | flops 17179869184 | bytes 1048576 | tf_op jit(solution)/shard_map/sigma/pallas_call | solution.py:57
  45.0 3.6 %all-to-all-done.1.got = bf16[16,16,256]{2,1,0:T(8,128)(2,1)S(1)} async-done(((bf16[16,16,256]{2,1,0:T(8,128)(2,1)}), bf16[16,16,256]{2,1,0:T(8,128)(2,1)S(1)}, u32[]{:S(2)}, u32[]{:S(2)}) %all-to-all-start.1) | async-done | bytes 131104 | tf_op jit(solution)/shard_map/all_to_all | solution.py:331
  48.6 0.8 %owner.1 = f32[32,256]{1,0:T(8,128)} custom-call(bf16[16,16,256]{2,1,0:T(8,128)(2,1)S(1)} %all-to-all-done.1.got, f32[32,16]{1,0:T(8,128)S(1)} %get-tuple-element.37.owner), custom_call_target="tpu_custom_call" | custom-call | flops 1048576 | bytes 1048576 | tf_op jit(solution)/shard_map/owner/pallas_call | solution.py:57
  (13 shorter events, 0.1 us)
Async XLA Ops:
  0.6 8.9 %copy-start = (bf16[2,2,128,256]{3,2,1,0:T(8,128)(2,1)S(1)}, bf16[2,2,128,256]{3,2,1,0:T(8,128)(2,1)}, u32[]{:S(2)}) copy-start(bf16[2,2,128,256]{3,2,1,0:T(8,128)(2,1)} %green.7) | copy-start | bytes 786436
  1.7 17.7 %collective-permute-start = (bf16[272,256]{1,0:T(8,128)(2,1)S(1)}, bf16[272,256]{1,0:T(8,128)(2,1)S(1)}, u32[]{:S(2)}, u32[]{:S(2)}) collective-permute-start(bf16[272,256]{1,0:T(8,128)(2,1)S(1)} %get-tuple-element.25), channel_id=1, source_target_pairs={{0,8},{8,0},{1,9},{9,1},{2,10},{10,2},{3,11},{11,3},{4,12},{12,4},... | collective-permute-start | bytes 417800 | tf_op jit(solution)/shard_map/ppermute | solution.py:283
  9.7 9.8 %collective-permute-start.2 = (bf16[2,128,256]{2,1,0:T(8,128)(2,1)S(1)}, bf16[2,128,256]{2,1,0:T(8,128)(2,1)S(1)}, u32[]{:S(2)}, u32[]{:S(2)}) collective-permute-start(bf16[2,128,256]{2,1,0:T(8,128)(2,1)S(1)} %get-tuple-element.28), channel_id=1, source_target_pairs={{0,32},{16,48},{32,0},{48,16},{1,33},{17,49},{33,1},{49,17},{2,34}... | collective-permute-start | bytes 393224 | tf_op jit(solution)/shard_map/ppermute | solution.py:281
  12.7 6.8 %collective-permute-start.1 = (bf16[2,128,256]{2,1,0:T(8,128)(2,1)S(1)}, bf16[2,128,256]{2,1,0:T(8,128)(2,1)S(1)}, u32[]{:S(2)}, u32[]{:S(2)}) collective-permute-start(bf16[2,128,256]{2,1,0:T(8,128)(2,1)S(1)} %get-tuple-element.28), channel_id=1, source_target_pairs={{0,16},{16,0},{32,48},{48,32},{1,17},{17,1},{33,49},{49,33},{2,18}... | collective-permute-start | bytes 393224 | tf_op jit(solution)/shard_map/ppermute | solution.py:280
  13.1 6.1 %collective-permute-start.4 = (bf16[6,16,256]{2,1,0:T(8,128)(2,1)S(1)}, bf16[6,16,256]{2,1,0:T(8,128)(2,1)S(1)}, u32[]{:S(2)}, u32[]{:S(2)}) collective-permute-start(bf16[6,16,256]{2,1,0:T(8,128)(2,1)S(1)} %get-tuple-element.41), channel_id=1, source_target_pairs={{1,2},{3,4},{5,6},{2,1},{4,3},{6,5},{9,10},{11,12},{13,14},{10,9},... | collective-permute-start | bytes 147464 | tf_op jit(solution)/shard_map/ppermute | solution.py:294
  17.1 1.3 %collective-permute-start.3 = (bf16[6,16,256]{2,1,0:T(8,128)(2,1)S(1)}, bf16[6,16,256]{2,1,0:T(8,128)(2,1)S(1)}, u32[]{:S(2)}, u32[]{:S(2)}) collective-permute-start(bf16[6,16,256]{2,1,0:T(8,128)(2,1)S(1)} %get-tuple-element.40), channel_id=1, source_target_pairs={{0,1},{1,0},{2,3},{3,2},{4,5},{5,4},{6,7},{7,6},{8,9},{9,8},{10,11... | collective-permute-start | bytes 147464 | tf_op jit(solution)/shard_map/ppermute | solution.py:291
  20.9 13.1 %all-to-all-start = ((bf16[16,32,256]{2,1,0:T(8,128)(2,1)}), bf16[16,32,256]{2,1,0:T(8,128)(2,1)S(1)}, u32[]{:S(2)}, u32[]{:S(2)}) async-start(bf16[16,32,256]{2,1,0:T(8,128)(2,1)} %bitcast.15), calls=%async_computation | async-start | bytes 524288 | tf_op jit(solution)/shard_map/all_to_all | solution.py:327
  26.5 16.9 %collective-permute-start.5 = (bf16[2,144,256]{2,1,0:T(8,128)(2,1)S(1)}, bf16[2,144,256]{2,1,0:T(8,128)(2,1)S(1)}, u32[]{:S(2)}, u32[]{:S(2)}) collective-permute-start(bf16[2,144,256]{2,1,0:T(8,128)(2,1)S(1)} %get-tuple-element.36.own), channel_id=1, source_target_pairs={{0,8},{8,0},{1,9},{9,1},{2,10},{10,2},{3,11},{11,3},{4,12},{12,4},... | collective-permute-start | bytes 442376 | tf_op jit(solution)/shard_map/ppermute | solution.py:326
  26.6 16.8 %collective-permute-start.7 = (bf16[2,144,256]{2,1,0:T(8,128)(2,1)S(1)}, bf16[2,144,256]{2,1,0:T(8,128)(2,1)S(1)}, u32[]{:S(2)}, u32[]{:S(2)}) collective-permute-start(bf16[2,144,256]{2,1,0:T(8,128)(2,1)S(1)} %get-tuple-element.36.own), channel_id=1, source_target_pairs={{0,32},{16,48},{32,0},{48,16},{1,33},{17,49},{33,1},{49,17},{2,34}... | collective-permute-start | bytes 442376 | tf_op jit(solution)/shard_map/ppermute | solution.py:281
  29.5 13.9 %collective-permute-start.6 = (bf16[2,144,256]{2,1,0:T(8,128)(2,1)S(1)}, bf16[2,144,256]{2,1,0:T(8,128)(2,1)S(1)}, u32[]{:S(2)}, u32[]{:S(2)}) collective-permute-start(bf16[2,144,256]{2,1,0:T(8,128)(2,1)S(1)} %get-tuple-element.36.own), channel_id=1, source_target_pairs={{0,16},{16,0},{32,48},{48,32},{1,17},{17,1},{33,49},{49,33},{2,18}... | collective-permute-start | bytes 442376 | tf_op jit(solution)/shard_map/ppermute | solution.py:280
  34.7 13.9 %all-to-all-start.1 = ((bf16[16,16,256]{2,1,0:T(8,128)(2,1)}), bf16[16,16,256]{2,1,0:T(8,128)(2,1)S(1)}, u32[]{:S(2)}, u32[]{:S(2)}) async-start(bf16[16,16,256]{2,1,0:T(8,128)(2,1)} %column.1), calls=%async_computation.1 | async-start | bytes 262144 | tf_op jit(solution)/shard_map/all_to_all | solution.py:331

commit v6 on v5

--- a/solution.py
+++ b/solution.py
@@ -49,7 +49,7 @@
 
 
 def choose(blocks, index):
-    low, high = blocks[0].astype(F32), blocks[1].astype(F32)
+    low, high = blocks[0][...].astype(F32), blocks[1][...].astype(F32)
     return jnp.where(jnp.broadcast_to(index, low.shape) == 0, low, high)
 
 
@@ -71,14 +71,11 @@
 
 
 def begin_kernel(green, *refs):
-    count = (len(refs) - 3) // 2
-    small, great, wide, kept, sems = refs[:count], refs[count], refs[count + 1], refs[count + 2 : -1], refs[-1]
+    count = (len(refs) - 2) // 2
+    small, great, kept, sems = refs[:count], refs[count], refs[count + 1 : -1], refs[-1]
     pairs = list(zip(small, kept))
-    kd, width, _ = great.shape
-    pairs.append((green.at[0, 0, pl.ds(0, 16)], wide.at[pl.ds(0, 16)]))
-    for k in range(kd):
+    for k in range(great.shape[0]):
         pairs.append((green.at[1, k], great.at[k]))
-        pairs.append((green.at[1, k], wide.at[pl.ds(16 + k * width, width)]))
     copies = [pltpu.make_async_copy(a, b, sems.at[i]) for i, (a, b) in enumerate(pairs)]
     for copy in reversed(copies):
         copy.start()
@@ -89,14 +86,14 @@
 def begin(green, *small):
     anywhere = pl.BlockSpec(memory_space=pltpu.HBM)
     _, kd, width, norb = green.shape
-    outs = [shape(kd, width, norb), shape(16 + kd * width, norb)] + [shape(*x.shape, dtype=x.dtype) for x in small]
+    outs = [shape(kd, width, norb)] + [shape(*x.shape, dtype=x.dtype) for x in small]
     green, *small = [pltpu.with_memory_space_constraint(x, pltpu.HBM) for x in (green, *small)]
     return pl.pallas_call(
         begin_kernel,
         out_shape=outs,
         in_specs=[anywhere] * (1 + len(small)),
         out_specs=[VMEM] * len(outs),
-        scratch_shapes=[pltpu.SemaphoreType.DMA((len(small) + 2 * kd + 1,))],
+        scratch_shapes=[pltpu.SemaphoreType.DMA((len(small) + kd,))],
         compiler_params=pltpu.CompilerParams(vmem_limit_bytes=BEGIN_LIMIT),
         cost_estimate=pl.CostEstimate(flops=0, bytes_accessed=2**18, transcendentals=0),
         name="begin",
@@ -126,30 +123,34 @@
     core, chip = from_core[...].astype(F32), from_chip[...].astype(F32)
     before = jnp.where(first_core, chip, core).astype(BF16)
     after = jnp.where(first_core, core, chip).astype(BF16)
-    rows, cols = iota((16, 16), 0), iota((16, 16), 1)
-    row, col = iota((16, 64), 0), iota((16, 64), 1)
+    size = before.shape[0] * before.shape[1]
+    before, after = before.reshape(size, -1), after.reshape(size, -1)
+    both = jnp.concatenate([before, after], axis=0)
+    rows, cols = iota((16, size), 0), iota((16, size), 1)
+    row, col = iota((16, 2 * size), 0), iota((16, 2 * size), 1)
     kind = row // HALO
-    pick = (col == kind * 16 + (1 - kind % 2) * (16 - HALO) + row % HALO).astype(F32).astype(BF16)
+    source = kind // 2 * 8 * kd + kind % 2 * size + (1 - kind % 2) * (8 - HALO) + row % HALO
     for k in range(kd):
         for d in range(1, HALO + 1):
             at = k * HALO + d - 1
-            wrap = (cols + 16 == rows + d).astype(F32).astype(BF16)
-            moved = dot(wrap, after[2 * kd + k])
+            wrap = (rows + d >= 16) & (cols == rows + d - 16 + (2 * kd + k) * 8)
+            moved = dot(wrap.astype(F32).astype(BF16), after)
             full[at, : width - 16] = shifted[at, : width - 16]
             full[at, width - 16 :] = (shifted[at, width - 16 :].astype(F32) + moved).astype(BF16)
-        ends = [before[k], after[k], before[kd + k], after[kd + k]]
         extended[k, :width] = green[0, k]
-        extended[k, width:] = dot(pick, jnp.concatenate(ends, axis=0)).astype(BF16)
+        pick = (col == source + 8 * k).astype(F32).astype(BF16)
+        extended[k, width:] = dot(pick, both).astype(BF16)
     lines = []
     for k in range(kd):
-        lines += pair_products(choose(green[1], entry(order, k, 0)), full, k)
+        lines += pair_products(choose(green.at[1], entry(order, k, 0)), full, k)
     first[...] = jnp.concatenate(lines, axis=0)
 
 
-def terms_kernel(order, far, near, next_near, shifted, first, onehot, out, held, sems):
+def terms_kernel(order, far0, far1, near, next_near, shifted, first, onehot, out, held, sems):
     lines = [first[...]]
+    far = (far0, far1)
     for r, ref in ((1, far), (2, near), (3, next_near)):
-        for k in range(far.shape[0]):
+        for k in range(len(far)):
             lines += pair_products(choose(ref, entry(order, k, r)), shifted, k)
     terms = jnp.concatenate(lines, axis=0).astype(BF16)
     step = out.shape[0] // PIECES
@@ -230,7 +231,7 @@
             main[ck, :, rounds * width :] = jnp.concatenate(ends, axis=1).astype(BF16)
 
 
-def sigma_kernel(order, main, green, own, less1, less2, less3, great1, great2, great3, sigma):
+def sigma_kernel(order, main, green, own, less1, less2, less3, far0, far1, great2, great3, sigma):
     kd, rounds = order.shape
     width = green.shape[2]
     less = (own, less1, less2, less3)
@@ -242,7 +243,8 @@
                 blocks = [x[i, :width] for x, i in zip(less, index)]
             else:
                 blocks = [green[1, index[0]]]
-                blocks += [x[i] for x, i in zip((great1, great2, great3), index[1:])]
+                blocks.append(jnp.where(index[1] == 0, far0[...].astype(F32), far1[...].astype(F32)).astype(BF16))
+                blocks += [x[i] for x, i in zip((great2, great3), index[2:])]
             weights = main[comp * kd + k]
             acc = dot(weights[:, : rounds * width], jnp.concatenate(blocks, axis=0))
             sigma[comp, k] = (acc + dot(weights[:, rounds * width :], ends)).astype(BF16)
@@ -262,7 +264,7 @@
     rounds = pair_order.shape[0]
     count = lax.axis_size(("zl", "c"))
     owned = coupling.shape[0] // lax.axis_size(("x", "y", "zh"))
-    mine, wide, order, q_row, spread, mask_row, offset_row, occupancy_row = begin(
+    mine, order, q_row, spread, mask_row, offset_row, occupancy_row = begin(
         green,
         pair_order[:, 0].T,
         q_index.T,
@@ -280,19 +282,20 @@
         near = lax.ppermute(x, "y", [(i, i ^ 1) for i in range(4)])
         return near, lax.ppermute(x, "y", [(i, i ^ 2) for i in range(4)])
 
-    far = lax.ppermute(wide, "zh", swap)[16:].reshape(kd, width, norb)
-    first, last = green[:, :, :16], green[:, :, width - 16 :]
-    masked = first[0] * mask_row[0, None, :16, None].astype(BF16)
+    far = lax.ppermute(mine, "zh", swap)
+    far = [far[k] for k in range(kd)]
+    first, last = green[:, :, :8], green[:, :, width - 8 :]
+    masked = first[0] * mask_row[0, None, :8, None].astype(BF16)
     first_core = lax.axis_index("c") == 0
 
     def edge(x):
-        return jnp.concatenate([x.reshape(2 * kd, 16, norb), masked], axis=0)
+        rows = jnp.concatenate([x.reshape(2 * kd, 8, norb), masked], axis=0)
+        return rows.reshape(-1, 16, norb)
 
     from_core = lax.ppermute(edge(jnp.where(first_core, last, first)), "c", swap)
     meet = [(i, i + 1) for i in range(1, count - 1, 2)]
     to_chip = edge(jnp.where(first_core, first, last))
     from_chip = lax.ppermute(to_chip, ("zl", "c"), meet + [(j, i) for i, j in meet])
-    great = (far, *exchange(tie(mine, to_chip)))
     onehot, shifted = call(
         shift_kernel,
         "shift",
@@ -303,6 +306,7 @@
         [VMEM] * 3,
         (q_row, mask_row, green),
     )
+    great = (*far, *exchange(tie(mine, onehot)))
     shifted, first, extended = call(
         halo_kernel,
         "halo",
@@ -318,7 +322,7 @@
         terms_kernel,
         "terms",
         shape(onehot.shape[0], norb),
-        [VMEM] * 7,
+        [VMEM] * 8,
         (order, *great, shifted, first, onehot),
         scratch=[pltpu.VMEM((onehot.shape[0], norb), BF16), pltpu.SemaphoreType.DMA((PIECES,))],
         out_specs=pl.BlockSpec(memory_space=pl.ANY),
@@ -344,7 +348,7 @@
         sigma_kernel,
         "sigma",
         shape(*green.shape),
-        [SMEM] + [VMEM] * 9,
+        [SMEM] + [VMEM] * 10,
         (order, main, green, extended, *less, *great),
         flops=2**34,
     )

time: 49.8 us -> 49.3 us (0.990)
  starting transfers between devices: 30.8 us -> 29.2 us
  waiting for transfers between devices: 9.4 us -> 10.7 us
    ppermute x1, waiting for transfers between devices: 0.74 us -> 2.55 us  [on_device(): lax.ppermute(to_chip, ('zl', 'c'), meet + [(j, i) for i, j in meet])]
    ppermute x1, starting transfers between devices: 4.04 us -> 2.55 us  [on_device(): lax.ppermute(to_chip, ('zl', 'c'), meet + [(j, i) for i, j in meet])]
    ppermute x1, starting transfers between devices: 0.09 us -> 1.56 us  [on_device(): lax.ppermute(edge(jnp.where(first_core, last, first)), 'c', swap)]
    all_to_all x1, starting transfers between devices: 6.63 us -> 5.22 us  [on_device(): got = lax.all_to_all(sent, ('c', 'zh', 'zl'), 0, 0, tiled=True)]
    ppermute x1, waiting for transfers between devices: 0.84 us -> 0.01 us  [on_device(): lax.ppermute(edge(jnp.where(first_core, last, first)), 'c', swap)]
  transfers between devices with their start and end apart: 10 -> 10, of which waited for: 4 -> 3; matrix products, arithmetic and copies ran while one was open for 0% -> 0% of each run, Pallas kernels for 10% -> 10%
where the time goes in v6:
time: 49.3 us; the launch traced here: 49 us
  starting transfers between devices  29.2 us (59%)
  waiting for transfers between devices  10.7 us (22%)
  Pallas kernels  8.05 us (16%)
  between operations  0.78 us (2%)
    ppermute x1, starting transfers between devices, on_device(): far = lax.ppermute(mine, 'zh', swap)  7.83 us
    pallas_call x7, Pallas kernels, call(): pl.pallas_call(kernel, out_shape=outs, in_specs=specs, out_specs=out_spec...  7.06 us
    ppermute x2, starting transfers between devices, exchange(): return (near, lax.ppermute(x, 'y', [(i, i ^ 2) for i in range(4)]))  5.87 us
    all_to_all x1, starting transfers between devices, on_device(): lax.all_to_all(dense.reshape(16, -1, norb), ('x', 'y'), 0, 0, tiled=True)  5.42 us
    all_to_all x1, starting transfers between devices, on_device(): got = lax.all_to_all(sent, ('c', 'zh', 'zl'), 0, 0, tiled=True)  5.22 us
    all_to_all x1, waiting for transfers between devices, on_device(): lax.all_to_all(dense.reshape(16, -1, norb), ('x', 'y'), 0, 0, tiled=True)  4.58 us
    all_to_all x1, waiting for transfers between devices, on_device(): got = lax.all_to_all(sent, ('c', 'zh', 'zl'), 0, 0, tiled=True)  3.59 us
    ppermute x1, waiting for transfers between devices, on_device(): lax.ppermute(to_chip, ('zl', 'c'), meet + [(j, i) for i, j in meet])  2.55 us
  transfers between devices with their start and end apart: 10, of which 3 were waited for; matrix products, arithmetic and copies ran while one was open for 0% of the time, Pallas kernels for 10%

profile of v6, /device:TPU:1, one launch (start us, length us, event | category | flops | bytes accessed | tf_op | source)
XLA Modules:
  0.0 49.0 jit_solution(6421180527723623658)
XLA Ops:
  0.6 1.0 %begin.1 = (bf16[2,128,256]{2,1,0:T(8,128)(2,1)S(1)}, s32[2,4]{1,0:T(2,128)S(1)}, s32[2,4]{1,0:T(2,128)S(1)}, f32[8,128]{1,0:T(8,128)S(1)}, s32[1,128]{1,0:T(1,1...) custom-call(bf16[2,2,128,256]{3,2,1,0:T(8,128)(2,1)} %green.7, s32[2,4]{1,0:T(2,128)} %bitcast.32, s32[2,4]{1,0:T(2,128)} %bitcast.33, ...), custom_call_target="tpu_custom_call" | custom-call | bytes 262144 | tf_op jit(solution)/shard_map/begin/pallas_call | solution.py:91
  1.6 7.8 %collective-permute-start = (bf16[2,128,256]{2,1,0:T(8,128)(2,1)S(1)}, bf16[2,128,256]{2,1,0:T(8,128)(2,1)S(1)}, u32[]{:S(2)}, u32[]{:S(2)}) collective-permute-start(bf16[2,128,256]{2,1,0:T(8,128)(2,1)S(1)} %get-tuple-element.27), channel_id=1, source_target_pairs={{0,8},{8,0},{1,9},{9,1},{2,10},{10,2},{3,11},{11,3},{4,12},{12,4},... | collective-permute-start | bytes 393224 | tf_op jit(solution)/shard_map/ppermute | solution.py:285
  9.5 0.3 shift.1
  9.8 3.0 %collective-permute-start.2 = (bf16[2,128,256]{2,1,0:T(8,128)(2,1)S(1)}, bf16[2,128,256]{2,1,0:T(8,128)(2,1)S(1)}, u32[]{:S(2)}, u32[]{:S(2)}) collective-permute-start(bf16[2,128,256]{2,1,0:T(8,128)(2,1)S(1)} %get-tuple-element.27), channel_id=1, source_target_pairs={{0,32},{16,48},{32,0},{48,16},{1,33},{17,49},{33,1},{49,17},{2,34}... | collective-permute-start | bytes 393224 | tf_op jit(solution)/shard_map/ppermute | solution.py:283
  12.8 0.4 collective-permute-start.1
  13.2 0.1 bitcast_multiply_fusion
  13.3 1.6 %collective-permute-start.3 = (bf16[3,16,256]{2,1,0:T(8,128)(2,1)S(1)}, bf16[3,16,256]{2,1,0:T(8,128)(2,1)S(1)}, u32[]{:S(2)}, u32[]{:S(2)}) collective-permute-start(bf16[3,16,256]{2,1,0:T(8,128)(2,1)S(1)} %bitcast.30), channel_id=1, source_target_pairs={{0,1},{1,0},{2,3},{3,2},{4,5},{5,4},{6,7},{7,6},{8,9},{9,8},{10,11... | collective-permute-start | bytes 73736 | tf_op jit(solution)/shard_map/ppermute | solution.py:295
  14.8 2.5 %collective-permute-start.4 = (bf16[3,16,256]{2,1,0:T(8,128)(2,1)S(1)}, bf16[3,16,256]{2,1,0:T(8,128)(2,1)S(1)}, u32[]{:S(2)}, u32[]{:S(2)}) collective-permute-start(bf16[3,16,256]{2,1,0:T(8,128)(2,1)S(1)} %bitcast.29), channel_id=1, source_target_pairs={{1,2},{3,4},{5,6},{2,1},{4,3},{6,5},{9,10},{11,12},{13,14},{10,9},... | collective-permute-start | bytes 73736 | tf_op jit(solution)/shard_map/ppermute | solution.py:298
  17.4 0.1 add_bitcast_fusion.place
  17.5 0.0 collective-permute-done.3.from_core
  17.5 2.6 %collective-permute-done.4.from_chip = bf16[3,16,256]{2,1,0:T(8,128)(2,1)S(1)} collective-permute-done((bf16[3,16,256]{2,1,0:T(8,128)(2,1)S(1)}, bf16[3,16,256]{2,1,0:T(8,128)(2,1)S(1)}, u32[]{:S(2)}, u32[]{:S(2)}) %collective-permute-start.4) | collective-permute-done | bytes 24608 | tf_op jit(solution)/shard_map/ppermute | solution.py:298
  20.0 0.3 halo.1
  20.4 1.3 %terms.1 = bf16[512,256]{1,0:T(8,128)(2,1)} custom-call(s32[2,4]{1,0:T(2,128)S(1)} %get-tuple-element.19.order, bf16[128,256]{1,0:T(8,128)(2,1)S(1)} %get-tuple-element.39.far0, bf16[128,256]{1,0:T(8,128)(2,1)S(1)} %get-tuple-element.38.far1, bf16[2,128,256]{2,1,0:T(8,128)(2,1)S(1)} %collective-permute-done.1.near.great2, ...), custom_call_target="tpu_custom_call" | custom-call | flops 1048576 | bytes 1048576 | tf_op jit(solution)/shard_map/terms/pallas_call | solution.py:57
  21.7 5.4 %all-to-all-start = ((bf16[16,32,256]{2,1,0:T(8,128)(2,1)}), bf16[16,32,256]{2,1,0:T(8,128)(2,1)S(1)}, u32[]{:S(2)}, u32[]{:S(2)}) async-start(bf16[16,32,256]{2,1,0:T(8,128)(2,1)} %bitcast.18), calls=%async_computation | async-start | bytes 524288 | tf_op jit(solution)/shard_map/all_to_all | solution.py:331
  27.1 0.1 collective-permute-start.5
  27.2 2.9 %collective-permute-start.7 = (bf16[2,144,256]{2,1,0:T(8,128)(2,1)S(1)}, bf16[2,144,256]{2,1,0:T(8,128)(2,1)S(1)}, u32[]{:S(2)}, u32[]{:S(2)}) collective-permute-start(bf16[2,144,256]{2,1,0:T(8,128)(2,1)S(1)} %get-tuple-element.34.own), channel_id=1, source_target_pairs={{0,32},{16,48},{32,0},{48,16},{1,33},{17,49},{33,1},{49,17},{2,34}... | collective-permute-start | bytes 442376 | tf_op jit(solution)/shard_map/ppermute | solution.py:283
  30.1 0.3 collective-permute-start.6
  30.4 4.6 %all-to-all-done.got = bf16[16,32,256]{2,1,0:T(8,128)(2,1)S(1)} async-done(((bf16[16,32,256]{2,1,0:T(8,128)(2,1)}), bf16[16,32,256]{2,1,0:T(8,128)(2,1)S(1)}, u32[]{:S(2)}, u32[]{:S(2)}) %all-to-all-start) | async-done | bytes 262176 | tf_op jit(solution)/shard_map/all_to_all | solution.py:331
  35.0 0.7 %column.1 = bf16[16,16,256]{2,1,0:T(8,128)(2,1)} custom-call(bf16[16,32,256]{2,1,0:T(8,128)(2,1)S(1)} %all-to-all-done.got), custom_call_target="tpu_custom_call" | custom-call | flops 1048576 | bytes 1048576 | tf_op jit(solution)/shard_map/column/pallas_call | solution.py:57
  35.6 5.2 %all-to-all-start.1 = ((bf16[16,16,256]{2,1,0:T(8,128)(2,1)}), bf16[16,16,256]{2,1,0:T(8,128)(2,1)S(1)}, u32[]{:S(2)}, u32[]{:S(2)}) async-start(bf16[16,16,256]{2,1,0:T(8,128)(2,1)} %column.1), calls=%async_computation.1 | async-start | bytes 262144 | tf_op jit(solution)/shard_map/all_to_all | solution.py:335
  40.9 2.0 %weights.1 = (bf16[4,128,576]{2,1,0:T(8,128)(2,1)S(1)}, f32[32,16]{1,0:T(8,128)S(1)}) custom-call(s32[2,4]{1,0:T(2,128)S(1)} %get-tuple-element.20.q_row, s32[1,2]{1,0:T(1,128)S(1)} %add_bitcast_fusion.place, s32[1,8]{1,0:T(1,128)S(1)} %get-tuple-element.21.offsets, f32[1,8]{1,0:T(1,128)S(1)} %get-tuple-element.22.occupancy, ...), custom_call_target="tpu_custom_call" | custom-call | flops 1048576 | bytes 1048576 | tf_op jit(solution)/shard_map/weights/pallas_call | solution.py:57
  43.0 1.6 %sigma.1 = bf16[2,2,128,256]{3,2,1,0:T(8,128)(2,1)} custom-call(s32[2,4]{1,0:T(2,128)S(1)} %get-tuple-element.19.order, bf16[4,128,576]{2,1,0:T(8,128)(2,1)S(1)} %get-tuple-element.32.main, bf16[2,2,128,256]{3,2,1,0:T(8,128)(2,1)S(1)} %copy-done, bf16[2,144,256]{2,1,0:T(8,128)(2,1)S(1)} %get-tuple-element.34.own, ...), custom_call_target="tpu_custom_call" | custom-call | flops 17179869184 | bytes 1048576 | tf_op jit(solution)/shard_map/sigma/pallas_call | solution.py:57
  44.6 3.6 %all-to-all-done.1.got = bf16[16,16,256]{2,1,0:T(8,128)(2,1)S(1)} async-done(((bf16[16,16,256]{2,1,0:T(8,128)(2,1)}), bf16[16,16,256]{2,1,0:T(8,128)(2,1)S(1)}, u32[]{:S(2)}, u32[]{:S(2)}) %all-to-all-start.1) | async-done | bytes 131104 | tf_op jit(solution)/shard_map/all_to_all | solution.py:335
  48.2 0.8 %owner.1 = f32[32,256]{1,0:T(8,128)} custom-call(bf16[16,16,256]{2,1,0:T(8,128)(2,1)S(1)} %all-to-all-done.1.got, f32[32,16]{1,0:T(8,128)S(1)} %get-tuple-element.35.owner), custom_call_target="tpu_custom_call" | custom-call | flops 1048576 | bytes 1048576 | tf_op jit(solution)/shard_map/owner/pallas_call | solution.py:57
  (13 shorter events, 0.1 us)
Async XLA Ops:
  0.6 8.8 %copy-start = (bf16[2,2,128,256]{3,2,1,0:T(8,128)(2,1)S(1)}, bf16[2,2,128,256]{3,2,1,0:T(8,128)(2,1)}, u32[]{:S(2)}) copy-start(bf16[2,2,128,256]{3,2,1,0:T(8,128)(2,1)} %green.7) | copy-start | bytes 786436
  1.6 18.7 %collective-permute-start = (bf16[2,128,256]{2,1,0:T(8,128)(2,1)S(1)}, bf16[2,128,256]{2,1,0:T(8,128)(2,1)S(1)}, u32[]{:S(2)}, u32[]{:S(2)}) collective-permute-start(bf16[2,128,256]{2,1,0:T(8,128)(2,1)S(1)} %get-tuple-element.27), channel_id=1, source_target_pairs={{0,8},{8,0},{1,9},{9,1},{2,10},{10,2},{3,11},{11,3},{4,12},{12,4},... | collective-permute-start | bytes 393224 | tf_op jit(solution)/shard_map/ppermute | solution.py:285
  9.8 10.6 %collective-permute-start.2 = (bf16[2,128,256]{2,1,0:T(8,128)(2,1)S(1)}, bf16[2,128,256]{2,1,0:T(8,128)(2,1)S(1)}, u32[]{:S(2)}, u32[]{:S(2)}) collective-permute-start(bf16[2,128,256]{2,1,0:T(8,128)(2,1)S(1)} %get-tuple-element.27), channel_id=1, source_target_pairs={{0,32},{16,48},{32,0},{48,16},{1,33},{17,49},{33,1},{49,17},{2,34}... | collective-permute-start | bytes 393224 | tf_op jit(solution)/shard_map/ppermute | solution.py:283
  12.8 7.6 %collective-permute-start.1 = (bf16[2,128,256]{2,1,0:T(8,128)(2,1)S(1)}, bf16[2,128,256]{2,1,0:T(8,128)(2,1)S(1)}, u32[]{:S(2)}, u32[]{:S(2)}) collective-permute-start(bf16[2,128,256]{2,1,0:T(8,128)(2,1)S(1)} %get-tuple-element.27), channel_id=1, source_target_pairs={{0,16},{16,0},{32,48},{48,32},{1,17},{17,1},{33,49},{49,33},{2,18}... | collective-permute-start | bytes 393224 | tf_op jit(solution)/shard_map/ppermute | solution.py:282
  13.3 4.2 %collective-permute-start.3 = (bf16[3,16,256]{2,1,0:T(8,128)(2,1)S(1)}, bf16[3,16,256]{2,1,0:T(8,128)(2,1)S(1)}, u32[]{:S(2)}, u32[]{:S(2)}) collective-permute-start(bf16[3,16,256]{2,1,0:T(8,128)(2,1)S(1)} %bitcast.30), channel_id=1, source_target_pairs={{0,1},{1,0},{2,3},{3,2},{4,5},{5,4},{6,7},{7,6},{8,9},{9,8},{10,11... | collective-permute-start | bytes 73736 | tf_op jit(solution)/shard_map/ppermute | solution.py:295
  14.8 5.2 %collective-permute-start.4 = (bf16[3,16,256]{2,1,0:T(8,128)(2,1)S(1)}, bf16[3,16,256]{2,1,0:T(8,128)(2,1)S(1)}, u32[]{:S(2)}, u32[]{:S(2)}) collective-permute-start(bf16[3,16,256]{2,1,0:T(8,128)(2,1)S(1)} %bitcast.29), channel_id=1, source_target_pairs={{1,2},{3,4},{5,6},{2,1},{4,3},{6,5},{9,10},{11,12},{13,14},{10,9},... | collective-permute-start | bytes 73736 | tf_op jit(solution)/shard_map/ppermute | solution.py:298
  21.7 13.3 %all-to-all-start = ((bf16[16,32,256]{2,1,0:T(8,128)(2,1)}), bf16[16,32,256]{2,1,0:T(8,128)(2,1)S(1)}, u32[]{:S(2)}, u32[]{:S(2)}) async-start(bf16[16,32,256]{2,1,0:T(8,128)(2,1)} %bitcast.18), calls=%async_computation | async-start | bytes 524288 | tf_op jit(solution)/shard_map/all_to_all | solution.py:331
  27.1 15.8 %collective-permute-start.5 = (bf16[2,144,256]{2,1,0:T(8,128)(2,1)S(1)}, bf16[2,144,256]{2,1,0:T(8,128)(2,1)S(1)}, u32[]{:S(2)}, u32[]{:S(2)}) collective-permute-start(bf16[2,144,256]{2,1,0:T(8,128)(2,1)S(1)} %get-tuple-element.34.own), channel_id=1, source_target_pairs={{0,8},{8,0},{1,9},{9,1},{2,10},{10,2},{3,11},{11,3},{4,12},{12,4},... | collective-permute-start | bytes 442376 | tf_op jit(solution)/shard_map/ppermute | solution.py:330
  27.2 15.7 %collective-permute-start.7 = (bf16[2,144,256]{2,1,0:T(8,128)(2,1)S(1)}, bf16[2,144,256]{2,1,0:T(8,128)(2,1)S(1)}, u32[]{:S(2)}, u32[]{:S(2)}) collective-permute-start(bf16[2,144,256]{2,1,0:T(8,128)(2,1)S(1)} %get-tuple-element.34.own), channel_id=1, source_target_pairs={{0,32},{16,48},{32,0},{48,16},{1,33},{17,49},{33,1},{49,17},{2,34}... | collective-permute-start | bytes 442376 | tf_op jit(solution)/shard_map/ppermute | solution.py:283
  30.1 12.9 %collective-permute-start.6 = (bf16[2,144,256]{2,1,0:T(8,128)(2,1)S(1)}, bf16[2,144,256]{2,1,0:T(8,128)(2,1)S(1)}, u32[]{:S(2)}, u32[]{:S(2)}) collective-permute-start(bf16[2,144,256]{2,1,0:T(8,128)(2,1)S(1)} %get-tuple-element.34.own), channel_id=1, source_target_pairs={{0,16},{16,0},{32,48},{48,32},{1,17},{17,1},{33,49},{49,33},{2,18}... | collective-permute-start | bytes 442376 | tf_op jit(solution)/shard_map/ppermute | solution.py:282
  35.6 12.5 %all-to-all-start.1 = ((bf16[16,16,256]{2,1,0:T(8,128)(2,1)}), bf16[16,16,256]{2,1,0:T(8,128)(2,1)S(1)}, u32[]{:S(2)}, u32[]{:S(2)}) async-start(bf16[16,16,256]{2,1,0:T(8,128)(2,1)} %column.1), calls=%async_computation.1 | async-start | bytes 262144 | tf_op jit(solution)/shard_map/all_to_all | solution.py:335

commit v7 on v6

--- a/solution.py
+++ b/solution.py
@@ -264,15 +264,8 @@
     rounds = pair_order.shape[0]
     count = lax.axis_size(("zl", "c"))
     owned = coupling.shape[0] // lax.axis_size(("x", "y", "zh"))
-    mine, order, q_row, spread, mask_row, offset_row, occupancy_row = begin(
-        green,
-        pair_order[:, 0].T,
-        q_index.T,
-        coupling.T,
-        mask[None, :],
-        offsets[None, :],
-        occupancy[None, :],
-    )
+    mine, order, q_row, mask_row = begin(green, pair_order[:, 0].T, q_index.T, mask[None, :])
+    spread, offset_row, occupancy_row = coupling.T, offsets[None, :], occupancy[None, :]
     place = [lax.axis_index(("x", "y", "zh")) * owned, lax.axis_index("c")]
     place = jnp.stack([jnp.asarray(x, jnp.int32) for x in place])[None]
 

time: 49.3 us -> 49.3 us (level)
  waiting for transfers between devices: 10.7 us -> 10 us
  local copies, waits for them, and re-layouts: 0.02 us -> 0.69 us
    all_to_all x1, waiting for transfers between devices: 3.59 us -> 2.89 us  [on_device(): got = lax.all_to_all(sent, ('c', 'zh', 'zl'), 0, 0, tiled=True)]
    unnamed x2 -> x8, local copies, waits for them, and re-layouts: 0.01 us -> 0.67 us
where the time goes in v7:
time: 49.3 us; the launch traced here: 48.9 us
  starting transfers between devices  29.2 us (59%)
  waiting for transfers between devices  10 us (20%)
  Pallas kernels  8.02 us (16%)
  between operations  0.8 us (2%)
  local copies, waits for them, and re-layouts  0.69 us (1%)
    ppermute x1, starting transfers between devices, on_device(): far = lax.ppermute(mine, 'zh', swap)  7.83 us
    pallas_call x7, Pallas kernels, call(): pl.pallas_call(kernel, out_shape=outs, in_specs=specs, out_specs=out_spec...  7.06 us
    ppermute x2, starting transfers between devices, exchange(): return (near, lax.ppermute(x, 'y', [(i, i ^ 2) for i in range(4)]))  5.87 us
    all_to_all x1, starting transfers between devices, on_device(): lax.all_to_all(dense.reshape(16, -1, norb), ('x', 'y'), 0, 0, tiled=True)  5.42 us
    all_to_all x1, starting transfers between devices, on_device(): got = lax.all_to_all(sent, ('c', 'zh', 'zl'), 0, 0, tiled=True)  5.23 us
    all_to_all x1, waiting for transfers between devices, on_device(): lax.all_to_all(dense.reshape(16, -1, norb), ('x', 'y'), 0, 0, tiled=True)  4.58 us
    all_to_all x1, waiting for transfers between devices, on_device(): got = lax.all_to_all(sent, ('c', 'zh', 'zl'), 0, 0, tiled=True)  2.89 us
    ppermute x1, waiting for transfers between devices, on_device(): lax.ppermute(to_chip, ('zl', 'c'), meet + [(j, i) for i, j in meet])  2.55 us
  transfers between devices with their start and end apart: 10, of which 3 were waited for; matrix products, arithmetic and copies ran while one was open for 0% of the time, Pallas kernels for 10%

profile of v7, /device:TPU:1, one launch (start us, length us, event | category | flops | bytes accessed | tf_op | source)
XLA Modules:
  0.0 48.9 jit_solution(16458404468798977174)
XLA Ops:
  0.6 1.0 %begin.1 = (bf16[2,128,256]{2,1,0:T(8,128)(2,1)S(1)}, s32[2,4]{1,0:T(2,128)S(1)}, s32[2,4]{1,0:T(2,128)S(1)}, s32[1,128]{1,0:T(1,128)S(1)}) custom-call(bf16[2,2,128,256]{3,2,1,0:T(8,128)(2,1)} %green.7, s32[2,4]{1,0:T(2,128)} %bitcast.34, s32[2,4]{1,0:T(2,128)} %bitcast.35, s32[1,128]{1,0:T(1,128)} %bitcast.36), custom_call_target="tpu_custom_call" | custom-call | bytes 262144 | tf_op jit(solution)/shard_map/begin/pallas_call | solution.py:91
  1.6 7.8 %collective-permute-start = (bf16[2,128,256]{2,1,0:T(8,128)(2,1)S(1)}, bf16[2,128,256]{2,1,0:T(8,128)(2,1)S(1)}, u32[]{:S(2)}, u32[]{:S(2)}) collective-permute-start(bf16[2,128,256]{2,1,0:T(8,128)(2,1)S(1)} %get-tuple-element.21), channel_id=1, source_target_pairs={{0,8},{8,0},{1,9},{9,1},{2,10},{10,2},{3,11},{11,3},{4,12},{12,4},... | collective-permute-start | bytes 393224 | tf_op jit(solution)/shard_map/ppermute | solution.py:278
  9.4 0.3 shift.1
  9.7 3.0 %collective-permute-start.2 = (bf16[2,128,256]{2,1,0:T(8,128)(2,1)S(1)}, bf16[2,128,256]{2,1,0:T(8,128)(2,1)S(1)}, u32[]{:S(2)}, u32[]{:S(2)}) collective-permute-start(bf16[2,128,256]{2,1,0:T(8,128)(2,1)S(1)} %get-tuple-element.21), channel_id=1, source_target_pairs={{0,32},{16,48},{32,0},{48,16},{1,33},{17,49},{33,1},{49,17},{2,34}... | collective-permute-start | bytes 393224 | tf_op jit(solution)/shard_map/ppermute | solution.py:276
  12.7 0.4 collective-permute-start.1
  13.2 0.1 bitcast_multiply_fusion
  13.2 1.6 %collective-permute-start.3 = (bf16[3,16,256]{2,1,0:T(8,128)(2,1)S(1)}, bf16[3,16,256]{2,1,0:T(8,128)(2,1)S(1)}, u32[]{:S(2)}, u32[]{:S(2)}) collective-permute-start(bf16[3,16,256]{2,1,0:T(8,128)(2,1)S(1)} %bitcast.33), channel_id=1, source_target_pairs={{0,1},{1,0},{2,3},{3,2},{4,5},{5,4},{6,7},{7,6},{8,9},{9,8},{10,11... | collective-permute-start | bytes 73736 | tf_op jit(solution)/shard_map/ppermute | solution.py:288
  14.8 2.5 %collective-permute-start.4 = (bf16[3,16,256]{2,1,0:T(8,128)(2,1)S(1)}, bf16[3,16,256]{2,1,0:T(8,128)(2,1)S(1)}, u32[]{:S(2)}, u32[]{:S(2)}) collective-permute-start(bf16[3,16,256]{2,1,0:T(8,128)(2,1)S(1)} %bitcast.32), channel_id=1, source_target_pairs={{1,2},{3,4},{5,6},{2,1},{4,3},{6,5},{9,10},{11,12},{13,14},{10,9},... | collective-permute-start | bytes 73736 | tf_op jit(solution)/shard_map/ppermute | solution.py:291
  17.4 0.1 add_bitcast_fusion.place
  17.4 2.6 %collective-permute-done.4.from_chip = bf16[3,16,256]{2,1,0:T(8,128)(2,1)S(1)} collective-permute-done((bf16[3,16,256]{2,1,0:T(8,128)(2,1)S(1)}, bf16[3,16,256]{2,1,0:T(8,128)(2,1)S(1)}, u32[]{:S(2)}, u32[]{:S(2)}) %collective-permute-start.4) | collective-permute-done | bytes 24608 | tf_op jit(solution)/shard_map/ppermute | solution.py:291
  20.0 0.3 halo.1
  20.3 1.3 %terms.1 = bf16[512,256]{1,0:T(8,128)(2,1)} custom-call(s32[2,4]{1,0:T(2,128)S(1)} %get-tuple-element.16.order, bf16[128,256]{1,0:T(8,128)(2,1)S(1)} %get-tuple-element.33.far0, bf16[128,256]{1,0:T(8,128)(2,1)S(1)} %get-tuple-element.32.far1, bf16[2,128,256]{2,1,0:T(8,128)(2,1)S(1)} %collective-permute-done.1.near.great2, ...), custom_call_target="tpu_custom_call" | custom-call | flops 1048576 | bytes 1048576 | tf_op jit(solution)/shard_map/terms/pallas_call | solution.py:57
  21.7 5.4 %all-to-all-start = ((bf16[16,32,256]{2,1,0:T(8,128)(2,1)}), bf16[16,32,256]{2,1,0:T(8,128)(2,1)S(1)}, u32[]{:S(2)}, u32[]{:S(2)}) async-start(bf16[16,32,256]{2,1,0:T(8,128)(2,1)} %bitcast.18), calls=%async_computation | async-start | bytes 524288 | tf_op jit(solution)/shard_map/all_to_all | solution.py:324
  27.1 0.1 collective-permute-start.5
  27.2 2.9 %collective-permute-start.7 = (bf16[2,144,256]{2,1,0:T(8,128)(2,1)S(1)}, bf16[2,144,256]{2,1,0:T(8,128)(2,1)S(1)}, u32[]{:S(2)}, u32[]{:S(2)}) collective-permute-start(bf16[2,144,256]{2,1,0:T(8,128)(2,1)S(1)} %get-tuple-element.28.own), channel_id=1, source_target_pairs={{0,32},{16,48},{32,0},{48,16},{1,33},{17,49},{33,1},{49,17},{2,34}... | collective-permute-start | bytes 442376 | tf_op jit(solution)/shard_map/ppermute | solution.py:276
  30.1 0.3 collective-permute-start.6
  30.3 4.6 %all-to-all-done.got = bf16[16,32,256]{2,1,0:T(8,128)(2,1)S(1)} async-done(((bf16[16,32,256]{2,1,0:T(8,128)(2,1)}), bf16[16,32,256]{2,1,0:T(8,128)(2,1)S(1)}, u32[]{:S(2)}, u32[]{:S(2)}) %all-to-all-start) | async-done | bytes 262176 | tf_op jit(solution)/shard_map/all_to_all | solution.py:324
  34.9 0.7 %column.1 = bf16[16,16,256]{2,1,0:T(8,128)(2,1)} custom-call(bf16[16,32,256]{2,1,0:T(8,128)(2,1)S(1)} %all-to-all-done.got), custom_call_target="tpu_custom_call" | custom-call | flops 1048576 | bytes 1048576 | tf_op jit(solution)/shard_map/column/pallas_call | solution.py:57
  35.6 5.2 %all-to-all-start.1 = ((bf16[16,16,256]{2,1,0:T(8,128)(2,1)}), bf16[16,16,256]{2,1,0:T(8,128)(2,1)S(1)}, u32[]{:S(2)}, u32[]{:S(2)}) async-start(bf16[16,16,256]{2,1,0:T(8,128)(2,1)} %column.1), calls=%async_computation.1 | async-start | bytes 262144 | tf_op jit(solution)/shard_map/all_to_all | solution.py:328
  40.9 0.7 %copy-done.1 = f32[128,8]{0,1:T(8,128)S(1)} copy-done((f32[128,8]{0,1:T(8,128)S(1)}, f32[128,8]{0,1:T(8,128)}, u32[]{:S(2)}) %copy-start.1) | copy-done | bytes 4120
  41.5 2.0 %weights.1 = (bf16[4,128,576]{2,1,0:T(8,128)(2,1)S(1)}, f32[32,16]{1,0:T(8,128)S(1)}) custom-call(s32[2,4]{1,0:T(2,128)S(1)} %get-tuple-element.17.q_row, s32[1,2]{1,0:T(1,128)S(1)} %add_bitcast_fusion.place, s32[1,8]{1,0:T(1,128)S(1)} %bitcast.27, f32[1,8]{1,0:T(1,128)S(1)} %bitcast.28, f32[8,128]{1,0:T(8,128)S(1)} %bitcast.26, ...), custom_call_target="tpu_custom_call" | custom-call | flops 1048576 | bytes 1048576 | tf_op jit(solution)/shard_map/weights/pallas_call | solution.py:57
  43.6 1.6 %sigma.1 = bf16[2,2,128,256]{3,2,1,0:T(8,128)(2,1)} custom-call(s32[2,4]{1,0:T(2,128)S(1)} %get-tuple-element.16.order, bf16[4,128,576]{2,1,0:T(8,128)(2,1)S(1)} %get-tuple-element.26.main, bf16[2,2,128,256]{3,2,1,0:T(8,128)(2,1)S(1)} %copy-done, bf16[2,144,256]{2,1,0:T(8,128)(2,1)S(1)} %get-tuple-element.28.own, ...), custom_call_target="tpu_custom_call" | custom-call | flops 17179869184 | bytes 1048576 | tf_op jit(solution)/shard_map/sigma/pallas_call | solution.py:57
  45.2 2.9 %all-to-all-done.1.got = bf16[16,16,256]{2,1,0:T(8,128)(2,1)S(1)} async-done(((bf16[16,16,256]{2,1,0:T(8,128)(2,1)}), bf16[16,16,256]{2,1,0:T(8,128)(2,1)S(1)}, u32[]{:S(2)}, u32[]{:S(2)}) %all-to-all-start.1) | async-done | bytes 131104 | tf_op jit(solution)/shard_map/all_to_all | solution.py:328
  48.1 0.8 %owner.1 = f32[32,256]{1,0:T(8,128)} custom-call(bf16[16,16,256]{2,1,0:T(8,128)(2,1)S(1)} %all-to-all-done.1.got, f32[32,16]{1,0:T(8,128)S(1)} %get-tuple-element.29.owner), custom_call_target="tpu_custom_call" | custom-call | flops 1048576 | bytes 1048576 | tf_op jit(solution)/shard_map/owner/pallas_call | solution.py:57
  (19 shorter events, 0.1 us)
Async XLA Ops:
  0.6 8.8 %copy-start = (bf16[2,2,128,256]{3,2,1,0:T(8,128)(2,1)S(1)}, bf16[2,2,128,256]{3,2,1,0:T(8,128)(2,1)}, u32[]{:S(2)}) copy-start(bf16[2,2,128,256]{3,2,1,0:T(8,128)(2,1)} %green.7) | copy-start | bytes 786436
  1.6 18.7 %collective-permute-start = (bf16[2,128,256]{2,1,0:T(8,128)(2,1)S(1)}, bf16[2,128,256]{2,1,0:T(8,128)(2,1)S(1)}, u32[]{:S(2)}, u32[]{:S(2)}) collective-permute-start(bf16[2,128,256]{2,1,0:T(8,128)(2,1)S(1)} %get-tuple-element.21), channel_id=1, source_target_pairs={{0,8},{8,0},{1,9},{9,1},{2,10},{10,2},{3,11},{11,3},{4,12},{12,4},... | collective-permute-start | bytes 393224 | tf_op jit(solution)/shard_map/ppermute | solution.py:278
  9.7 10.6 %collective-permute-start.2 = (bf16[2,128,256]{2,1,0:T(8,128)(2,1)S(1)}, bf16[2,128,256]{2,1,0:T(8,128)(2,1)S(1)}, u32[]{:S(2)}, u32[]{:S(2)}) collective-permute-start(bf16[2,128,256]{2,1,0:T(8,128)(2,1)S(1)} %get-tuple-element.21), channel_id=1, source_target_pairs={{0,32},{16,48},{32,0},{48,16},{1,33},{17,49},{33,1},{49,17},{2,34}... | collective-permute-start | bytes 393224 | tf_op jit(solution)/shard_map/ppermute | solution.py:276
  12.7 7.6 %collective-permute-start.1 = (bf16[2,128,256]{2,1,0:T(8,128)(2,1)S(1)}, bf16[2,128,256]{2,1,0:T(8,128)(2,1)S(1)}, u32[]{:S(2)}, u32[]{:S(2)}) collective-permute-start(bf16[2,128,256]{2,1,0:T(8,128)(2,1)S(1)} %get-tuple-element.21), channel_id=1, source_target_pairs={{0,16},{16,0},{32,48},{48,32},{1,17},{17,1},{33,49},{49,33},{2,18}... | collective-permute-start | bytes 393224 | tf_op jit(solution)/shard_map/ppermute | solution.py:275
  13.2 4.2 %collective-permute-start.3 = (bf16[3,16,256]{2,1,0:T(8,128)(2,1)S(1)}, bf16[3,16,256]{2,1,0:T(8,128)(2,1)S(1)}, u32[]{:S(2)}, u32[]{:S(2)}) collective-permute-start(bf16[3,16,256]{2,1,0:T(8,128)(2,1)S(1)} %bitcast.33), channel_id=1, source_target_pairs={{0,1},{1,0},{2,3},{3,2},{4,5},{5,4},{6,7},{7,6},{8,9},{9,8},{10,11... | collective-permute-start | bytes 73736 | tf_op jit(solution)/shard_map/ppermute | solution.py:288
  14.8 5.2 %collective-permute-start.4 = (bf16[3,16,256]{2,1,0:T(8,128)(2,1)S(1)}, bf16[3,16,256]{2,1,0:T(8,128)(2,1)S(1)}, u32[]{:S(2)}, u32[]{:S(2)}) collective-permute-start(bf16[3,16,256]{2,1,0:T(8,128)(2,1)S(1)} %bitcast.32), channel_id=1, source_target_pairs={{1,2},{3,4},{5,6},{2,1},{4,3},{6,5},{9,10},{11,12},{13,14},{10,9},... | collective-permute-start | bytes 73736 | tf_op jit(solution)/shard_map/ppermute | solution.py:291
  21.7 13.3 %all-to-all-start = ((bf16[16,32,256]{2,1,0:T(8,128)(2,1)}), bf16[16,32,256]{2,1,0:T(8,128)(2,1)S(1)}, u32[]{:S(2)}, u32[]{:S(2)}) async-start(bf16[16,32,256]{2,1,0:T(8,128)(2,1)} %bitcast.18), calls=%async_computation | async-start | bytes 524288 | tf_op jit(solution)/shard_map/all_to_all | solution.py:324
  27.1 16.5 %collective-permute-start.5 = (bf16[2,144,256]{2,1,0:T(8,128)(2,1)S(1)}, bf16[2,144,256]{2,1,0:T(8,128)(2,1)S(1)}, u32[]{:S(2)}, u32[]{:S(2)}) collective-permute-start(bf16[2,144,256]{2,1,0:T(8,128)(2,1)S(1)} %get-tuple-element.28.own), channel_id=1, source_target_pairs={{0,8},{8,0},{1,9},{9,1},{2,10},{10,2},{3,11},{11,3},{4,12},{12,4},... | collective-permute-start | bytes 442376 | tf_op jit(solution)/shard_map/ppermute | solution.py:323
  27.2 16.4 %collective-permute-start.7 = (bf16[2,144,256]{2,1,0:T(8,128)(2,1)S(1)}, bf16[2,144,256]{2,1,0:T(8,128)(2,1)S(1)}, u32[]{:S(2)}, u32[]{:S(2)}) collective-permute-start(bf16[2,144,256]{2,1,0:T(8,128)(2,1)S(1)} %get-tuple-element.28.own), channel_id=1, source_target_pairs={{0,32},{16,48},{32,0},{48,16},{1,33},{17,49},{33,1},{49,17},{2,34}... | collective-permute-start | bytes 442376 | tf_op jit(solution)/shard_map/ppermute | solution.py:276
  30.1 13.6 %collective-permute-start.6 = (bf16[2,144,256]{2,1,0:T(8,128)(2,1)S(1)}, bf16[2,144,256]{2,1,0:T(8,128)(2,1)S(1)}, u32[]{:S(2)}, u32[]{:S(2)}) collective-permute-start(bf16[2,144,256]{2,1,0:T(8,128)(2,1)S(1)} %get-tuple-element.28.own), channel_id=1, source_target_pairs={{0,16},{16,0},{32,48},{48,32},{1,17},{17,1},{33,49},{49,33},{2,18}... | collective-permute-start | bytes 442376 | tf_op jit(solution)/shard_map/ppermute | solution.py:275
  35.6 12.5 %all-to-all-start.1 = ((bf16[16,16,256]{2,1,0:T(8,128)(2,1)}), bf16[16,16,256]{2,1,0:T(8,128)(2,1)S(1)}, u32[]{:S(2)}, u32[]{:S(2)}) async-start(bf16[16,16,256]{2,1,0:T(8,128)(2,1)} %column.1), calls=%async_computation.1 | async-start | bytes 262144 | tf_op jit(solution)/shard_map/all_to_all | solution.py:328
  40.8 0.7 %copy-start.1 = (f32[128,8]{0,1:T(8,128)S(1)}, f32[128,8]{0,1:T(8,128)}, u32[]{:S(2)}) copy-start(f32[128,8]{0,1:T(8,128)} %param.13) | copy-start | bytes 12292
  40.8 0.7 %copy-start.2 = (s32[8]{0:T(128)S(1)}, s32[8]{0:T(128)}, u32[]{:S(2)}) copy-start(s32[8]{0:T(128)} %param.11) | copy-start | bytes 100
  40.9 0.7 %copy-start.3 = (f32[8]{0:T(128)S(1)}, f32[8]{0:T(128)}, u32[]{:S(2)}) copy-start(f32[8]{0:T(128)} %param.12) | copy-start | bytes 100

commit v8 on v7

--- a/solution.py
+++ b/solution.py
@@ -252,7 +252,10 @@
 
 def owner_kernel(got, owner, pol):
     total = jnp.sum(got[...].astype(F32), axis=0)
-    pol[...] = dot(owner[...], total, HIGHEST)
+    high, top = owner[...].astype(BF16), total.astype(BF16)
+    low = (owner[...] - high.astype(F32)).astype(BF16)
+    rest = (total - top.astype(F32)).astype(BF16)
+    pol[...] = dot(high, top) + (dot(high, rest) + dot(low, top))
 
 
 def tie(x, y):

time: 49.3 us -> 49.3 us (level)
  no operation moved by 1% of the time
where the time goes in v8:
time: 49.3 us; the launch traced here: 48.9 us
  starting transfers between devices  29.2 us (59%)
  waiting for transfers between devices  10 us (20%)
  Pallas kernels  8.01 us (16%)
  between operations  0.8 us (2%)
  local copies, waits for them, and re-layouts  0.69 us (1%)
    ppermute x1, starting transfers between devices, on_device(): far = lax.ppermute(mine, 'zh', swap)  7.83 us
    pallas_call x7, Pallas kernels, call(): pl.pallas_call(kernel, out_shape=outs, in_specs=specs, out_specs=out_spec...  7.05 us
    ppermute x2, starting transfers between devices, exchange(): return (near, lax.ppermute(x, 'y', [(i, i ^ 2) for i in range(4)]))  5.87 us
    all_to_all x1, starting transfers between devices, on_device(): lax.all_to_all(dense.reshape(16, -1, norb), ('x', 'y'), 0, 0, tiled=True)  5.42 us
    all_to_all x1, starting transfers between devices, on_device(): got = lax.all_to_all(sent, ('c', 'zh', 'zl'), 0, 0, tiled=True)  5.23 us
    all_to_all x1, waiting for transfers between devices, on_device(): lax.all_to_all(dense.reshape(16, -1, norb), ('x', 'y'), 0, 0, tiled=True)  4.58 us
    all_to_all x1, waiting for transfers between devices, on_device(): got = lax.all_to_all(sent, ('c', 'zh', 'zl'), 0, 0, tiled=True)  2.88 us
    ppermute x1, waiting for transfers between devices, on_device(): lax.ppermute(to_chip, ('zl', 'c'), meet + [(j, i) for i, j in meet])  2.55 us
  transfers between devices with their start and end apart: 10, of which 3 were waited for; matrix products, arithmetic and copies ran while one was open for 0% of the time, Pallas kernels for 10%

profile of v8, /device:TPU:1, one launch (start us, length us, event | category | flops | bytes accessed | tf_op | source)
XLA Modules:
  0.0 48.9 jit_solution(648857888557513229)
XLA Ops:
  0.6 1.0 %begin.1 = (bf16[2,128,256]{2,1,0:T(8,128)(2,1)S(1)}, s32[2,4]{1,0:T(2,128)S(1)}, s32[2,4]{1,0:T(2,128)S(1)}, s32[1,128]{1,0:T(1,128)S(1)}) custom-call(bf16[2,2,128,256]{3,2,1,0:T(8,128)(2,1)} %green.7, s32[2,4]{1,0:T(2,128)} %bitcast.34, s32[2,4]{1,0:T(2,128)} %bitcast.35, s32[1,128]{1,0:T(1,128)} %bitcast.36), custom_call_target="tpu_custom_call" | custom-call | bytes 262144 | tf_op jit(solution)/shard_map/begin/pallas_call | solution.py:91
  1.6 7.8 %collective-permute-start = (bf16[2,128,256]{2,1,0:T(8,128)(2,1)S(1)}, bf16[2,128,256]{2,1,0:T(8,128)(2,1)S(1)}, u32[]{:S(2)}, u32[]{:S(2)}) collective-permute-start(bf16[2,128,256]{2,1,0:T(8,128)(2,1)S(1)} %get-tuple-element.21), channel_id=1, source_target_pairs={{0,8},{8,0},{1,9},{9,1},{2,10},{10,2},{3,11},{11,3},{4,12},{12,4},... | collective-permute-start | bytes 393224 | tf_op jit(solution)/shard_map/ppermute | solution.py:281
  9.4 0.3 shift.1
  9.7 3.0 %collective-permute-start.2 = (bf16[2,128,256]{2,1,0:T(8,128)(2,1)S(1)}, bf16[2,128,256]{2,1,0:T(8,128)(2,1)S(1)}, u32[]{:S(2)}, u32[]{:S(2)}) collective-permute-start(bf16[2,128,256]{2,1,0:T(8,128)(2,1)S(1)} %get-tuple-element.21), channel_id=1, source_target_pairs={{0,32},{16,48},{32,0},{48,16},{1,33},{17,49},{33,1},{49,17},{2,34}... | collective-permute-start | bytes 393224 | tf_op jit(solution)/shard_map/ppermute | solution.py:279
  12.7 0.4 collective-permute-start.1
  13.2 0.1 bitcast_multiply_fusion
  13.2 1.6 %collective-permute-start.3 = (bf16[3,16,256]{2,1,0:T(8,128)(2,1)S(1)}, bf16[3,16,256]{2,1,0:T(8,128)(2,1)S(1)}, u32[]{:S(2)}, u32[]{:S(2)}) collective-permute-start(bf16[3,16,256]{2,1,0:T(8,128)(2,1)S(1)} %bitcast.33), channel_id=1, source_target_pairs={{0,1},{1,0},{2,3},{3,2},{4,5},{5,4},{6,7},{7,6},{8,9},{9,8},{10,11... | collective-permute-start | bytes 73736 | tf_op jit(solution)/shard_map/ppermute | solution.py:291
  14.8 2.5 %collective-permute-start.4 = (bf16[3,16,256]{2,1,0:T(8,128)(2,1)S(1)}, bf16[3,16,256]{2,1,0:T(8,128)(2,1)S(1)}, u32[]{:S(2)}, u32[]{:S(2)}) collective-permute-start(bf16[3,16,256]{2,1,0:T(8,128)(2,1)S(1)} %bitcast.32), channel_id=1, source_target_pairs={{1,2},{3,4},{5,6},{2,1},{4,3},{6,5},{9,10},{11,12},{13,14},{10,9},... | collective-permute-start | bytes 73736 | tf_op jit(solution)/shard_map/ppermute | solution.py:294
  17.4 0.1 add_bitcast_fusion.place
  17.4 2.6 %collective-permute-done.4.from_chip = bf16[3,16,256]{2,1,0:T(8,128)(2,1)S(1)} collective-permute-done((bf16[3,16,256]{2,1,0:T(8,128)(2,1)S(1)}, bf16[3,16,256]{2,1,0:T(8,128)(2,1)S(1)}, u32[]{:S(2)}, u32[]{:S(2)}) %collective-permute-start.4) | collective-permute-done | bytes 24608 | tf_op jit(solution)/shard_map/ppermute | solution.py:294
  20.0 0.3 halo.1
  20.3 1.3 %terms.1 = bf16[512,256]{1,0:T(8,128)(2,1)} custom-call(s32[2,4]{1,0:T(2,128)S(1)} %get-tuple-element.16.order, bf16[128,256]{1,0:T(8,128)(2,1)S(1)} %get-tuple-element.33.far0, bf16[128,256]{1,0:T(8,128)(2,1)S(1)} %get-tuple-element.32.far1, bf16[2,128,256]{2,1,0:T(8,128)(2,1)S(1)} %collective-permute-done.1.near.great2, ...), custom_call_target="tpu_custom_call" | custom-call | flops 1048576 | bytes 1048576 | tf_op jit(solution)/shard_map/terms/pallas_call | solution.py:57
  21.7 5.4 %all-to-all-start = ((bf16[16,32,256]{2,1,0:T(8,128)(2,1)}), bf16[16,32,256]{2,1,0:T(8,128)(2,1)S(1)}, u32[]{:S(2)}, u32[]{:S(2)}) async-start(bf16[16,32,256]{2,1,0:T(8,128)(2,1)} %bitcast.18), calls=%async_computation | async-start | bytes 524288 | tf_op jit(solution)/shard_map/all_to_all | solution.py:327
  27.1 0.1 collective-permute-start.5
  27.2 2.9 %collective-permute-start.7 = (bf16[2,144,256]{2,1,0:T(8,128)(2,1)S(1)}, bf16[2,144,256]{2,1,0:T(8,128)(2,1)S(1)}, u32[]{:S(2)}, u32[]{:S(2)}) collective-permute-start(bf16[2,144,256]{2,1,0:T(8,128)(2,1)S(1)} %get-tuple-element.28.own), channel_id=1, source_target_pairs={{0,32},{16,48},{32,0},{48,16},{1,33},{17,49},{33,1},{49,17},{2,34}... | collective-permute-start | bytes 442376 | tf_op jit(solution)/shard_map/ppermute | solution.py:279
  30.1 0.3 collective-permute-start.6
  30.3 4.6 %all-to-all-done.got = bf16[16,32,256]{2,1,0:T(8,128)(2,1)S(1)} async-done(((bf16[16,32,256]{2,1,0:T(8,128)(2,1)}), bf16[16,32,256]{2,1,0:T(8,128)(2,1)S(1)}, u32[]{:S(2)}, u32[]{:S(2)}) %all-to-all-start) | async-done | bytes 262176 | tf_op jit(solution)/shard_map/all_to_all | solution.py:327
  34.9 0.7 %column.1 = bf16[16,16,256]{2,1,0:T(8,128)(2,1)} custom-call(bf16[16,32,256]{2,1,0:T(8,128)(2,1)S(1)} %all-to-all-done.got), custom_call_target="tpu_custom_call" | custom-call | flops 1048576 | bytes 1048576 | tf_op jit(solution)/shard_map/column/pallas_call | solution.py:57
  35.6 5.2 %all-to-all-start.1 = ((bf16[16,16,256]{2,1,0:T(8,128)(2,1)}), bf16[16,16,256]{2,1,0:T(8,128)(2,1)S(1)}, u32[]{:S(2)}, u32[]{:S(2)}) async-start(bf16[16,16,256]{2,1,0:T(8,128)(2,1)} %column.1), calls=%async_computation.1 | async-start | bytes 262144 | tf_op jit(solution)/shard_map/all_to_all | solution.py:331
  40.9 0.7 %copy-done.1 = f32[128,8]{0,1:T(8,128)S(1)} copy-done((f32[128,8]{0,1:T(8,128)S(1)}, f32[128,8]{0,1:T(8,128)}, u32[]{:S(2)}) %copy-start.1) | copy-done | bytes 4120
  41.5 2.0 %weights.1 = (bf16[4,128,576]{2,1,0:T(8,128)(2,1)S(1)}, f32[32,16]{1,0:T(8,128)S(1)}) custom-call(s32[2,4]{1,0:T(2,128)S(1)} %get-tuple-element.17.q_row, s32[1,2]{1,0:T(1,128)S(1)} %add_bitcast_fusion.place, s32[1,8]{1,0:T(1,128)S(1)} %bitcast.27, f32[1,8]{1,0:T(1,128)S(1)} %bitcast.28, f32[8,128]{1,0:T(8,128)S(1)} %bitcast.26, ...), custom_call_target="tpu_custom_call" | custom-call | flops 1048576 | bytes 1048576 | tf_op jit(solution)/shard_map/weights/pallas_call | solution.py:57
  43.6 1.6 %sigma.1 = bf16[2,2,128,256]{3,2,1,0:T(8,128)(2,1)} custom-call(s32[2,4]{1,0:T(2,128)S(1)} %get-tuple-element.16.order, bf16[4,128,576]{2,1,0:T(8,128)(2,1)S(1)} %get-tuple-element.26.main, bf16[2,2,128,256]{3,2,1,0:T(8,128)(2,1)S(1)} %copy-done, bf16[2,144,256]{2,1,0:T(8,128)(2,1)S(1)} %get-tuple-element.28.own, ...), custom_call_target="tpu_custom_call" | custom-call | flops 17179869184 | bytes 1048576 | tf_op jit(solution)/shard_map/sigma/pallas_call | solution.py:57
  45.3 2.9 %all-to-all-done.1.got = bf16[16,16,256]{2,1,0:T(8,128)(2,1)S(1)} async-done(((bf16[16,16,256]{2,1,0:T(8,128)(2,1)}), bf16[16,16,256]{2,1,0:T(8,128)(2,1)S(1)}, u32[]{:S(2)}, u32[]{:S(2)}) %all-to-all-start.1) | async-done | bytes 131104 | tf_op jit(solution)/shard_map/all_to_all | solution.py:331
  48.1 0.8 %owner.1 = f32[32,256]{1,0:T(8,128)} custom-call(bf16[16,16,256]{2,1,0:T(8,128)(2,1)S(1)} %all-to-all-done.1.got, f32[32,16]{1,0:T(8,128)S(1)} %get-tuple-element.29.owner), custom_call_target="tpu_custom_call" | custom-call | flops 1048576 | bytes 1048576 | tf_op jit(solution)/shard_map/owner/pallas_call | solution.py:57
  (19 shorter events, 0.1 us)
Async XLA Ops:
  0.6 8.8 %copy-start = (bf16[2,2,128,256]{3,2,1,0:T(8,128)(2,1)S(1)}, bf16[2,2,128,256]{3,2,1,0:T(8,128)(2,1)}, u32[]{:S(2)}) copy-start(bf16[2,2,128,256]{3,2,1,0:T(8,128)(2,1)} %green.7) | copy-start | bytes 786436
  1.6 18.7 %collective-permute-start = (bf16[2,128,256]{2,1,0:T(8,128)(2,1)S(1)}, bf16[2,128,256]{2,1,0:T(8,128)(2,1)S(1)}, u32[]{:S(2)}, u32[]{:S(2)}) collective-permute-start(bf16[2,128,256]{2,1,0:T(8,128)(2,1)S(1)} %get-tuple-element.21), channel_id=1, source_target_pairs={{0,8},{8,0},{1,9},{9,1},{2,10},{10,2},{3,11},{11,3},{4,12},{12,4},... | collective-permute-start | bytes 393224 | tf_op jit(solution)/shard_map/ppermute | solution.py:281
  9.7 10.6 %collective-permute-start.2 = (bf16[2,128,256]{2,1,0:T(8,128)(2,1)S(1)}, bf16[2,128,256]{2,1,0:T(8,128)(2,1)S(1)}, u32[]{:S(2)}, u32[]{:S(2)}) collective-permute-start(bf16[2,128,256]{2,1,0:T(8,128)(2,1)S(1)} %get-tuple-element.21), channel_id=1, source_target_pairs={{0,32},{16,48},{32,0},{48,16},{1,33},{17,49},{33,1},{49,17},{2,34}... | collective-permute-start | bytes 393224 | tf_op jit(solution)/shard_map/ppermute | solution.py:279
  12.7 7.6 %collective-permute-start.1 = (bf16[2,128,256]{2,1,0:T(8,128)(2,1)S(1)}, bf16[2,128,256]{2,1,0:T(8,128)(2,1)S(1)}, u32[]{:S(2)}, u32[]{:S(2)}) collective-permute-start(bf16[2,128,256]{2,1,0:T(8,128)(2,1)S(1)} %get-tuple-element.21), channel_id=1, source_target_pairs={{0,16},{16,0},{32,48},{48,32},{1,17},{17,1},{33,49},{49,33},{2,18}... | collective-permute-start | bytes 393224 | tf_op jit(solution)/shard_map/ppermute | solution.py:278
  13.2 4.2 %collective-permute-start.3 = (bf16[3,16,256]{2,1,0:T(8,128)(2,1)S(1)}, bf16[3,16,256]{2,1,0:T(8,128)(2,1)S(1)}, u32[]{:S(2)}, u32[]{:S(2)}) collective-permute-start(bf16[3,16,256]{2,1,0:T(8,128)(2,1)S(1)} %bitcast.33), channel_id=1, source_target_pairs={{0,1},{1,0},{2,3},{3,2},{4,5},{5,4},{6,7},{7,6},{8,9},{9,8},{10,11... | collective-permute-start | bytes 73736 | tf_op jit(solution)/shard_map/ppermute | solution.py:291
  14.8 5.2 %collective-permute-start.4 = (bf16[3,16,256]{2,1,0:T(8,128)(2,1)S(1)}, bf16[3,16,256]{2,1,0:T(8,128)(2,1)S(1)}, u32[]{:S(2)}, u32[]{:S(2)}) collective-permute-start(bf16[3,16,256]{2,1,0:T(8,128)(2,1)S(1)} %bitcast.32), channel_id=1, source_target_pairs={{1,2},{3,4},{5,6},{2,1},{4,3},{6,5},{9,10},{11,12},{13,14},{10,9},... | collective-permute-start | bytes 73736 | tf_op jit(solution)/shard_map/ppermute | solution.py:294
  21.7 13.3 %all-to-all-start = ((bf16[16,32,256]{2,1,0:T(8,128)(2,1)}), bf16[16,32,256]{2,1,0:T(8,128)(2,1)S(1)}, u32[]{:S(2)}, u32[]{:S(2)}) async-start(bf16[16,32,256]{2,1,0:T(8,128)(2,1)} %bitcast.18), calls=%async_computation | async-start | bytes 524288 | tf_op jit(solution)/shard_map/all_to_all | solution.py:327
  27.1 16.5 %collective-permute-start.5 = (bf16[2,144,256]{2,1,0:T(8,128)(2,1)S(1)}, bf16[2,144,256]{2,1,0:T(8,128)(2,1)S(1)}, u32[]{:S(2)}, u32[]{:S(2)}) collective-permute-start(bf16[2,144,256]{2,1,0:T(8,128)(2,1)S(1)} %get-tuple-element.28.own), channel_id=1, source_target_pairs={{0,8},{8,0},{1,9},{9,1},{2,10},{10,2},{3,11},{11,3},{4,12},{12,4},... | collective-permute-start | bytes 442376 | tf_op jit(solution)/shard_map/ppermute | solution.py:326
  27.2 16.4 %collective-permute-start.7 = (bf16[2,144,256]{2,1,0:T(8,128)(2,1)S(1)}, bf16[2,144,256]{2,1,0:T(8,128)(2,1)S(1)}, u32[]{:S(2)}, u32[]{:S(2)}) collective-permute-start(bf16[2,144,256]{2,1,0:T(8,128)(2,1)S(1)} %get-tuple-element.28.own), channel_id=1, source_target_pairs={{0,32},{16,48},{32,0},{48,16},{1,33},{17,49},{33,1},{49,17},{2,34}... | collective-permute-start | bytes 442376 | tf_op jit(solution)/shard_map/ppermute | solution.py:279
  30.1 13.6 %collective-permute-start.6 = (bf16[2,144,256]{2,1,0:T(8,128)(2,1)S(1)}, bf16[2,144,256]{2,1,0:T(8,128)(2,1)S(1)}, u32[]{:S(2)}, u32[]{:S(2)}) collective-permute-start(bf16[2,144,256]{2,1,0:T(8,128)(2,1)S(1)} %get-tuple-element.28.own), channel_id=1, source_target_pairs={{0,16},{16,0},{32,48},{48,32},{1,17},{17,1},{33,49},{49,33},{2,18}... | collective-permute-start | bytes 442376 | tf_op jit(solution)/shard_map/ppermute | solution.py:278
  35.6 12.5 %all-to-all-start.1 = ((bf16[16,16,256]{2,1,0:T(8,128)(2,1)}), bf16[16,16,256]{2,1,0:T(8,128)(2,1)S(1)}, u32[]{:S(2)}, u32[]{:S(2)}) async-start(bf16[16,16,256]{2,1,0:T(8,128)(2,1)} %column.1), calls=%async_computation.1 | async-start | bytes 262144 | tf_op jit(solution)/shard_map/all_to_all | solution.py:331
  40.8 0.7 %copy-start.1 = (f32[128,8]{0,1:T(8,128)S(1)}, f32[128,8]{0,1:T(8,128)}, u32[]{:S(2)}) copy-start(f32[128,8]{0,1:T(8,128)} %param.13) | copy-start | bytes 12292
  40.8 0.7 %copy-start.2 = (s32[8]{0:T(128)S(1)}, s32[8]{0:T(128)}, u32[]{:S(2)}) copy-start(s32[8]{0:T(128)} %param.11) | copy-start | bytes 100
  40.9 0.7 %copy-start.3 = (f32[8]{0:T(128)S(1)}, f32[8]{0:T(128)}, u32[]{:S(2)}) copy-start(f32[8]{0:T(128)} %param.12) | copy-start | bytes 100
